TPU v7x, 32 devices: a whole 2x2x4 slice. The times are simulated.
32 devices in a mesh: dp: 8 (over z, x), mp: 4 (over y, core).
Axes of the slice: x: 2, y: 2, z: 4, core: 2. Of those that a mesh axis runs over, the one named last changes fastest.
Arguments:
- input_field: bfloat16 [8, 192, 512], P('dp'), may hold values from -6 to 6
- variable_ids: int32 [48], replicated, may hold values from 0 to 47, as said below
- lead_bucket: int32 [8], P('dp'), may hold values from 0 to 55
- patch_table: bfloat16 [48, 4, 1024], replicated, may hold values from -3 to 3
- variable_table: bfloat16 [48, 1024], replicated, may hold values from -6 to 6
- variable_query: bfloat16 [1024], replicated, may hold values from -6 to 6
- mix_weights: bfloat16 [1024, 3, 1024], P(None, None, 'mp'), may hold values from -0.1875 to 0.1875
- mix_output: bfloat16 [1024, 1024], P('mp'), may hold values from -0.375 to 0.375
- pos_table: bfloat16 [512, 1024], replicated, may hold values from -6 to 6
- lead_table: bfloat16 [56, 1024], replicated, may hold values from -6 to 6
- first_gain: float32 [1024], replicated, may hold values from 0.5 to 1.5
- first_bias: float32 [1024], replicated, may hold values from -3 to 3
- attn_weights: bfloat16 [1024, 3, 1024], P(None, None, 'mp'), may hold values from -0.1875 to 0.1875
- attn_output: bfloat16 [1024, 1024], P('mp'), may hold values from -1.5 to 1.5
- second_gain: float32 [1024], replicated, may hold values from 0.5 to 1.5
- second_bias: float32 [1024], replicated, may hold values from -3 to 3
- up_weight: bfloat16 [1024, 4096], P(None, 'mp'), may hold values from -0.1875 to 0.1875
- down_weight: bfloat16 [4096, 1024], P('mp'), may hold values from -0.1875 to 0.1875
- cotangent: bfloat16 [4096, 1024], P(('dp', 'mp')), may hold values from -6 to 6
Outputs:
- activations: float32 [4096, 1024], P(('dp', 'mp'))
- field_grad: float32 [8, 192, 512], P('dp', None, 'mp')
- patch_grad: float32 [48, 4, 1024], P(None, None, ('dp', 'mp'))
- variable_grad: float32 [48, 1024], P(None, ('dp', 'mp'))
- query_grad: float32 [1024], P(('dp', 'mp'))
- mix_weights_grad: float32 [1024, 3, 1024], P('dp', None, 'mp')
- mix_output_grad: float32 [1024, 1024], P('mp', 'dp')
- pos_grad: float32 [512, 1024], P('mp', 'dp')
- lead_grad: float32 [56, 1024], P(None, ('dp', 'mp'))
- first_gain_grad: float32 [1024], P(('dp', 'mp'))
- first_bias_grad: float32 [1024], P(('dp', 'mp'))
- attn_weights_grad: float32 [1024, 3, 1024], P('dp', None, 'mp')
- attn_output_grad: float32 [1024, 1024], P('mp', 'dp')
- second_gain_grad: float32 [1024], P(('dp', 'mp'))
- second_bias_grad: float32 [1024], P(('dp', 'mp'))
- up_grad: float32 [1024, 4096], P('dp', 'mp')
- down_grad: float32 [4096, 1024], P('mp', 'dp')
Inputs may be any that keep to these rules, and one draw needn't show every extreme that they name: `variable_ids`: 48 distinct table rows; rows 0 and 47 are always among them.
All inputs are finite; a program needn't handle non-finite values.
Results may differ from a plain program's by a relative error of at most 0.025.
Values may be sent and summed in bfloat16 or wider, within the bound.
No kernel may reach another device: no remote copies, remote signals or barrier semaphores. Data moves between devices by JAX's collectives and lax.ppermute only.
A program may use at most 320 MiB of HBM per device.

v0:
```python
import functools

import jax
import jax.numpy as jnp
from jax import lax
from jax.experimental import pallas as pl
from jax.experimental.pallas import tpu as pltpu
from jax.sharding import PartitionSpec as P

HEAD_DIM = 64
LANES = 128
EPS = 1e-05
SCALE = HEAD_DIM ** (-0.5)
HIGH = lax.Precision.HIGHEST
F32 = jnp.float32
BF16 = jnp.bfloat16
VMEM = pl.BlockSpec(memory_space=pltpu.VMEM)
SMEM = pl.BlockSpec(memory_space=pltpu.SMEM)
ANY = pl.BlockSpec(memory_space=pl.ANY)
HBM = pl.BlockSpec(memory_space=pltpu.HBM)
MIB = 1024 * 1024


def dot(left, right, left_dim=1, right_dim=0, precision=None):
    return lax.dot_general(
        left,
        right,
        (((left_dim,), (right_dim,)), ((), ())),
        precision=precision,
        preferred_element_type=F32,
    )


def call(kernel, outs, args, fetch=(), smem=(), after=(), limit=24, cost=1, scratch=()):
    fetch = [item if isinstance(item, tuple) else (item, item.shape, None) for item in fetch]
    count = len(smem)

    def run(*refs):
        at = count + len(fetch)
        sources, rest = refs[count:at], refs[at:]
        inputs, rest = rest[: len(args)], rest[len(args) + len(after) :]
        if not fetch:
            kernel(*refs[:count], *inputs, *rest)
            return
        *rest, marks = rest
        rest, places = rest[: len(rest) - len(fetch)], rest[len(rest) - len(fetch) :]
        copies = []
        for i, (_, _, pick) in enumerate(fetch):
            source = sources[i] if pick is None else pick(sources[i])
            copies.append(pltpu.make_async_copy(source, places[i], marks.at[i]))
        for copy in copies:
            copy.start()
        for copy in copies:
            copy.wait()
        kernel(*refs[:count], *places, *inputs, *rest)

    places = [pltpu.VMEM(shape, array.dtype) for array, shape, _ in fetch]
    marks = [pltpu.SemaphoreType.DMA((len(fetch),))] if fetch else []
    return pl.pallas_call(
        run,
        out_shape=[jax.ShapeDtypeStruct(shape, kind) for shape, kind in outs],
        in_specs=[SMEM] * count + [HBM] * len(fetch) + [VMEM] * len(args) + [ANY] * len(after),
        out_specs=[VMEM] * len(outs),
        scratch_shapes=list(scratch) + places + marks,
        compiler_params=pltpu.CompilerParams(vmem_limit_bytes=limit * MIB),
        cost_estimate=pl.CostEstimate(
            flops=int(cost * 1e9), bytes_accessed=0, transcendentals=0
        ),
    )(*smem, *(array for array, _, _ in fetch), *args, *after)


def my_bit(bit):
    return (lax.axis_index("dp") // bit) % 2


def my_core():
    return lax.axis_index("mp") % 2


def my_chip():
    return lax.axis_index("mp") // 2


def iota(shape, dim):
    return lax.broadcasted_iota(jnp.int32, shape, dim)


def exact(mask):
    return mask.astype(F32).astype(BF16)


def lanes_of(rows, head):
    lane = iota((1, rows.shape[1]), 1)
    mine = (lane >= head * HEAD_DIM) & (lane < (head + 1) * HEAD_DIM)
    return jnp.where(mine, rows, jnp.zeros_like(rows))


def spread(rows, pixels, top, bottom):
    variables = top.shape[0]
    parts = [top * rows[p * variables : (p + 1) * variables] for p in range(pixels)]
    parts.append(top)
    if bottom:
        parts.append(jnp.zeros((bottom, top.shape[1]), top.dtype))
    return jnp.concatenate(parts, axis=0)


def mix_forward(
    pixels,
    quarter,
    ids_ref,
    x_ref,
    patch_ref,
    variable_ref,
    w_ref,
    w_out_ref,
    query_ref,
    table_ref,
    pick_ref,
    xt_ref,
    probs_ref,
    values_ref,
    keys_t_ref,
    score_ref,
    query_col_ref,
    mixed_ref,
    send_a_ref,
    send_b_ref,
    keep_a_ref,
    keep_b_ref,
):
    channels = x_ref.shape[1]
    variables = channels // pixels
    rows, model_width = table_ref.shape
    width = w_ref.shape[2]
    heads = width // HEAD_DIM
    bottom = rows - channels - variables
    row = iota((channels, channels), 0)
    column = iota((channels, channels), 1)
    major = jnp.zeros((channels, channels), jnp.int32)
    for p in range(pixels):
        inside = (row >= p * variables) & (row < (p + 1) * variables)
        major = jnp.where(inside, (row - p * variables) * pixels + p, major)
    flat = patch_ref[...].reshape(channels, model_width)
    table_ref[0:channels] = dot(exact(column == major), flat).astype(BF16)
    table_ref[channels : channels + variables] = variable_ref[...]
    if bottom:
        table_ref[channels + variables :] = jnp.zeros((bottom, model_width), BF16)
    channel = iota((1, channels), 1)
    place = jnp.zeros((1, channels), jnp.int32)
    for v in range(variables):
        pixel = channel - v * pixels
        inside = (pixel >= 0) & (pixel < pixels)
        place = jnp.where(inside, pixel * variables + ids_ref[v], place)
    pick = (iota((channels, channels), 0) == place).astype(F32)
    pick_ref[...] = pick.T.astype(BF16)
    core = my_core()
    starts = [core, 1 - core, core + 2, 3 - core]
    field = jnp.concatenate(
        [x_ref[0, :, pl.ds(pl.multiple_of(s * quarter, LANES), quarter)] for s in starts], axis=1
    )
    xt = dot(pick.astype(BF16), field)
    xt_ref[...] = xt.astype(BF16)
    query_rows = jnp.broadcast_to(query_ref[...].astype(F32)[None], (16, model_width)).astype(BF16)
    query = dot(query_rows, w_ref[0])[0:1].astype(BF16).astype(F32)
    table = table_ref[...]
    keys = dot(table, w_ref[1])
    values = dot(table, w_ref[2])
    values_ref[...] = values.astype(BF16)
    keys_t_ref[...] = keys.T
    query_col_ref[...] = jnp.broadcast_to(query, (LANES, width)).T
    lane = iota((width, LANES), 1) * HEAD_DIM
    row = iota((width, LANES), 0)
    same = ((row >= lane) & (row < lane + HEAD_DIM)).astype(F32)
    score = dot(keys * query, same, precision=HIGH) * SCALE
    score_ref[...] = score
    values_t = values.T.astype(BF16)
    for head in range(heads):
        column = score[:, head : head + 1]
        logits = jnp.broadcast_to(column[channels : channels + variables], (variables, xt.shape[1]))
        for p in range(pixels):
            part = slice(p * variables, (p + 1) * variables)
            logits = logits + column[part] * xt[part]
        weights = jnp.exp(logits - jnp.max(logits, axis=0, keepdims=True))
        probs = weights / jnp.sum(weights, axis=0, keepdims=True)
        probs_ref[head * variables : (head + 1) * variables] = probs
        low = probs.astype(BF16).astype(F32)
        mixing = spread(xt, pixels, low, bottom).astype(BF16)
        part = slice(head * HEAD_DIM, (head + 1) * HEAD_DIM)
        mixed_ref[part] = dot(values_t[part], mixing).astype(BF16)
    out = dot(mixed_ref[...], w_out_ref[...], 0, 0)
    keep_a_ref[...] = out[0:quarter]
    send_a_ref[...] = out[quarter : 2 * quarter].astype(BF16)
    keep_b_ref[...] = out[2 * quarter : 3 * quarter]
    send_b_ref[...] = out[3 * quarter :].astype(BF16)


def mix_backward(
    pixels,
    pick_ref,
    xt_ref,
    probs_ref,
    values_ref,
    score_ref,
    w_out_ref,
    a0_ref,
    a1_ref,
    b0_ref,
    b1_ref,
    mass_ref,
    mass_low_ref,
    bias_ref,
    field_send_ref,
    field_keep_ref,
):
    channels, length = xt_ref.shape
    variables = channels // pixels
    rows, width = values_ref.shape
    heads = width // HEAD_DIM
    bottom = rows - channels - variables
    quarter = length // 4
    xt = xt_ref[...].astype(F32)
    grad = jnp.concatenate([a0_ref[...], a1_ref[...], b0_ref[...], b1_ref[...]], axis=0)
    grad_t = dot(w_out_ref[...], grad, 1, 1).astype(BF16)
    values = values_ref[...]
    score = score_ref[...]
    field = jnp.zeros(xt.shape, F32)
    lane = iota((rows, LANES), 1)
    sums = jnp.zeros((rows, LANES), F32)
    for head in range(heads):
        probs = probs_ref[head * variables : (head + 1) * variables]
        low = probs.astype(BF16).astype(F32)
        back = dot(lanes_of(values, head), grad_t)
        prob_grad = back[channels : channels + variables]
        for p in range(pixels):
            part = slice(p * variables, (p + 1) * variables)
            prob_grad = prob_grad + xt[part] * back[part]
        middle = jnp.sum(probs * prob_grad, axis=0, keepdims=True)
        score_grad = probs * (prob_grad - middle)
        column = score[:, head : head + 1]
        field = field + jnp.concatenate(
            [
                score_grad * column[p * variables : (p + 1) * variables]
                + low * back[p * variables : (p + 1) * variables]
                for p in range(pixels)
            ],
            axis=0,
        )
        spreading = spread(xt, pixels, score_grad * SCALE, bottom)
        sums = jnp.where(lane == head, jnp.sum(spreading, axis=1, keepdims=True), sums)
        mixing = spread(xt, pixels, low, bottom).astype(BF16)
        part = slice(head * HEAD_DIM, (head + 1) * HEAD_DIM)
        mass_ref[part] = dot(grad_t[part], mixing, 1, 1)
    mass_low_ref[...] = mass_ref[...].astype(BF16)
    bias_ref[...] = sums.T[0:8]
    field = dot(pick_ref[...], field.astype(BF16))
    field_keep_ref[:, 0:quarter] = field[:, 0:quarter]
    field_keep_ref[:, quarter:] = field[:, 2 * quarter : 3 * quarter]
    field_send_ref[:, 0:quarter] = field[:, quarter : 2 * quarter].astype(BF16)
    field_send_ref[:, quarter:] = field[:, 3 * quarter :].astype(BF16)


def norm_forward(*refs):
    *terms, gain_ref, bias_ref, out_ref, low_ref = refs
    total = terms[0][...].astype(F32)
    for term in terms[1:]:
        total = total + term[...].astype(F32)
    out_ref[...] = total
    centered = total - jnp.mean(total, axis=1, keepdims=True)
    inv_std = lax.rsqrt(jnp.mean(centered * centered, axis=1, keepdims=True) + EPS)
    low_ref[...] = (centered * inv_std * gain_ref[...] + bias_ref[...]).astype(BF16)


def norm_backward(with_sum, add_refs, *refs):
    keep_ref, far_ref, rows_ref, gain_ref, above_ref = refs[:5]
    more = refs[5 : 5 + add_refs]
    out_ref, low_ref, sums_ref = refs[5 + add_refs :]
    grad = keep_ref[...] + far_ref[...].astype(F32)
    rows = rows_ref[...]
    centered = rows - jnp.mean(rows, axis=1, keepdims=True)
    inv_std = lax.rsqrt(jnp.mean(centered * centered, axis=1, keepdims=True) + EPS)
    normed = centered * inv_std
    scaled = grad * gain_ref[...]
    first = jnp.mean(scaled, axis=1, keepdims=True)
    second = jnp.mean(scaled * normed, axis=1, keepdims=True)
    out = above_ref[...].astype(F32) + inv_std * (scaled - first - normed * second)
    out_ref[...] = out
    low_ref[...] = out.astype(BF16)
    lines = [
        jnp.sum(grad * normed, axis=0, keepdims=True),
        jnp.sum(grad, axis=0, keepdims=True),
    ]
    lines.append(jnp.sum(out, axis=0, keepdims=True) if with_sum else jnp.zeros_like(lines[0]))
    if add_refs:
        one, two_a, two_b = (ref[...] for ref in more)
        lines = [
            lines[0] + one[0:1],
            lines[1] + one[1:2],
            two_a[0:1] + two_b[0:1],
            two_a[1:2] + two_b[1:2],
            lines[2] + one[2:3],
        ]
    lines.append(jnp.zeros((8 - len(lines), grad.shape[1]), F32))
    sums_ref[...] = jnp.concatenate(lines, axis=0)


def project(own_ref, near_ref, w_ref, out_ref):
    rows = jnp.concatenate([own_ref[...], near_ref[...]], axis=0)
    for i in range(3):
        out_ref[i] = dot(rows, w_ref[i]).astype(BF16)


def attend(query, keys, values_t, logs_ref):
    scaled = (query.astype(F32) * SCALE).astype(BF16)
    parts = []
    for head in range(keys.shape[1] // HEAD_DIM):
        scores = dot(lanes_of(keys, head), scaled, 1, 1)
        top = jnp.max(scores, axis=0, keepdims=True)
        weights = jnp.exp(scores - top)
        total = jnp.sum(weights, axis=0, keepdims=True)
        logs_ref[head : head + 1] = top + jnp.log(total)
        probs = (weights * (1.0 / total)).astype(BF16)
        parts.append(dot(values_t[head * HEAD_DIM : (head + 1) * HEAD_DIM], probs))
    return jnp.concatenate(parts, axis=0).T.astype(BF16)


def split_out(out, keep_ref, send_ref):
    quarter = out.shape[0] // 2
    keep_ref[...] = out[:quarter]
    send_ref[...] = out[quarter:].astype(BF16)


def attend_first(own_ref, near_ref, w_ref, first_ref, w_out_ref, second_ref, out_ref, logs_ref, keep_ref, send_ref):
    project(own_ref, near_ref, w_ref, second_ref)
    keys = jnp.concatenate([first_ref[1], second_ref[1]], axis=0)
    values = jnp.concatenate([first_ref[2], second_ref[2]], axis=0)
    out_ref[...] = attend(first_ref[0], keys, values.astype(F32).T.astype(BF16), logs_ref)
    split_out(dot(out_ref[...], w_out_ref[...]), keep_ref, send_ref)


def attend_second(first_ref, second_ref, w_out_ref, out_ref, logs_ref, keep_ref, send_ref):
    keys = jnp.concatenate([first_ref[1], second_ref[1]], axis=0)
    values = jnp.concatenate([first_ref[2], second_ref[2]], axis=0)
    out_ref[...] = attend(second_ref[0], keys, values.astype(F32).T.astype(BF16), logs_ref)
    split_out(dot(out_ref[...], w_out_ref[...]), keep_ref, send_ref)


def attend_grad(grad, query, keys, values, logs_ref):
    scaled = (query.astype(F32) * SCALE).astype(BF16)
    keys_t = keys.astype(F32).T.astype(BF16)
    query_parts = []
    key_grad = jnp.zeros(keys.shape, F32)
    value_grad = jnp.zeros(keys.shape, F32)
    for head in range(keys.shape[1] // HEAD_DIM):
        scores = dot(lanes_of(keys, head), scaled, 1, 1)
        probs = jnp.exp(scores - logs_ref[head : head + 1])
        prob_grad = dot(lanes_of(values, head), grad, 1, 1)
        middle = jnp.sum(probs * prob_grad, axis=0, keepdims=True)
        score_grad = (probs * (prob_grad - middle)).astype(BF16)
        query_parts.append(dot(keys_t[head * HEAD_DIM : (head + 1) * HEAD_DIM], score_grad))
        key_grad = key_grad + dot(score_grad, lanes_of(scaled, head))
        value_grad = value_grad + dot(probs.astype(BF16), lanes_of(grad, head))
    query_grad = (jnp.concatenate(query_parts, axis=0).T * SCALE).astype(BF16)
    return query_grad, key_grad, value_grad


def attend_back_first(own_ref, near_ref, w_out_ref, first_ref, second_ref, logs_ref, query_ref, key_ref, value_ref):
    rows = jnp.concatenate([own_ref[...], near_ref[...]], axis=0)
    grad = dot(rows, w_out_ref[...], 1, 1).astype(BF16)
    keys = jnp.concatenate([first_ref[1], second_ref[1]], axis=0)
    values = jnp.concatenate([first_ref[2], second_ref[2]], axis=0)
    query_ref[...], key_ref[...], value_ref[...] = attend_grad(
        grad, first_ref[0], keys, values, logs_ref
    )


def project_back(rows_ref, start, count, w_ref):
    total = dot(rows_ref[0, start : start + count], w_ref[0], 1, 1)
    for i in range(1, 3):
        total = total + dot(rows_ref[i, start : start + count], w_ref[i], 1, 1)
    return total


def attend_back_second(
    own_ref,
    near_ref,
    w_out_ref,
    first_ref,
    second_ref,
    logs_ref,
    query_ref,
    key_ref,
    value_ref,
    w_ref,
    out_ref,
    keep_ref,
    send_ref,
):
    rows = jnp.concatenate([own_ref[...], near_ref[...]], axis=0)
    half = rows.shape[0]
    grad = dot(rows, w_out_ref[...], 1, 1).astype(BF16)
    keys = jnp.concatenate([first_ref[1], second_ref[1]], axis=0)
    values = jnp.concatenate([first_ref[2], second_ref[2]], axis=0)
    query_grad, key_grad, value_grad = attend_grad(grad, second_ref[0], keys, values, logs_ref)
    out_ref[0, 0:half] = query_ref[...]
    out_ref[0, half:] = query_grad
    out_ref[1] = (key_ref[...] + key_grad).astype(BF16)
    out_ref[2] = (value_ref[...] + value_grad).astype(BF16)
    split_out(project_back(out_ref, 0, half, w_ref), keep_ref, send_ref)


def attend_back_last(rows_ref, w_ref, keep_ref, send_ref):
    half = rows_ref.shape[1] // 2
    split_out(project_back(rows_ref, half, half, w_ref), keep_ref, send_ref)


def hidden_back(own_ref, near_ref, w_ref, out_ref):
    rows = jnp.concatenate([own_ref[...], near_ref[...]], axis=0)
    out_ref[...] = dot(rows, w_ref[...], 1, 1)


ROOT = 0.7978845608028654
CUBE = 0.044715


def mlp(own_ref, near_ref, w_ref, grad_ref, hidden_ref, out_ref, keep_ref, send_ref):
    rows = jnp.concatenate([own_ref[...], near_ref[...]], axis=0)
    pre = dot(rows, w_ref[...])
    square = pre * pre
    bend = jnp.tanh(ROOT * pre * (1.0 + CUBE * square))
    half = 0.5 * (1.0 + bend)
    hidden_ref[...] = (pre * half).astype(BF16)
    slope = half + (0.5 * ROOT) * pre * (1.0 - bend * bend) * (1.0 + (3.0 * CUBE) * square)
    out_ref[...] = (slope * grad_ref[...]).astype(BF16)
    split_out(dot(out_ref[...], w_ref[...], 1, 1), keep_ref, send_ref)


def mlp_out(first_ref, second_ref, w_ref, keep_a_ref, send_a_ref, keep_b_ref, send_b_ref):
    split_out(dot(first_ref[...], w_ref[...]), keep_a_ref, send_a_ref)
    split_out(dot(second_ref[...], w_ref[...]), keep_b_ref, send_b_ref)


def grad_rows(parts, step, width, which):
    groups = width // (2 * step)
    outs = []
    for group in range(groups):
        start = pl.multiple_of((2 * group + which) * step, LANES)
        line = []
        for left, rights in parts:
            picked = jnp.concatenate([ref[:, pl.ds(start, step)] for ref in left], axis=0)
            line.extend(dot(picked, right, 0, 0) for right in rights)
        outs.append(line)
    return outs, groups


def write_half(ref, parts, step, width, which, dtype):
    outs, groups = grad_rows(parts, step, width, which)
    for group in range(groups):
        column = 0
        for value in outs[group]:
            ref[group * step : (group + 1) * step, column : column + value.shape[1]] = value.astype(dtype)
            column += value.shape[1]


def take_half(out_ref, source, step, which, dtype):
    for group in range(source.shape[0] // (2 * step)):
        start = pl.multiple_of((2 * group + which) * step, 16)
        out_ref[group * step : (group + 1) * step] = source[pl.ds(start, step)].astype(dtype)


def sum_start(load, step, bit, *refs):
    *inputs, out_ref = refs
    parts, width = load(inputs)
    write_half(out_ref, parts, step, width, 1 - my_bit(bit), BF16)


def sum_second(load, step, next_step, bit, next_bit, *refs):
    got_ref, *inputs, keep_ref, send_ref, total = refs
    parts, width = load(inputs)
    write_half(total, parts, step, width, my_bit(bit), F32)
    total[...] = total[...] + got_ref[...].astype(F32)
    take_half(send_ref, total, next_step, 1 - my_bit(next_bit), BF16)
    take_half(keep_ref, total, next_step, my_bit(next_bit), F32)


def sum_next(next_step, next_bit, kept_ref, got_ref, keep_ref, send_ref, total):
    total[...] = kept_ref[...] + got_ref[...].astype(F32)
    take_half(send_ref, total, next_step, 1 - my_bit(next_bit), BF16)
    take_half(keep_ref, total, next_step, my_bit(next_bit), F32)


def load_plain(inputs):
    *left, first, second = inputs
    right = jnp.concatenate([first[...], second[...]], axis=0)
    return [(left, [right])], left[0].shape[1]


def load_attn(inputs):
    left, middle = inputs[0:4], inputs[4:8]
    proj, first, second = inputs[8:]
    attended = jnp.concatenate([first[...], second[...]], axis=0)
    return [(left, [proj[0], proj[1], proj[2]]), (middle, [attended])], left[0].shape[1]


def last_plain(kept_ref, got_ref, out_ref):
    out_ref[...] = kept_ref[...] + got_ref[...].astype(F32)


def last_turned(kept_ref, got_ref, out_ref):
    out_ref[...] = (kept_ref[...] + got_ref[...].astype(F32)).T


def last_attn(kept_ref, got_ref, proj_ref, out_ref):
    total = kept_ref[...] + got_ref[...].astype(F32)
    width = proj_ref.shape[2]
    for i in range(3):
        proj_ref[i] = total[:, i * width : (i + 1) * width]
    out_ref[...] = total[:, 3 * width :].T


def mix_lines(samples, lines, bucket_ref, inputs, rest_ref):
    first_ref, second_ref, own_ref, near_ref = inputs
    quarter, width = first_ref.shape
    rest_ref[0:quarter] = jnp.where(my_chip() == 0, first_ref[...], second_ref[...])
    sample = lax.axis_index("dp")
    sums = own_ref[...] + near_ref[...]
    row = iota((lines, width), 0)
    filled = jnp.concatenate([sums, jnp.zeros((lines - 8, width), F32)], axis=0)
    filled = jnp.where(row < 4, filled, 0.0)
    filled = jnp.where(row == 4 + sample, sums[4:5], filled)
    bucket = bucket_ref[0].astype(F32)
    rest_ref[quarter:] = jnp.where(row == 4 + samples + sample, bucket, filled)


def write_mix(ref, step, which, inputs, rest_ref, dtype):
    left, mixed_ref = inputs[0:4], inputs[4]
    width = left[0].shape[1]
    heads_width = mixed_ref.shape[0]
    for group in range(width // (2 * step)):
        start = pl.multiple_of((2 * group + which) * step, LANES)
        picked = jnp.concatenate([part[:, pl.ds(start, step)] for part in left], axis=0)
        rows = slice(group * step, (group + 1) * step)
        ref[rows, 0:heads_width] = dot(picked, mixed_ref[...], 0, 1).astype(dtype)
        ref[rows, heads_width:] = rest_ref[:, pl.ds(start, step)].T.astype(dtype)


def mix_start(samples, lines, step, bit, bucket_ref, *refs):
    *inputs, out_ref, rest = refs
    mix_lines(samples, lines, bucket_ref, inputs[5:], rest)
    write_mix(out_ref, step, 1 - my_bit(bit), inputs, rest, BF16)


def mix_second(samples, lines, step, next_step, bit, next_bit, bucket_ref, *refs):
    got_ref, *inputs, keep_ref, send_ref, rest, total = refs
    mix_lines(samples, lines, bucket_ref, inputs[5:], rest)
    write_mix(total, step, my_bit(bit), inputs, rest, F32)
    total[...] = total[...] + got_ref[...].astype(F32)
    take_half(send_ref, total, next_step, 1 - my_bit(next_bit), BF16)
    take_half(keep_ref, total, next_step, my_bit(next_bit), F32)


def mix_last(samples, quarter, final, kept_ref, got_ref, out_ref, pos_ref, lead_ref, small_ref):
    total = kept_ref[...] + got_ref[...].astype(F32)
    heads_width = out_ref.shape[0]
    out_ref[...] = total[:, :heads_width].T
    pos_ref[...] = total[:, heads_width : heads_width + quarter].T
    rest = total[:, heads_width + quarter :]
    rows = max(final, 8)
    mine = iota((rows, rest.shape[0]), 1) == iota((rows, rest.shape[0]), 0) + lax.axis_index("mp") * final
    own = dot(mine.astype(F32), rest, precision=HIGH)
    bucket = iota((rows, lead_ref.shape[1]), 1).astype(F32)
    lead = jnp.zeros(bucket.shape, F32)
    for s in range(samples):
        mark = own[:, 4 + samples + s : 5 + samples + s]
        lead = jnp.where(bucket == mark, lead + own[:, 4 + s : 5 + s], lead)
    lead_ref[...] = lead[:final]
    small_ref[...] = own.T[0:8, :final]


def mass_add(mass_ref, got_ref, bias_ref, bias_got_ref, out_ref, low_ref, bias_out_ref):
    total = mass_ref[...] + got_ref[...].astype(F32)
    out_ref[...] = total
    low_ref[...] = total.astype(BF16)
    bias_out_ref[...] = bias_ref[...] + bias_got_ref[...]


def mix_finish(
    mass_ref,
    got_ref,
    bias_ref,
    bias_got_ref,
    query_col_ref,
    keys_t_ref,
    table_ref,
    w_ref,
    query_ref,
    grad_ref,
    keep_ref,
    send_ref,
    scratch,
):
    width, rows = mass_ref.shape
    heads = width // HEAD_DIM
    mass = (mass_ref[...] + got_ref[...].astype(F32)).astype(BF16)
    sums = bias_ref[...] + bias_got_ref[...]
    bias = jnp.concatenate(
        [jnp.broadcast_to(sums[head : head + 1], (HEAD_DIM, rows)) for head in range(heads)], axis=0
    )
    key_mass = (bias * query_col_ref[:, 0:1]).astype(BF16)
    total = jnp.sum(keys_t_ref[...] * bias, axis=1, keepdims=True)
    own = grad_ref.shape[1]
    start = lax.axis_index("dp") * own
    model_width = table_ref.shape[1]
    mine = exact(iota((own, model_width), 1) == iota((own, model_width), 0) + start)
    total_row = jnp.broadcast_to(total, (width, LANES)).T[0:1]
    table_t = dot(mine, table_ref[...], 1, 1).astype(BF16)
    query_rows = jnp.broadcast_to(query_ref[...].astype(F32)[None], (16, model_width)).astype(BF16)
    grad_ref[0] = dot(mine, query_rows, 1, 1)[:, 0:1] * total_row
    grad_ref[1] = dot(table_t, key_mass, 1, 1)
    grad_ref[2] = dot(table_t, mass, 1, 1)
    back = dot(w_ref[1], key_mass) + dot(w_ref[2], mass)
    query_back = jnp.sum(w_ref[0].astype(F32) * total_row, axis=1, keepdims=True)
    scratch[...] = jnp.where(iota((own, rows), 1) == rows - 1, query_back, back)
    keep_part(scratch, keep_ref, send_ref, my_chip())


def keep_part(source, keep_ref, send_ref, which):
    step = keep_ref.shape[0]
    if step % 8:
        first, second = source[0:step], source[step : 2 * step]
        keep_ref[...] = jnp.where(which == 0, first, second)
        send_ref[...] = jnp.where(which == 0, second, first)
    else:
        keep_ref[...] = source[pl.ds(pl.multiple_of(which * step, 8), step)]
        send_ref[...] = source[pl.ds(pl.multiple_of((1 - which) * step, 8), step)]


def tables_next(kept_ref, got_ref, keep_ref, send_ref, scratch):
    scratch[...] = kept_ref[...] + got_ref[...]
    keep_part(scratch, keep_ref, send_ref, my_core())


def pair_sum(keep_ref, got_ref, out_ref, low_ref):
    total = keep_ref[...] + got_ref[...].astype(F32)
    out_ref[...] = total
    low_ref[...] = total.astype(BF16)


def by_chip(own_ref, far_ref, first_ref, second_ref):
    own, far = own_ref[...], far_ref[...]
    first = my_chip() == 0
    first_ref[...] = jnp.where(first, own, far)
    second_ref[...] = jnp.where(first, far, own)


def base_rows(bucket_ref, first_ref, second_ref, lead_ref, out_a_ref, out_b_ref):
    rows = lead_ref.shape[0]
    mark = exact(iota((16, rows), 1) == bucket_ref[0])
    lead = dot(mark, lead_ref[...])[0:1]
    out_a_ref[...] = first_ref[...].astype(F32) + lead
    out_b_ref[...] = second_ref[...].astype(F32) + lead


def field_sum(keep_ref, got_ref, own_ref, send_ref):
    total = keep_ref[...] + got_ref[...].astype(F32)
    quarter = own_ref.shape[1]
    first = my_chip() == 0
    own_ref[...] = jnp.where(first, total[:, :quarter], total[:, quarter:])
    send_ref[...] = jnp.where(first, total[:, quarter:], total[:, :quarter]).astype(BF16)


def field_last(own_ref, far_ref, out_ref):
    out_ref[0] = own_ref[...] + far_ref[...].astype(F32)


def rows_sum(keep_a_ref, got_a_ref, keep_b_ref, got_b_ref, mid_a_ref, mid_b_ref, own_ref, send_ref):
    part_a = keep_a_ref[...] + got_a_ref[...].astype(F32)
    part_b = keep_b_ref[...] + got_b_ref[...].astype(F32)
    first = my_chip() == 0
    own_ref[...] = jnp.where(first, part_a + mid_a_ref[...], part_b + mid_b_ref[...])
    send_ref[...] = jnp.where(first, part_b, part_a).astype(BF16)


def tables_last(pixels, variables, kept_ref, got_ref, patch_ref, variable_ref, query_ref):
    total = kept_ref[...] + got_ref[...]
    for p in range(pixels):
        patch_ref[p] = total[:, p * variables : (p + 1) * variables]
    variable_ref[...] = total[:, pixels * variables : (pixels + 1) * variables]
    query_ref[...] = total.T[total.shape[1] - 8 :]


def pairs(count, bit):
    return [(i, i ^ bit) for i in range(count)]


def body(
    mesh_dp,
    mesh_mp,
    input_field,
    variable_ids,
    lead_bucket,
    patch_table,
    variable_table,
    variable_query,
    mix_weights,
    mix_output,
    pos_table,
    lead_table,
    first_gain,
    first_bias,
    attn_weights,
    attn_output,
    second_gain,
    second_bias,
    up_weight,
    down_weight,
    cotangent,
):
    length = input_field.shape[2]
    channels = input_field.shape[1]
    variables = variable_ids.shape[0]
    pixels = channels // variables
    model_width = pos_table.shape[1]
    quarter = cotangent.shape[0]
    head_width = mix_weights.shape[2]
    hidden_width = up_weight.shape[1]
    heads = head_width // HEAD_DIM
    own_width = model_width // mesh_dp
    half = 2 * quarter
    rows32 = ((quarter, model_width), F32)
    rows16 = ((quarter, model_width), BF16)

    def swap_core(value):
        return lax.ppermute(value, "mp", pairs(mesh_mp, 1))

    def swap_chip(value):
        return lax.ppermute(value, "mp", pairs(mesh_mp, 2))

    def add_core(keep, send):
        kept, low = call(pair_sum, [rows32, rows16], [keep, swap_core(send)], cost=0.3)
        return kept, swap_chip(low)

    def swap_sample(value, bit):
        return lax.ppermute(value, "dp", pairs(mesh_dp, bit))

    all_bits = [1 << i for i in range(mesh_dp.bit_length() - 1)]
    wide = [bit for bit in all_bits if bit * own_width % LANES == 0]

    def order_from(which):
        first = all_bits.index(wide[which % len(wide)])
        return all_bits[first:] + all_bits[:first]

    def steps_of(order):
        left = list(all_bits)
        steps = []
        for bit in order:
            steps.append(own_width << left.index(bit))
            left.remove(bit)
        return steps

    def start_sum(load, inputs, width, order, after=()):
        step = steps_of(order)[0]
        (send,) = call(
            functools.partial(sum_start, load, step, order[0]),
            [((model_width // 2, width), BF16)],
            inputs,
            after=after,
        )
        return send, swap_sample(send, order[0])

    def halves(width, scratch_rows):
        kept = scratch_rows // 2
        return [((kept, width), F32), ((kept, width), BF16)]

    def second_sum(load, inputs, got, width, order, after=()):
        steps = steps_of(order)
        rows = model_width // 2
        keep, send = call(
            functools.partial(sum_second, load, steps[0], steps[1], order[0], order[1]),
            halves(width, rows),
            [got] + inputs,
            after=after,
            scratch=[pltpu.VMEM((rows, width), F32)],
        )
        return keep, swap_sample(send, order[1])

    def rest_sum(keep, got, order):
        steps = steps_of(order)
        for i in range(2, len(order)):
            rows, width = keep.shape
            keep, send = call(
                functools.partial(sum_next, steps[i], order[i]),
                halves(width, rows),
                [keep, got],
                scratch=[pltpu.VMEM((rows, width), F32)],
            )
            got = swap_sample(send, order[i])
        return keep, got

    cot_a0, cot_b0 = call(by_chip, [rows16] * 2, [cotangent, swap_chip(cotangent)], cost=0.3)
    cot_a1 = swap_core(cot_a0)
    cot_b1 = swap_core(cot_b0)

    w_mix = mix_weights.transpose(1, 0, 2)
    w_attn = attn_weights.transpose(1, 0, 2)
    gain_one, bias_one = first_gain[None], first_bias[None]
    gain_two, bias_two = second_gain[None], second_bias[None]
    table_rows = channels + variables
    padded = -(-(table_rows + 1) // LANES) * LANES
    (
        table,
        pick,
        field_t,
        probs,
        values,
        keys_t,
        score,
        query_col,
        mixed_t,
        send_a,
        send_b,
        keep_a,
        keep_b,
    ) = call(
        functools.partial(mix_forward, pixels, quarter),
        [
            ((padded, model_width), BF16),
            ((channels, channels), BF16),
            ((channels, length), BF16),
            ((heads * variables, length), F32),
            ((padded, head_width), BF16),
            ((head_width, padded), F32),
            ((padded, LANES), F32),
            ((head_width, LANES), F32),
            ((head_width, length), BF16),
            rows16,
            rows16,
            rows32,
            rows32,
        ],
        [variable_query],
        fetch=[input_field, patch_table, variable_table, w_mix, mix_output],
        smem=[variable_ids],
    )
    blocks = [
        (pos_table, (quarter, model_width), lambda ref, k=k: ref.at[pl.ds((2 * k + my_core()) * quarter, quarter)])
        for k in range(2)
    ]
    base_a, base_b = call(
        base_rows, [rows32] * 2, [], fetch=blocks + [lead_table], smem=[lead_bucket], cost=0.3
    )
    kept_a, far_a = add_core(keep_a, send_a)
    kept_b, far_b = add_core(keep_b, send_b)

    def norm_rows(terms, gain, bias, after=()):
        return call(norm_forward, [rows32, rows16], terms + [gain, bias], after=after, cost=0.5)

    in_a, one_a0 = norm_rows([kept_a, far_a, base_a], gain_one, bias_one)
    one_a1 = swap_core(one_a0)
    proj_kind = ((3, half, head_width), BF16)
    (proj_a,) = call(project, [proj_kind], [one_a0, one_a1, w_attn])
    (grad_hidden_a,) = call(hidden_back, [((half, hidden_width), F32)], [cot_a0, cot_a1, down_weight])
    (grad_hidden_b,) = call(hidden_back, [((half, hidden_width), F32)], [cot_b0, cot_b1, down_weight])
    in_b, one_b0 = norm_rows(
        [kept_b, far_b, base_b], gain_one, bias_one, after=[grad_hidden_a, grad_hidden_b]
    )
    one_b1 = swap_core(one_b0)
    attend_kinds = [((half, head_width), BF16), ((8, half), F32), rows32, rows16]
    proj_b, attended_a, logs_a, keep_a, send_a = call(
        attend_first,
        [proj_kind] + attend_kinds,
        [one_b0, one_b1, w_attn, proj_a, attn_output],
    )
    attended_b, logs_b, keep_b, send_b = call(
        attend_second, attend_kinds, [proj_a, proj_b, attn_output]
    )
    kept_a, far_a = add_core(keep_a, send_a)
    kept_b, far_b = add_core(keep_b, send_b)
    mid_a, two_a0 = norm_rows([kept_a, far_a, in_a], gain_two, bias_two)
    two_a1 = swap_core(two_a0)
    mlp_kinds = [((half, hidden_width), BF16)] * 2 + [rows32, rows16]
    hidden_a, pre_a, keep_a, send_a = call(mlp, mlp_kinds, [two_a0, two_a1, up_weight, grad_hidden_a])
    kept_a, far_a = add_core(keep_a, send_a)
    mid_b, two_b0 = norm_rows([kept_b, far_b, in_b], gain_two, bias_two)
    two_b1 = swap_core(two_b0)
    hidden_b, pre_b, keep_b, send_b = call(mlp, mlp_kinds, [two_b0, two_b1, up_weight, grad_hidden_b])
    kept_b, far_b = add_core(keep_b, send_b)

    down_order, up_order, attn_order, mix_order = (order_from(i) for i in (1, 0, 0, 0))
    down_in = [cot_a0, cot_a1, cot_b0, cot_b1, hidden_a, hidden_b]
    up_in = [two_a0, two_a1, two_b0, two_b1, pre_a, pre_b]
    down_send, down_got = start_sum(load_plain, down_in, hidden_width, down_order)
    up_send, up_got = start_sum(load_plain, up_in, hidden_width, up_order)

    sums_kind = ((8, model_width), F32)
    back_kinds = [rows32, rows16, sums_kind]
    back_two = functools.partial(norm_backward, False, 0)
    grad_mid_a, mid_a0, sums_two_a = call(
        back_two,
        back_kinds,
        [kept_a, far_a, mid_a, gain_two, cot_a0],
        after=[down_send, up_send],
        cost=0.5,
    )
    mid_a1 = swap_core(mid_a0)
    grad_kinds = [((half, head_width), BF16)] + [((length, head_width), F32)] * 2
    query_grad, key_grad, value_grad = call(
        attend_back_first, grad_kinds, [mid_a0, mid_a1, attn_output, proj_a, proj_b, logs_a]
    )
    grad_mid_b, mid_b0, sums_two_b = call(
        back_two, back_kinds, [kept_b, far_b, mid_b, gain_two, cot_b0], cost=0.5
    )
    mid_b1 = swap_core(mid_b0)
    grad_proj, keep_a, send_a = call(
        attend_back_second,
        [((3, length, head_width), BF16), rows32, rows16],
        [
            mid_b0,
            mid_b1,
            attn_output,
            proj_a,
            proj_b,
            logs_b,
            query_grad,
            key_grad,
            value_grad,
            w_attn,
        ],
    )
    kept_a, far_a = add_core(keep_a, send_a)
    keep_b, send_b = call(attend_back_last, [rows32, rows16], [grad_proj, w_attn])
    kept_b, far_b = add_core(keep_b, send_b)

    attn_in = [one_a0, one_a1, one_b0, one_b1, mid_a0, mid_a1, mid_b0, mid_b1, grad_proj, attended_a, attended_b]
    attn_width = 4 * head_width
    attn_send, attn_got = start_sum(load_attn, attn_in, attn_width, attn_order)
    down_keep, down_got = second_sum(load_plain, down_in, down_got, hidden_width, down_order)
    up_keep, up_got = second_sum(load_plain, up_in, up_got, hidden_width, up_order)

    grad_in_a, in_a0, sums_one_a = call(
        functools.partial(norm_backward, True, 0),
        back_kinds,
        [kept_a, far_a, in_a, gain_one, grad_mid_a],
        after=[attn_send, down_keep, up_keep],
        cost=0.5,
    )
    in_a1 = swap_core(in_a0)
    grad_in_b, in_b0, sums = call(
        functools.partial(norm_backward, True, 3),
        back_kinds,
        [kept_b, far_b, in_b, gain_one, grad_mid_b, sums_one_a, sums_two_a, sums_two_b],
        cost=0.5,
    )
    in_b1 = swap_core(in_b0)
    near_sums = swap_core(sums)
    mass, mass_low, bias, field_send, field_keep = call(
        functools.partial(mix_backward, pixels),
        [
            ((head_width, padded), F32),
            ((head_width, padded), BF16),
            ((8, padded), F32),
            ((channels, half), BF16),
            ((channels, half), F32),
        ],
        [pick, field_t, probs, values, score, mix_output, in_a0, in_a1, in_b0, in_b1],
    )
    mass_kinds = [
        ((head_width, padded), F32),
        ((head_width, padded), BF16),
        ((8, padded), F32),
    ]
    for bit in all_bits[:-1]:
        mass, mass_low, bias = call(
            mass_add,
            mass_kinds,
            [mass, swap_sample(mass_low, bit), bias, swap_sample(bias, bit)],
            cost=0.3,
        )
    mass_got = swap_sample(mass_low, all_bits[-1])
    bias_got = swap_sample(bias, all_bits[-1])

    (own_weights,) = call(
        lambda source, out: out.__setitem__(Ellipsis, source[...]),
        [((3, own_width, head_width), BF16)],
        [],
        fetch=[
            (
                w_mix,
                (3, own_width, head_width),
                lambda ref: ref.at[:, pl.ds(lax.axis_index("dp") * own_width, own_width)],
            )
        ],
        cost=0.1,
    )
    lines = -(-(4 + 2 * mesh_dp) // LANES) * LANES
    mix_in = [in_a0, in_a1, in_b0, in_b1, mixed_t, grad_in_a, grad_in_b, sums, near_sums]
    mix_width = head_width + quarter + lines
    steps = steps_of(mix_order)
    rest = pltpu.VMEM((quarter + lines, model_width), F32)
    (send,) = call(
        functools.partial(mix_start, mesh_dp, lines, steps[0], mix_order[0]),
        [((model_width // 2, mix_width), BF16)],
        mix_in,
        smem=[lead_bucket],
        scratch=[rest],
    )
    got = swap_sample(send, mix_order[0])
    mix_keep, send = call(
        functools.partial(mix_second, mesh_dp, lines, steps[0], steps[1], mix_order[0], mix_order[1]),
        halves(mix_width, model_width // 2),
        [got] + mix_in,
        smem=[lead_bucket],
        scratch=[rest, pltpu.VMEM((model_width // 2, mix_width), F32)],
    )
    mix_keep, mix_got = rest_sum(mix_keep, swap_sample(send, mix_order[1]), mix_order)

    own_field = (channels, quarter)
    field_own, field_far = call(
        field_sum, [(own_field, F32), (own_field, BF16)], [field_keep, swap_core(field_send)], cost=0.3
    )
    (field_grad,) = call(
        field_last, [((1,) + own_field, F32)], [field_own, swap_chip(field_far)], cost=0.3
    )

    attn_keep, attn_got = second_sum(load_attn, attn_in, attn_got, attn_width, attn_order)
    down_keep, down_got = rest_sum(down_keep, down_got, down_order)
    up_keep, up_got = rest_sum(up_keep, up_got, up_order)
    attn_keep, attn_got = rest_sum(attn_keep, attn_got, attn_order)

    keep_a, send_a, keep_b, send_b = call(
        mlp_out, [rows32, rows16] * 2, [hidden_a, hidden_b, down_weight], after=[in_b0]
    )
    rows_own, rows_far = call(
        rows_sum,
        [rows32, rows16],
        [keep_a, swap_core(send_a), keep_b, swap_core(send_b), mid_a, mid_b],
        cost=0.3,
    )
    (activations,) = call(last_plain, [rows32], [rows_own, swap_chip(rows_far)], cost=0.3)

    final = own_width // mesh_mp
    grad_mix, keep, send = call(
        mix_finish,
        [((3, own_width, head_width), F32)] + [((own_width // 2, padded), F32)] * 2,
        [mass, mass_got, bias, bias_got, query_col, keys_t, table, own_weights, variable_query],
        scratch=[pltpu.VMEM((own_width, padded), F32)],
    )
    keep, send = call(
        tables_next,
        [((final, padded), F32)] * 2,
        [keep, swap_chip(send)],
        scratch=[pltpu.VMEM((own_width // 2, padded), F32)],
        cost=0.3,
    )
    patch_total, variable_total, query_total = call(
        functools.partial(tables_last, pixels, variables),
        [((pixels, final, variables), F32), ((final, variables), F32), ((8, final), F32)],
        [keep, swap_core(send)],
    )
    (down_sum,) = call(last_turned, [((hidden_width, own_width), F32)], [down_keep, down_got])
    (up_sum,) = call(last_plain, [((own_width, hidden_width), F32)], [up_keep, up_got])
    attn_sum, attn_out_sum = call(
        last_attn,
        [((3, own_width, head_width), F32), ((head_width, own_width), F32)],
        [attn_keep, attn_got],
    )
    mix_out_sum, pos_sum, lead_total, small = call(
        functools.partial(mix_last, mesh_dp, quarter, final),
        [
            ((head_width, own_width), F32),
            ((quarter, own_width), F32),
            ((final, lead_table.shape[0]), F32),
            ((8, final), F32),
        ],
        [mix_keep, mix_got],
    )
    return (
        activations,
        field_grad,
        patch_total.transpose(2, 0, 1),
        variable_total.T,
        query_total[7],
        grad_mix.transpose(1, 0, 2),
        mix_out_sum,
        pos_sum,
        lead_total.T,
        small[0],
        small[1],
        attn_sum.transpose(1, 0, 2),
        attn_out_sum,
        small[2],
        small[3],
        up_sum,
        down_sum,
    )


def solution(mesh):
    in_specs = (
        P("dp", None, None),
        P(),
        P("dp"),
        P(),
        P(),
        P(),
        P(None, None, "mp"),
        P("mp", None),
        P(),
        P(),
        P(),
        P(),
        P(None, None, "mp"),
        P("mp", None),
        P(),
        P(),
        P(None, "mp"),
        P("mp", None),
        P(("dp", "mp"), None),
    )
    out_specs = (
        P(("dp", "mp"), None),
        P("dp", None, "mp"),
        P(None, None, ("dp", "mp")),
        P(None, ("dp", "mp")),
        P(("dp", "mp")),
        P("dp", None, "mp"),
        P("mp", "dp"),
        P("mp", "dp"),
        P(None, ("dp", "mp")),
        P(("dp", "mp")),
        P(("dp", "mp")),
        P("dp", None, "mp"),
        P("mp", "dp"),
        P(("dp", "mp")),
        P(("dp", "mp")),
        P("dp", "mp"),
        P("mp", "dp"),
    )
    step = functools.partial(body, mesh.shape["dp"], mesh.shape["mp"])
    return jax.shard_map(step, mesh=mesh, in_specs=in_specs, out_specs=out_specs, check_vma=False)
```

profile of v0, /device:TPU:0, one launch (start us, length us, event | category | flops | bytes accessed | tf_op | source)
XLA Modules:
  0.0 192.7 jit_solution(12442373395707769537)
XLA Ops:
  7.3 3.5 %shard_map.314 = (bf16[256,1024]{1,0:T(8,128)(2,1)S(1)}, bf16[192,192]{1,0:T(8,128)(2,1)S(1)}, bf16[192,512]{1,0:T(8,128)(2,1)S(1)}, f32[192,512]{1,0:T(8,128)S(...) custom-call(s32[48]{0:T(128)S(1)} %copy-done.20, ...), custom_call_target="tpu_custom_call" | custom-call | flops 1000000000 | tf_op jit(solution)/shard_map/pallas_call | solution.py:59
  11.3 2.6 %collective-permute-start.2 = (bf16[128,1024]{1,0:T(8,128)(2,1)S(1)}, bf16[128,1024]{1,0:T(8,128)(2,1)S(1)}, u32[]{:S(2)}, u32[]{:S(2)}) collective-permute-start(bf16[128,1024]{1,0:T(8,128)(2,1)S(1)} %copy-done.14), channel_id=1, source_target_pairs={{0,2},{1,3},{2,0},{3,1},{4,6},{5,7},{6,4},{7,5},{8,10},{9,11},{10,... | collective-permute-start | bytes 786440 | tf_op jit(solution)/shard_map/ppermute | solution.py:736
  15.6 5.5 %collective-permute-done.2.refs_1_ = bf16[128,1024]{1,0:T(8,128)(2,1)S(1)} collective-permute-done((bf16[128,1024]{1,0:T(8,128)(2,1)S(1)}, bf16[128,1024]{1,0:T(8,128)(2,1)S(1)}, u32[]{:S(2)}, u32[]{:S(2)}) %collective-permute-start.2) | collective-permute-done | bytes 262176 | tf_op jit(solution)/shard_map/ppermute | solution.py:736
  22.5 2.0 %collective-permute-start.1 = (bf16[128,1024]{1,0:T(8,128)(2,1)S(1)}, bf16[128,1024]{1,0:T(8,128)(2,1)S(1)}, u32[]{:S(2)}, u32[]{:S(2)}) collective-permute-start(bf16[128,1024]{1,0:T(8,128)(2,1)S(1)} %get-tuple-element.147), channel_id=1, source_target_pairs={{0,2},{1,3},{2,0},{3,1},{4,6},{5,7},{6,4},{7,5},{8,10},{9,11},{10,... | collective-permute-start | bytes 786440 | tf_op jit(solution)/shard_map/ppermute | solution.py:736
  28.6 3.4 %collective-permute-done.1.refs_1_ = bf16[128,1024]{1,0:T(8,128)(2,1)S(1)} collective-permute-done((bf16[128,1024]{1,0:T(8,128)(2,1)S(1)}, bf16[128,1024]{1,0:T(8,128)(2,1)S(1)}, u32[]{:S(2)}, u32[]{:S(2)}) %collective-permute-start.1) | collective-permute-done | bytes 262176 | tf_op jit(solution)/shard_map/ppermute | solution.py:736
  34.0 2.8 %shard_map.324 = (bf16[3,256,256]{2,1,0:T(8,128)(2,1)S(1)}, bf16[256,256]{1,0:T(8,128)(2,1)S(1)}, f32[8,256]{1,0:T(8,128)S(1)}, f32[128,1024]{1,0:T(8,128)S(1)}, bf16[128,1024]{1,0:T(8,128)(2,1)S(1)}) custom-call(bf16[128,1024]{1,0:T(8,128)(2,1)S(1)} %get-tuple-element.151.refs_0_.refs_2_.refs_3_, ...), custom_call_target="tpu_custom_call" | custom-call | flops 1000000000 | tf_op jit(solution)/shard_map/pallas_call | solution.py:59
  37.0 2.2 %shard_map.328 = (bf16[256,256]{1,0:T(8,128)(2,1)S(1)}, f32[8,256]{1,0:T(8,128)S(1)}, f32[128,1024]{1,0:T(8,128)S(1)}, bf16[128,1024]{1,0:T(8,128)(2,1)S(1)}) custom-call(bf16[3,256,256]{2,1,0:T(8,128)(2,1)S(1)} %shard_map.323.refs_3_.refs_0_, bf16[3,256,256]{2,1,0:T(8,128)(2,1)S(1)} %get-tuple-element.165.refs_1_.refs_4_, bf16[256,1024]{1,0:T(8,128)(2,1)S(1)} %copy-done.4), custom_call_target="tpu_custom_call" | custom-call | flops 1000000000 | tf_op jit(solution)/shard_map/pallas_call | solution.py:59
  39.7 1.8 collective-permute-start.10
  42.7 6.2 %collective-permute-done.10.refs_1_ = bf16[128,1024]{1,0:T(8,128)(2,1)S(1)} collective-permute-done((bf16[128,1024]{1,0:T(8,128)(2,1)S(1)}, bf16[128,1024]{1,0:T(8,128)(2,1)S(1)}, u32[]{:S(2)}, u32[]{:S(2)}) %collective-permute-start.10) | collective-permute-done | bytes 262176 | tf_op jit(solution)/shard_map/ppermute | solution.py:736
  49.2 4.5 %collective-permute-done.13.refs_1_ = bf16[128,1024]{1,0:T(8,128)(2,1)S(1)} collective-permute-done((bf16[128,1024]{1,0:T(8,128)(2,1)S(1)}, bf16[128,1024]{1,0:T(8,128)(2,1)S(1)}, u32[]{:S(2)}, u32[]{:S(2)}) %collective-permute-start.13) | collective-permute-done | bytes 262176 | tf_op jit(solution)/shard_map/ppermute | solution.py:736
  54.1 1.9 shard_map.327
  56.5 1.9 shard_map.331
  58.6 1.8 collective-permute-start.19
  68.6 4.4 %collective-permute-done.16.refs_1_ = bf16[128,1024]{1,0:T(8,128)(2,1)S(1)} collective-permute-done((bf16[128,1024]{1,0:T(8,128)(2,1)S(1)}, bf16[128,1024]{1,0:T(8,128)(2,1)S(1)}, u32[]{:S(2)}, u32[]{:S(2)}) %collective-permute-start.16) | collective-permute-done | bytes 262176 | tf_op jit(solution)/shard_map/ppermute | solution.py:736
  73.6 2.8 %shard_map.338 = (bf16[256,256]{1,0:T(8,128)(2,1)S(1)}, f32[512,256]{1,0:T(8,128)S(1)}, f32[512,256]{1,0:T(8,128)S(1)}) custom-call(bf16[128,1024]{1,0:T(8,128)(2,1)S(1)} %get-tuple-element.187.refs_0_.refs_4_.refs_5_, bf16[128,1024]{1,0:T(8,128)(2,1)S(1)} %collective-permute-done.20.refs_1_.refs_5_.refs_6_, bf16[256,1024]{1,0:T(8,128)(2,1)S(1)} %copy-done.4, ...), custom_call_target="tpu_custom_call" | custom-call | flops 1000000000 | tf_op jit(solution)/shard_map/pallas_call | solution.py:59
  76.4 3.2 %shard_map.339 = (bf16[3,512,256]{2,1,0:T(8,128)(2,1)S(1)}, f32[128,1024]{1,0:T(8,128)S(1)}, bf16[128,1024]{1,0:T(8,128)(2,1)S(1)}) custom-call(bf16[128,1024]{1,0:T(8,128)(2,1)S(1)} %get-tuple-element.178.refs_0_.refs_6_.refs_7_, bf16[128,1024]{1,0:T(8,128)(2,1)S(1)} %collective-permute-done.17.refs_1_.refs_7_.refs_8_, bf16[256,1024]{1,0:T(8,128)(2,1)S(1)} %copy-done.4, ...), custom_call_target="tpu_custom_call" | custom-call | flops 1000000000 | tf_op jit(solution)/shard_map/pallas_call | solution.py:59
  81.4 1.8 collective-permute-start.24
  88.6 2.7 %collective-permute-done.26.refs_0_ = bf16[512,1024]{1,0:T(8,128)(2,1)S(1)} collective-permute-done((bf16[512,1024]{1,0:T(8,128)(2,1)S(1)}, bf16[512,1024]{1,0:T(8,128)(2,1)S(1)}, u32[]{:S(2)}, u32[]{:S(2)}) %collective-permute-start.26) | collective-permute-done | bytes 1048608 | tf_op jit(solution)/shard_map/ppermute | solution.py:743
  92.7 2.9 %collective-permute-done.22.refs_1_ = bf16[128,1024]{1,0:T(8,128)(2,1)S(1)} collective-permute-done((bf16[128,1024]{1,0:T(8,128)(2,1)S(1)}, bf16[128,1024]{1,0:T(8,128)(2,1)S(1)}, u32[]{:S(2)}, u32[]{:S(2)}) %collective-permute-start.22) | collective-permute-done | bytes 262176 | tf_op jit(solution)/shard_map/ppermute | solution.py:736
  96.8 2.8 %collective-permute-start.51 = (bf16[256,1024]{1,0:T(8,128)(2,1)S(1)}, bf16[256,1024]{1,0:T(8,128)(2,1)S(1)}, u32[]{:S(2)}, u32[]{:S(2)}) collective-permute-start(bf16[256,1024]{1,0:T(8,128)(2,1)S(1)} %get-tuple-element.268), channel_id=1, source_target_pairs={{0,16},{4,20},{8,24},{12,28},{16,0},{20,4},{24,8},{28,12},{1,17},{... | collective-permute-start | bytes 1572872 | tf_op jit(solution)/shard_map/ppermute | solution.py:743
  103.1 1.9 shard_map.351
  107.9 7.4 %collective-permute-done.35.refs_3_ = f32[8,256]{1,0:T(8,128)S(1)} collective-permute-done((f32[8,256]{1,0:T(8,128)S(1)}, f32[8,256]{1,0:T(8,128)S(1)}, u32[]{:S(2)}, u32[]{:S(2)}) %collective-permute-start.35) | collective-permute-done | bytes 8224 | tf_op jit(solution)/shard_map/ppermute | solution.py:743
  117.1 6.3 %collective-permute-done.51.refs_1_ = bf16[256,1024]{1,0:T(8,128)(2,1)S(1)} collective-permute-done((bf16[256,1024]{1,0:T(8,128)(2,1)S(1)}, bf16[256,1024]{1,0:T(8,128)(2,1)S(1)}, u32[]{:S(2)}, u32[]{:S(2)}) %collective-permute-start.51) | collective-permute-done | bytes 524320 | tf_op jit(solution)/shard_map/ppermute | solution.py:743
  127.4 2.7 %collective-permute-done.37.refs_3_ = f32[8,256]{1,0:T(8,128)S(1)} collective-permute-done((f32[8,256]{1,0:T(8,128)S(1)}, f32[8,256]{1,0:T(8,128)S(1)}, u32[]{:S(2)}, u32[]{:S(2)}) %collective-permute-start.37) | collective-permute-done | bytes 8224 | tf_op jit(solution)/shard_map/ppermute | solution.py:743
  132.4 1.8 collective-permute-done.33.refs_1_
  134.2 2.9 %collective-permute-start.38 = (bf16[256,256]{1,0:T(8,128)(2,1)S(1)}, bf16[256,256]{1,0:T(8,128)(2,1)S(1)}, u32[]{:S(2)}, u32[]{:S(2)}) collective-permute-start(bf16[256,256]{1,0:T(8,128)(2,1)S(1)} %get-tuple-element.234), channel_id=1, source_target_pairs={{0,16},{4,20},{8,24},{12,28},{16,0},{20,4},{24,8},{28,12},{1,17},{... | collective-permute-start | bytes 393224 | tf_op jit(solution)/shard_map/ppermute | solution.py:743
  138.7 2.9 %collective-permute-start.39 = (f32[8,256]{1,0:T(8,128)S(1)}, f32[8,256]{1,0:T(8,128)S(1)}, u32[]{:S(2)}, u32[]{:S(2)}) collective-permute-start(f32[8,256]{1,0:T(8,128)S(1)} %get-tuple-element.235.refs_2_), channel_id=1, source_target_pairs={{0,16},{4,20},{8,24},{12,28},{16,0},{20,4},{24,8},{28,12},{1,17},{... | collective-permute-start | bytes 24584 | tf_op jit(solution)/shard_map/ppermute | solution.py:743
  142.6 10.5 %collective-permute-done.39.refs_3_ = f32[8,256]{1,0:T(8,128)S(1)} collective-permute-done((f32[8,256]{1,0:T(8,128)S(1)}, f32[8,256]{1,0:T(8,128)S(1)}, u32[]{:S(2)}, u32[]{:S(2)}) %collective-permute-start.39) | collective-permute-done | bytes 8224 | tf_op jit(solution)/shard_map/ppermute | solution.py:743
  161.2 10.0 %collective-permute-done.44.refs_1_ = bf16[256,512]{1,0:T(8,128)(2,1)S(1)} collective-permute-done((bf16[256,512]{1,0:T(8,128)(2,1)S(1)}, bf16[256,512]{1,0:T(8,128)(2,1)S(1)}, u32[]{:S(2)}, u32[]{:S(2)}) %collective-permute-start.44) | collective-permute-done | bytes 262176 | tf_op jit(solution)/shard_map/ppermute | solution.py:743
  171.3 3.4 %collective-permute-start.45 = (bf16[128,512]{1,0:T(8,128)(2,1)S(1)}, bf16[128,512]{1,0:T(8,128)(2,1)S(1)}, u32[]{:S(2)}, u32[]{:S(2)}) collective-permute-start(bf16[128,512]{1,0:T(8,128)(2,1)S(1)} %get-tuple-element.254), channel_id=1, source_target_pairs={{0,16},{4,20},{8,24},{12,28},{16,0},{20,4},{24,8},{28,12},{1,17},{... | collective-permute-start | bytes 393224 | tf_op jit(solution)/shard_map/ppermute | solution.py:743
  175.5 11.7 %collective-permute-done.45.refs_1_ = bf16[128,512]{1,0:T(8,128)(2,1)S(1)} collective-permute-done((bf16[128,512]{1,0:T(8,128)(2,1)S(1)}, bf16[128,512]{1,0:T(8,128)(2,1)S(1)}, u32[]{:S(2)}, u32[]{:S(2)}) %collective-permute-start.45) | collective-permute-done | bytes 131104 | tf_op jit(solution)/shard_map/ppermute | solution.py:743
  188.8 3.1 %collective-permute-done.48.refs_1_ = bf16[128,1024]{1,0:T(8,128)(2,1)S(1)} collective-permute-done((bf16[128,1024]{1,0:T(8,128)(2,1)S(1)}, bf16[128,1024]{1,0:T(8,128)(2,1)S(1)}, u32[]{:S(2)}, u32[]{:S(2)}) %collective-permute-start.48) | collective-permute-done | bytes 262176 | tf_op jit(solution)/shard_map/ppermute | solution.py:743
  (175 shorter events, 65.3 us)
Async XLA Ops:
  11.3 9.8 %collective-permute-start.2 = (bf16[128,1024]{1,0:T(8,128)(2,1)S(1)}, bf16[128,1024]{1,0:T(8,128)(2,1)S(1)}, u32[]{:S(2)}, u32[]{:S(2)}) collective-permute-start(bf16[128,1024]{1,0:T(8,128)(2,1)S(1)} %copy-done.14), channel_id=1, source_target_pairs={{0,2},{1,3},{2,0},{3,1},{4,6},{5,7},{6,4},{7,5},{8,10},{9,11},{10,... | collective-permute-start | bytes 786440 | tf_op jit(solution)/shard_map/ppermute | solution.py:736
  13.9 8.5 %collective-permute-start = (bf16[128,1024]{1,0:T(8,128)(2,1)S(1)}, bf16[128,1024]{1,0:T(8,128)(2,1)S(1)}, u32[]{:S(2)}, u32[]{:S(2)}) collective-permute-start(bf16[128,1024]{1,0:T(8,128)(2,1)S(1)} %get-tuple-element.145), channel_id=1, source_target_pairs={{0,1},{1,0},{2,3},{3,2},{4,5},{5,4},{6,7},{7,6},{8,9},{9,8},{10,11... | collective-permute-start | bytes 786440 | tf_op jit(solution)/shard_map/ppermute | solution.py:733
  14.2 12.5 %collective-permute-start.7 = (bf16[128,1024]{1,0:T(8,128)(2,1)S(1)}, bf16[128,1024]{1,0:T(8,128)(2,1)S(1)}, u32[]{:S(2)}, u32[]{:S(2)}) collective-permute-start(bf16[128,1024]{1,0:T(8,128)(2,1)S(1)} %get-tuple-element.155), channel_id=1, source_target_pairs={{0,2},{1,3},{2,0},{3,1},{4,6},{5,7},{6,4},{7,5},{8,10},{9,11},{10,... | collective-permute-start | bytes 786440 | tf_op jit(solution)/shard_map/ppermute | solution.py:736
  21.2 5.9 %collective-permute-start.4 = (bf16[128,1024]{1,0:T(8,128)(2,1)S(1)}, bf16[128,1024]{1,0:T(8,128)(2,1)S(1)}, u32[]{:S(2)}, u32[]{:S(2)}) collective-permute-start(bf16[128,1024]{1,0:T(8,128)(2,1)S(1)} %get-tuple-element.150.refs_0_.refs_4_.refs_2_.refs_3_), channel_id=1, source_target_pairs={{0,1},{1,0},{2,3},{3,2},{4,5},{5,4},{6,7},{7,6},{8,9},{9,8},{10,11... | collective-permute-start | bytes 786440 | tf_op jit(solution)/shard_map/ppermute | solution.py:733
  21.2 6.6 %collective-permute-start.3 = (bf16[128,1024]{1,0:T(8,128)(2,1)S(1)}, bf16[128,1024]{1,0:T(8,128)(2,1)S(1)}, u32[]{:S(2)}, u32[]{:S(2)}) collective-permute-start(bf16[128,1024]{1,0:T(8,128)(2,1)S(1)} %get-tuple-element.149.refs_0_.refs_4_.refs_1_), channel_id=1, source_target_pairs={{0,1},{1,0},{2,3},{3,2},{4,5},{5,4},{6,7},{7,6},{8,9},{9,8},{10,11... | collective-permute-start | bytes 786440 | tf_op jit(solution)/shard_map/ppermute | solution.py:733
  22.5 9.6 %collective-permute-start.1 = (bf16[128,1024]{1,0:T(8,128)(2,1)S(1)}, bf16[128,1024]{1,0:T(8,128)(2,1)S(1)}, u32[]{:S(2)}, u32[]{:S(2)}) collective-permute-start(bf16[128,1024]{1,0:T(8,128)(2,1)S(1)} %get-tuple-element.147), channel_id=1, source_target_pairs={{0,2},{1,3},{2,0},{3,1},{4,6},{5,7},{6,4},{7,5},{8,10},{9,11},{10,... | collective-permute-start | bytes 786440 | tf_op jit(solution)/shard_map/ppermute | solution.py:736
  39.7 9.2 %collective-permute-start.10 = (bf16[128,1024]{1,0:T(8,128)(2,1)S(1)}, bf16[128,1024]{1,0:T(8,128)(2,1)S(1)}, u32[]{:S(2)}, u32[]{:S(2)}) collective-permute-start(bf16[128,1024]{1,0:T(8,128)(2,1)S(1)} %get-tuple-element.161), channel_id=1, source_target_pairs={{0,2},{1,3},{2,0},{3,1},{4,6},{5,7},{6,4},{7,5},{8,10},{9,11},{10,... | collective-permute-start | bytes 786440 | tf_op jit(solution)/shard_map/ppermute | solution.py:736
  41.6 12.1 %collective-permute-start.13 = (bf16[128,1024]{1,0:T(8,128)(2,1)S(1)}, bf16[128,1024]{1,0:T(8,128)(2,1)S(1)}, u32[]{:S(2)}, u32[]{:S(2)}) collective-permute-start(bf16[128,1024]{1,0:T(8,128)(2,1)S(1)} %get-tuple-element.169), channel_id=1, source_target_pairs={{0,2},{1,3},{2,0},{3,1},{4,6},{5,7},{6,4},{7,5},{8,10},{9,11},{10,... | collective-permute-start | bytes 786440 | tf_op jit(solution)/shard_map/ppermute | solution.py:736
  58.6 9.2 %collective-permute-start.19 = (bf16[128,1024]{1,0:T(8,128)(2,1)S(1)}, bf16[128,1024]{1,0:T(8,128)(2,1)S(1)}, u32[]{:S(2)}, u32[]{:S(2)}) collective-permute-start(bf16[128,1024]{1,0:T(8,128)(2,1)S(1)} %get-tuple-element.183), channel_id=1, source_target_pairs={{0,2},{1,3},{2,0},{3,1},{4,6},{5,7},{6,4},{7,5},{8,10},{9,11},{10,... | collective-permute-start | bytes 786440 | tf_op jit(solution)/shard_map/ppermute | solution.py:736
  60.5 12.5 %collective-permute-start.16 = (bf16[128,1024]{1,0:T(8,128)(2,1)S(1)}, bf16[128,1024]{1,0:T(8,128)(2,1)S(1)}, u32[]{:S(2)}, u32[]{:S(2)}) collective-permute-start(bf16[128,1024]{1,0:T(8,128)(2,1)S(1)} %get-tuple-element.176), channel_id=1, source_target_pairs={{0,2},{1,3},{2,0},{3,1},{4,6},{5,7},{6,4},{7,5},{8,10},{9,11},{10,... | collective-permute-start | bytes 786440 | tf_op jit(solution)/shard_map/ppermute | solution.py:736
  62.7 25.0 %collective-permute-start.25 = (bf16[512,1024]{1,0:T(8,128)(2,1)S(1)}, bf16[512,1024]{1,0:T(8,128)(2,1)S(1)}, u32[]{:S(2)}, u32[]{:S(2)}) collective-permute-start(bf16[512,1024]{1,0:T(8,128)(2,1)S(1)} %shard_map.335.refs_5_), channel_id=1, source_target_pairs={{0,8},{4,12},{8,0},{12,4},{16,24},{20,28},{24,16},{28,20},{1,9},{5... | collective-permute-start | bytes 3145736 | tf_op jit(solution)/shard_map/ppermute | solution.py:743
  65.1 26.2 %collective-permute-start.26 = (bf16[512,1024]{1,0:T(8,128)(2,1)S(1)}, bf16[512,1024]{1,0:T(8,128)(2,1)S(1)}, u32[]{:S(2)}, u32[]{:S(2)}) collective-permute-start(bf16[512,1024]{1,0:T(8,128)(2,1)S(1)} %shard_map.336.refs_6_), channel_id=1, source_target_pairs={{0,4},{4,0},{8,12},{12,8},{16,20},{20,16},{24,28},{28,24},{1,5},{5... | collective-permute-start | bytes 3145736 | tf_op jit(solution)/shard_map/ppermute | solution.py:743
  81.4 10.9 %collective-permute-start.24 = (bf16[128,1024]{1,0:T(8,128)(2,1)S(1)}, bf16[128,1024]{1,0:T(8,128)(2,1)S(1)}, u32[]{:S(2)}, u32[]{:S(2)}) collective-permute-start(bf16[128,1024]{1,0:T(8,128)(2,1)S(1)} %get-tuple-element.201), channel_id=1, source_target_pairs={{0,2},{1,3},{2,0},{3,1},{4,6},{5,7},{6,4},{7,5},{8,10},{9,11},{10,... | collective-permute-start | bytes 786440 | tf_op jit(solution)/shard_map/ppermute | solution.py:736
  83.3 12.4 %collective-permute-start.22 = (bf16[128,1024]{1,0:T(8,128)(2,1)S(1)}, bf16[128,1024]{1,0:T(8,128)(2,1)S(1)}, u32[]{:S(2)}, u32[]{:S(2)}) collective-permute-start(bf16[128,1024]{1,0:T(8,128)(2,1)S(1)} %get-tuple-element.196), channel_id=1, source_target_pairs={{0,2},{1,3},{2,0},{3,1},{4,6},{5,7},{6,4},{7,5},{8,10},{9,11},{10,... | collective-permute-start | bytes 786440 | tf_op jit(solution)/shard_map/ppermute | solution.py:736
  85.0 53.6 %collective-permute-start.46 = (bf16[512,1024]{1,0:T(8,128)(2,1)S(1)}, bf16[512,1024]{1,0:T(8,128)(2,1)S(1)}, u32[]{:S(2)}, u32[]{:S(2)}) collective-permute-start(bf16[512,1024]{1,0:T(8,128)(2,1)S(1)} %shard_map.343.refs_5_), channel_id=1, source_target_pairs={{0,4},{4,0},{8,12},{12,8},{16,20},{20,16},{24,28},{28,24},{1,5},{5... | collective-permute-start | bytes 3145736 | tf_op jit(solution)/shard_map/ppermute | solution.py:743
  96.2 6.3 %collective-permute-start.31 = (bf16[128,1024]{1,0:T(8,128)(2,1)S(1)}, bf16[128,1024]{1,0:T(8,128)(2,1)S(1)}, u32[]{:S(2)}, u32[]{:S(2)}) collective-permute-start(bf16[128,1024]{1,0:T(8,128)(2,1)S(1)} %get-tuple-element.210.refs_3_.refs_8_.refs_4_), channel_id=1, source_target_pairs={{0,1},{1,0},{2,3},{3,2},{4,5},{5,4},{6,7},{7,6},{8,9},{9,8},{10,11... | collective-permute-start | bytes 786440 | tf_op jit(solution)/shard_map/ppermute | solution.py:733
  96.2 6.3 %collective-permute-start.30 = (bf16[128,1024]{1,0:T(8,128)(2,1)S(1)}, bf16[128,1024]{1,0:T(8,128)(2,1)S(1)}, u32[]{:S(2)}, u32[]{:S(2)}) collective-permute-start(bf16[128,1024]{1,0:T(8,128)(2,1)S(1)} %get-tuple-element.222.refs_6_.refs_1_.refs_2_), channel_id=1, source_target_pairs={{0,1},{1,0},{2,3},{3,2},{4,5},{5,4},{6,7},{7,6},{8,9},{9,8},{10,11... | collective-permute-start | bytes 786440 | tf_op jit(solution)/shard_map/ppermute | solution.py:733
  96.8 26.7 %collective-permute-start.51 = (bf16[256,1024]{1,0:T(8,128)(2,1)S(1)}, bf16[256,1024]{1,0:T(8,128)(2,1)S(1)}, u32[]{:S(2)}, u32[]{:S(2)}) collective-permute-start(bf16[256,1024]{1,0:T(8,128)(2,1)S(1)} %get-tuple-element.268), channel_id=1, source_target_pairs={{0,16},{4,20},{8,24},{12,28},{16,0},{20,4},{24,8},{28,12},{1,17},{... | collective-permute-start | bytes 1572872 | tf_op jit(solution)/shard_map/ppermute | solution.py:743
  99.6 25.4 %collective-permute-start.49 = (bf16[256,1024]{1,0:T(8,128)(2,1)S(1)}, bf16[256,1024]{1,0:T(8,128)(2,1)S(1)}, u32[]{:S(2)}, u32[]{:S(2)}) collective-permute-start(bf16[256,1024]{1,0:T(8,128)(2,1)S(1)} %get-tuple-element.265), channel_id=1, source_target_pairs={{0,8},{4,12},{8,0},{12,4},{16,24},{20,28},{24,16},{28,20},{1,9},{5... | collective-permute-start | bytes 1572872 | tf_op jit(solution)/shard_map/ppermute | solution.py:743
  104.9 12.1 %collective-permute-start.34 = (bf16[256,256]{1,0:T(8,128)(2,1)S(1)}, bf16[256,256]{1,0:T(8,128)(2,1)S(1)}, u32[]{:S(2)}, u32[]{:S(2)}) collective-permute-start(bf16[256,256]{1,0:T(8,128)(2,1)S(1)} %get-tuple-element.228), channel_id=1, source_target_pairs={{0,4},{4,0},{8,12},{12,8},{16,20},{20,16},{24,28},{28,24},{1,5},{5... | collective-permute-start | bytes 393224 | tf_op jit(solution)/shard_map/ppermute | solution.py:743
  106.6 8.7 %collective-permute-start.35 = (f32[8,256]{1,0:T(8,128)S(1)}, f32[8,256]{1,0:T(8,128)S(1)}, u32[]{:S(2)}, u32[]{:S(2)}) collective-permute-start(f32[8,256]{1,0:T(8,128)S(1)} %get-tuple-element.229.refs_2_), channel_id=1, source_target_pairs={{0,4},{4,0},{8,12},{12,8},{16,20},{20,16},{24,28},{28,24},{1,5},{5... | collective-permute-start | bytes 24584 | tf_op jit(solution)/shard_map/ppermute | solution.py:743
  115.3 40.2 %collective-permute-start.43 = (bf16[512,512]{1,0:T(8,128)(2,1)S(1)}, bf16[512,512]{1,0:T(8,128)(2,1)S(1)}, u32[]{:S(2)}, u32[]{:S(2)}) collective-permute-start(bf16[512,512]{1,0:T(8,128)(2,1)S(1)} %shard_map.360), channel_id=1, source_target_pairs={{0,4},{4,0},{8,12},{12,8},{16,20},{20,16},{24,28},{28,24},{1,5},{5... | collective-permute-start | bytes 1572872 | tf_op jit(solution)/shard_map/ppermute | solution.py:743
  117.0 8.9 %collective-permute-start.32 = (bf16[192,256]{1,0:T(8,128)(2,1)S(1)}, bf16[192,256]{1,0:T(8,128)(2,1)S(1)}, u32[]{:S(2)}, u32[]{:S(2)}) collective-permute-start(bf16[192,256]{1,0:T(8,128)(2,1)S(1)} %get-tuple-element.224), channel_id=1, source_target_pairs={{0,1},{1,0},{2,3},{3,2},{4,5},{5,4},{6,7},{7,6},{8,9},{9,8},{10,11... | collective-permute-start | bytes 294920 | tf_op jit(solution)/shard_map/ppermute | solution.py:733
  123.5 14.3 %collective-permute-start.29 = (bf16[128,1024]{1,0:T(8,128)(2,1)S(1)}, bf16[128,1024]{1,0:T(8,128)(2,1)S(1)}, u32[]{:S(2)}, u32[]{:S(2)}) collective-permute-start(bf16[128,1024]{1,0:T(8,128)(2,1)S(1)} %get-tuple-element.216), channel_id=1, source_target_pairs={{0,2},{1,3},{2,0},{3,1},{4,6},{5,7},{6,4},{7,5},{8,10},{9,11},{10,... | collective-permute-start | bytes 786440 | tf_op jit(solution)/shard_map/ppermute | solution.py:736
  130.8 27.1 %collective-permute-start.52 = (bf16[128,1024]{1,0:T(8,128)(2,1)S(1)}, bf16[128,1024]{1,0:T(8,128)(2,1)S(1)}, u32[]{:S(2)}, u32[]{:S(2)}) collective-permute-start(bf16[128,1024]{1,0:T(8,128)(2,1)S(1)} %get-tuple-element.270), channel_id=1, source_target_pairs={{0,4},{4,0},{8,12},{12,8},{16,20},{20,16},{24,28},{28,24},{1,5},{5... | collective-permute-start | bytes 786440 | tf_op jit(solution)/shard_map/ppermute | solution.py:743
  134.2 19.3 %collective-permute-start.38 = (bf16[256,256]{1,0:T(8,128)(2,1)S(1)}, bf16[256,256]{1,0:T(8,128)(2,1)S(1)}, u32[]{:S(2)}, u32[]{:S(2)}) collective-permute-start(bf16[256,256]{1,0:T(8,128)(2,1)S(1)} %get-tuple-element.234), channel_id=1, source_target_pairs={{0,16},{4,20},{8,24},{12,28},{16,0},{20,4},{24,8},{28,12},{1,17},{... | collective-permute-start | bytes 393224 | tf_op jit(solution)/shard_map/ppermute | solution.py:743
  137.8 21.5 %collective-permute-start.50 = (bf16[128,1024]{1,0:T(8,128)(2,1)S(1)}, bf16[128,1024]{1,0:T(8,128)(2,1)S(1)}, u32[]{:S(2)}, u32[]{:S(2)}) collective-permute-start(bf16[128,1024]{1,0:T(8,128)(2,1)S(1)} %get-tuple-element.267), channel_id=1, source_target_pairs={{0,16},{4,20},{8,24},{12,28},{16,0},{20,4},{24,8},{28,12},{1,17},{... | collective-permute-start | bytes 786440 | tf_op jit(solution)/shard_map/ppermute | solution.py:743
  138.7 14.4 %collective-permute-start.39 = (f32[8,256]{1,0:T(8,128)S(1)}, f32[8,256]{1,0:T(8,128)S(1)}, u32[]{:S(2)}, u32[]{:S(2)}) collective-permute-start(f32[8,256]{1,0:T(8,128)S(1)} %get-tuple-element.235.refs_2_), channel_id=1, source_target_pairs={{0,16},{4,20},{8,24},{12,28},{16,0},{20,4},{24,8},{28,12},{1,17},{... | collective-permute-start | bytes 24584 | tf_op jit(solution)/shard_map/ppermute | solution.py:743
  153.1 22.2 %collective-permute-start.47 = (bf16[256,1024]{1,0:T(8,128)(2,1)S(1)}, bf16[256,1024]{1,0:T(8,128)(2,1)S(1)}, u32[]{:S(2)}, u32[]{:S(2)}) collective-permute-start(bf16[256,1024]{1,0:T(8,128)(2,1)S(1)} %get-tuple-element.260), channel_id=1, source_target_pairs={{0,8},{4,12},{8,0},{12,4},{16,24},{20,28},{24,16},{28,20},{1,9},{5... | collective-permute-start | bytes 1572872 | tf_op jit(solution)/shard_map/ppermute | solution.py:743
  156.2 15.0 %collective-permute-start.44 = (bf16[256,512]{1,0:T(8,128)(2,1)S(1)}, bf16[256,512]{1,0:T(8,128)(2,1)S(1)}, u32[]{:S(2)}, u32[]{:S(2)}) collective-permute-start(bf16[256,512]{1,0:T(8,128)(2,1)S(1)} %get-tuple-element.252), channel_id=1, source_target_pairs={{0,8},{4,12},{8,0},{12,4},{16,24},{20,28},{24,16},{28,20},{1,9},{5... | collective-permute-start | bytes 786440 | tf_op jit(solution)/shard_map/ppermute | solution.py:743
  171.3 16.0 %collective-permute-start.45 = (bf16[128,512]{1,0:T(8,128)(2,1)S(1)}, bf16[128,512]{1,0:T(8,128)(2,1)S(1)}, u32[]{:S(2)}, u32[]{:S(2)}) collective-permute-start(bf16[128,512]{1,0:T(8,128)(2,1)S(1)} %get-tuple-element.254), channel_id=1, source_target_pairs={{0,16},{4,20},{8,24},{12,28},{16,0},{20,4},{24,8},{28,12},{1,17},{... | collective-permute-start | bytes 393224 | tf_op jit(solution)/shard_map/ppermute | solution.py:743
  175.5 16.4 %collective-permute-start.48 = (bf16[128,1024]{1,0:T(8,128)(2,1)S(1)}, bf16[128,1024]{1,0:T(8,128)(2,1)S(1)}, u32[]{:S(2)}, u32[]{:S(2)}) collective-permute-start(bf16[128,1024]{1,0:T(8,128)(2,1)S(1)} %get-tuple-element.262), channel_id=1, source_target_pairs={{0,16},{4,20},{8,24},{12,28},{16,0},{20,4},{24,8},{28,12},{1,17},{... | collective-permute-start | bytes 786440 | tf_op jit(solution)/shard_map/ppermute | solution.py:743
  (42 other events, 204.0 us)
where the time goes:
time: 193 us
  waiting for transfers between devices  89 us (46%)
  starting transfers between devices  50.4 us (26%)
  Pallas kernels  43.6 us (23%)
  local copies, waits for them, and re-layouts  7.71 us (4%)
  between operations  1.97 us (1%)
    ppermute x18, waiting for transfers between devices, swap_sample(): return lax.ppermute(value, 'dp', pairs(mesh_dp, bit))  55.6 us
    pallas_call x57, Pallas kernels, call(): pl.pallas_call(run, out_shape=[jax.ShapeDtypeStruct(shape, kind) for shap...  43.6 us
    ppermute x12, waiting for transfers between devices, swap_chip(): return lax.ppermute(value, 'mp', pairs(mesh_mp, 2))  31.6 us
    ppermute x18, starting transfers between devices, swap_sample(): return lax.ppermute(value, 'dp', pairs(mesh_dp, bit))  28 us
    ppermute x12, starting transfers between devices, swap_chip(): return lax.ppermute(value, 'mp', pairs(mesh_mp, 2))  17.5 us
    unnamed x42, local copies, waits for them, and re-layouts  6.67 us
    ppermute x23, starting transfers between devices, swap_core(): return lax.ppermute(value, 'mp', pairs(mesh_mp, 1))  4.94 us
  transfers between devices with their start and end apart: 53, of which 22 were waited for; matrix products, arithmetic and copies ran while one was open for 1% of the time, Pallas kernels for 19%

commit v1 on v0

--- a/solution.py
+++ b/solution.py
@@ -1,4 +1,5 @@
 import functools
+import types
 
 import jax
 import jax.numpy as jnp
@@ -19,6 +20,28 @@
 ANY = pl.BlockSpec(memory_space=pl.ANY)
 HBM = pl.BlockSpec(memory_space=pltpu.HBM)
 MIB = 1024 * 1024
+FIRST_LIMIT = 60
+PIECES = 2
+AXES = ((0, 1, 2), (1, 2, 0), (0, 1, 2), (0, 1, 2), (1, 0, 2))
+ORDER = (
+    "mix_a", "mix_b", "first_a", "first_b", "base", "norm_a", "proj", "norm_b", "attend_a", "second_a", "cot",
+    "attend_b", "hidden_a", "second_b", "two_a", "mlp_a", "hidden_b", "two_b", "third_a", "mlp_b", "down_1",
+    "up_1", "third_b", "mid_a", "back_a", "mid_b", "back_b", "attn_1", "back_c", "fourth_a", "down_2",
+    "weights", "fourth_b", "up_2", "in_a", "in_b", "mass_1", "down_3", "mix_1", "field_1", "attn_2", "mass_2",
+    "up_3", "mass_3", "rows_1", "down_4", "up_4", "rows_2", "mix_2", "attn_3", "finish", "tables_1", "mix_3",
+    "attn_4", "rows_3", "field_2", "tables_2", "mix_4",
+)
+COSTS = {
+    "two_a": 1,
+    "two_b": 0.3,
+    "mlp_b": 12,
+    "mid_a": 1,
+    "up_2": 1,
+    "in_a": 1,
+    "down_3": 2,
+    "up_3": 1,
+    "tables_1": 1,
+}
 
 
 def dot(left, right, left_dim=1, right_dim=0, precision=None):
@@ -31,16 +54,49 @@
     )
 
 
-def call(kernel, outs, args, fetch=(), smem=(), after=(), limit=24, cost=1, scratch=()):
+class Rows:
+    def __init__(self, refs):
+        self.refs = refs
+        self.shape = (sum(ref.shape[0] for ref in refs),) + refs[0].shape[1:]
+
+    def __getitem__(self, at):
+        return jnp.concatenate([ref[at] for ref in self.refs], axis=0)
+
+    def __setitem__(self, at, value):
+        step = self.refs[0].shape[0]
+        for i, ref in enumerate(self.refs):
+            ref[...] = value[i * step : (i + 1) * step]
+
+
+def gather_refs(refs, counts):
+    refs, grouped = list(refs), []
+    for count in counts:
+        grouped.append(refs.pop(0) if count is None else Rows([refs.pop(0) for _ in range(count)]))
+    return grouped
+
+
+def flat(items):
+    out, counts = [], []
+    for item in items:
+        pieces = isinstance(item, list)
+        out.extend(item if pieces else [item])
+        counts.append(len(item) if pieces else None)
+    return out, counts
+
+
+def launch(kernel, outs, args, fetch=(), smem=(), after=(), limit=24, scratch=(), cost=0.1, name=None):
     fetch = [item if isinstance(item, tuple) else (item, item.shape, None) for item in fetch]
+    args, arg_counts = flat(args)
+    outs, out_counts = flat(outs)
     count = len(smem)
 
     def run(*refs):
         at = count + len(fetch)
         sources, rest = refs[count:at], refs[at:]
-        inputs, rest = rest[: len(args)], rest[len(args) + len(after) :]
+        inputs, rest = gather_refs(rest[: len(args)], arg_counts), rest[len(args) + len(after) :]
+        results, rest = gather_refs(rest[: len(outs)], out_counts), rest[len(outs) :]
         if not fetch:
-            kernel(*refs[:count], *inputs, *rest)
+            kernel(*refs[:count], *inputs, *results, *rest)
             return
         *rest, marks = rest
         rest, places = rest[: len(rest) - len(fetch)], rest[len(rest) - len(fetch) :]
@@ -52,21 +108,32 @@
             copy.start()
         for copy in copies:
             copy.wait()
-        kernel(*refs[:count], *places, *inputs, *rest)
+        kernel(*refs[:count], *places, *inputs, *results, *rest)
 
     places = [pltpu.VMEM(shape, array.dtype) for array, shape, _ in fetch]
     marks = [pltpu.SemaphoreType.DMA((len(fetch),))] if fetch else []
-    return pl.pallas_call(
+    results = pl.pallas_call(
         run,
         out_shape=[jax.ShapeDtypeStruct(shape, kind) for shape, kind in outs],
         in_specs=[SMEM] * count + [HBM] * len(fetch) + [VMEM] * len(args) + [ANY] * len(after),
         out_specs=[VMEM] * len(outs),
         scratch_shapes=list(scratch) + places + marks,
+        name=name,
         compiler_params=pltpu.CompilerParams(vmem_limit_bytes=limit * MIB),
         cost_estimate=pl.CostEstimate(
             flops=int(cost * 1e9), bytes_accessed=0, transcendentals=0
         ),
     )(*smem, *(array for array, _, _ in fetch), *args, *after)
+    results, grouped = list(results), []
+    for pieces in out_counts:
+        grouped.append(results.pop(0) if pieces is None else [results.pop(0) for _ in range(pieces)])
+    return grouped
+
+
+def marked(kernel, *refs):
+    *rest, mark_ref = refs
+    mark_ref[...] = jnp.zeros_like(mark_ref)
+    kernel(*rest)
 
 
 def my_bit(bit):
@@ -102,6 +169,27 @@
     if bottom:
         parts.append(jnp.zeros((bottom, top.shape[1]), top.dtype))
     return jnp.concatenate(parts, axis=0)
+
+
+def pixel_major(channels, pixels):
+    variables = channels // pixels
+    row = iota((channels, channels), 0)
+    major = jnp.zeros((channels, channels), jnp.int32)
+    for p in range(pixels):
+        inside = (row >= p * variables) & (row < (p + 1) * variables)
+        major = jnp.where(inside, (row - p * variables) * pixels + p, major)
+    return exact(iota((channels, channels), 1) == major)
+
+
+def places(ids_ref, variables, pixels):
+    channels = variables * pixels
+    channel = iota((1, channels), 1)
+    place = jnp.zeros((1, channels), jnp.int32)
+    for v in range(variables):
+        pixel = channel - v * pixels
+        inside = (pixel >= 0) & (pixel < pixels)
+        place = jnp.where(inside, pixel * variables + ids_ref[v], place)
+    return place
 
 
 def mix_forward(
@@ -112,21 +200,15 @@
     patch_ref,
     variable_ref,
     w_ref,
-    w_out_ref,
     query_ref,
-    table_ref,
-    pick_ref,
+    mixed_ref,
     xt_ref,
     probs_ref,
     values_ref,
     keys_t_ref,
     score_ref,
     query_col_ref,
-    mixed_ref,
-    send_a_ref,
-    send_b_ref,
-    keep_a_ref,
-    keep_b_ref,
+    table_ref,
 ):
     channels = x_ref.shape[1]
     variables = channels // pixels
@@ -134,25 +216,12 @@
     width = w_ref.shape[2]
     heads = width // HEAD_DIM
     bottom = rows - channels - variables
-    row = iota((channels, channels), 0)
-    column = iota((channels, channels), 1)
-    major = jnp.zeros((channels, channels), jnp.int32)
-    for p in range(pixels):
-        inside = (row >= p * variables) & (row < (p + 1) * variables)
-        major = jnp.where(inside, (row - p * variables) * pixels + p, major)
     flat = patch_ref[...].reshape(channels, model_width)
-    table_ref[0:channels] = dot(exact(column == major), flat).astype(BF16)
+    table_ref[0:channels] = dot(pixel_major(channels, pixels), flat).astype(BF16)
     table_ref[channels : channels + variables] = variable_ref[...]
     if bottom:
         table_ref[channels + variables :] = jnp.zeros((bottom, model_width), BF16)
-    channel = iota((1, channels), 1)
-    place = jnp.zeros((1, channels), jnp.int32)
-    for v in range(variables):
-        pixel = channel - v * pixels
-        inside = (pixel >= 0) & (pixel < pixels)
-        place = jnp.where(inside, pixel * variables + ids_ref[v], place)
-    pick = (iota((channels, channels), 0) == place).astype(F32)
-    pick_ref[...] = pick.T.astype(BF16)
+    pick = (iota((channels, channels), 0) == places(ids_ref, variables, pixels)).astype(F32)
     core = my_core()
     starts = [core, 1 - core, core + 2, 3 - core]
     field = jnp.concatenate(
@@ -187,11 +256,28 @@
         mixing = spread(xt, pixels, low, bottom).astype(BF16)
         part = slice(head * HEAD_DIM, (head + 1) * HEAD_DIM)
         mixed_ref[part] = dot(values_t[part], mixing).astype(BF16)
+
+
+def mix_out(mixed_ref, w_out_ref, send_a_ref, send_b_ref, keep_a_ref, keep_b_ref):
+    quarter = keep_a_ref.shape[0]
     out = dot(mixed_ref[...], w_out_ref[...], 0, 0)
     keep_a_ref[...] = out[0:quarter]
     send_a_ref[...] = out[quarter : 2 * quarter].astype(BF16)
     keep_b_ref[...] = out[2 * quarter : 3 * quarter]
     send_b_ref[...] = out[3 * quarter :].astype(BF16)
+
+
+def pack_mass(mass, bias, packed_ref):
+    width = mass.shape[0]
+    high = bias.astype(BF16).astype(F32)
+    packed_ref[0:width] = mass.astype(BF16)
+    packed_ref[width:] = jnp.concatenate([high, bias - high], axis=0).astype(BF16)
+
+
+def add_mass(mass_ref, bias_ref, got_ref):
+    width = mass_ref.shape[0]
+    more = got_ref[width:].astype(F32)
+    return mass_ref[...] + got_ref[0:width].astype(F32), bias_ref[...] + more[0:8] + more[8:16]
 
 
 def mix_backward(
@@ -206,8 +292,8 @@
     a1_ref,
     b0_ref,
     b1_ref,
+    packed_ref,
     mass_ref,
-    mass_low_ref,
     bias_ref,
     field_send_ref,
     field_keep_ref,
@@ -250,8 +336,8 @@
         mixing = spread(xt, pixels, low, bottom).astype(BF16)
         part = slice(head * HEAD_DIM, (head + 1) * HEAD_DIM)
         mass_ref[part] = dot(grad_t[part], mixing, 1, 1)
-    mass_low_ref[...] = mass_ref[...].astype(BF16)
     bias_ref[...] = sums.T[0:8]
+    pack_mass(mass_ref[...], bias_ref[...], packed_ref)
     field = dot(pick_ref[...], field.astype(BF16))
     field_keep_ref[:, 0:quarter] = field[:, 0:quarter]
     field_keep_ref[:, quarter:] = field[:, 2 * quarter : 3 * quarter]
@@ -268,6 +354,12 @@
     centered = total - jnp.mean(total, axis=1, keepdims=True)
     inv_std = lax.rsqrt(jnp.mean(centered * centered, axis=1, keepdims=True) + EPS)
     low_ref[...] = (centered * inv_std * gain_ref[...] + bias_ref[...]).astype(BF16)
+
+
+def norm_relay(pass_ref, *refs):
+    *refs, out_ref = refs
+    out_ref[...] = pass_ref[...]
+    norm_forward(*refs)
 
 
 def norm_backward(with_sum, add_refs, *refs):
@@ -531,8 +623,7 @@
     rest_ref[quarter:] = jnp.where(row == 4 + samples + sample, bucket, filled)
 
 
-def write_mix(ref, step, which, inputs, rest_ref, dtype):
-    left, mixed_ref = inputs[0:4], inputs[4]
+def write_mix(ref, step, which, left, mixed_ref, rest_ref, dtype):
     width = left[0].shape[1]
     heads_width = mixed_ref.shape[0]
     for group in range(width // (2 * step)):
@@ -543,16 +634,16 @@
         ref[rows, heads_width:] = rest_ref[:, pl.ds(start, step)].T.astype(dtype)
 
 
-def mix_start(samples, lines, step, bit, bucket_ref, *refs):
+def mix_start(samples, lines, step, bit, bucket_ref, mixed_ref, *refs):
     *inputs, out_ref, rest = refs
-    mix_lines(samples, lines, bucket_ref, inputs[5:], rest)
-    write_mix(out_ref, step, 1 - my_bit(bit), inputs, rest, BF16)
-
-
-def mix_second(samples, lines, step, next_step, bit, next_bit, bucket_ref, *refs):
+    mix_lines(samples, lines, bucket_ref, inputs[4:], rest)
+    write_mix(out_ref, step, 1 - my_bit(bit), inputs[:4], mixed_ref, rest, BF16)
+
+
+def mix_second(samples, lines, step, next_step, bit, next_bit, bucket_ref, mixed_ref, *refs):
     got_ref, *inputs, keep_ref, send_ref, rest, total = refs
-    mix_lines(samples, lines, bucket_ref, inputs[5:], rest)
-    write_mix(total, step, my_bit(bit), inputs, rest, F32)
+    mix_lines(samples, lines, bucket_ref, inputs[4:], rest)
+    write_mix(total, step, my_bit(bit), inputs[:4], mixed_ref, rest, F32)
     total[...] = total[...] + got_ref[...].astype(F32)
     take_half(send_ref, total, next_step, 1 - my_bit(next_bit), BF16)
     take_half(keep_ref, total, next_step, my_bit(next_bit), F32)
@@ -576,32 +667,33 @@
     small_ref[...] = own.T[0:8, :final]
 
 
-def mass_add(mass_ref, got_ref, bias_ref, bias_got_ref, out_ref, low_ref, bias_out_ref):
-    total = mass_ref[...] + got_ref[...].astype(F32)
-    out_ref[...] = total
-    low_ref[...] = total.astype(BF16)
-    bias_out_ref[...] = bias_ref[...] + bias_got_ref[...]
+def mass_add(mass_ref, bias_ref, got_ref, packed_ref, mass_out_ref, bias_out_ref):
+    mass, bias = add_mass(mass_ref, bias_ref, got_ref)
+    mass_out_ref[...] = mass
+    bias_out_ref[...] = bias
+    pack_mass(mass, bias, packed_ref)
 
 
 def mix_finish(
-    mass_ref,
-    got_ref,
-    bias_ref,
-    bias_got_ref,
+    pixels,
     query_col_ref,
     keys_t_ref,
-    table_ref,
+    patch_ref,
+    variable_ref,
+    mass_ref,
+    bias_ref,
+    got_ref,
     w_ref,
     query_ref,
-    grad_ref,
     keep_ref,
     send_ref,
+    grad_ref,
     scratch,
 ):
     width, rows = mass_ref.shape
     heads = width // HEAD_DIM
-    mass = (mass_ref[...] + got_ref[...].astype(F32)).astype(BF16)
-    sums = bias_ref[...] + bias_got_ref[...]
+    mass, sums = add_mass(mass_ref, bias_ref, got_ref)
+    mass = mass.astype(BF16)
     bias = jnp.concatenate(
         [jnp.broadcast_to(sums[head : head + 1], (HEAD_DIM, rows)) for head in range(heads)], axis=0
     )
@@ -609,10 +701,16 @@
     total = jnp.sum(keys_t_ref[...] * bias, axis=1, keepdims=True)
     own = grad_ref.shape[1]
     start = lax.axis_index("dp") * own
-    model_width = table_ref.shape[1]
+    model_width = variable_ref.shape[1]
+    channels = patch_ref.shape[0] * pixels
     mine = exact(iota((own, model_width), 1) == iota((own, model_width), 0) + start)
     total_row = jnp.broadcast_to(total, (width, LANES)).T[0:1]
-    table_t = dot(mine, table_ref[...], 1, 1).astype(BF16)
+    flat = patch_ref[...].reshape(channels, model_width)
+    patch_t = dot(mine, flat, 1, 1).astype(BF16)
+    patch_t = dot(patch_t, pixel_major(channels, pixels), 1, 1)
+    variable_t = dot(mine, variable_ref[...], 1, 1)
+    bottom = rows - channels - variable_ref.shape[0]
+    table_t = jnp.concatenate([patch_t, variable_t, jnp.zeros((own, bottom), F32)], axis=1).astype(BF16)
     query_rows = jnp.broadcast_to(query_ref[...].astype(F32)[None], (16, model_width)).astype(BF16)
     grad_ref[0] = dot(mine, query_rows, 1, 1)[:, 0:1] * total_row
     grad_ref[1] = dot(table_t, key_mass, 1, 1)
@@ -643,6 +741,17 @@
     total = keep_ref[...] + got_ref[...].astype(F32)
     out_ref[...] = total
     low_ref[...] = total.astype(BF16)
+
+
+def take_rows(source_ref, out_ref):
+    out_ref[...] = source_ref[...]
+
+
+def take_weights(pixels, ids_ref, source_ref, out_ref, pick_ref):
+    out_ref[...] = source_ref[...]
+    channels = pick_ref.shape[0]
+    pick = iota((channels, channels), 0) == places(ids_ref, channels // pixels, pixels)
+    pick_ref[...] = pick.astype(F32).T.astype(BF16)
 
 
 def by_chip(own_ref, far_ref, first_ref, second_ref):
@@ -726,28 +835,44 @@
     heads = head_width // HEAD_DIM
     own_width = model_width // mesh_dp
     half = 2 * quarter
+    latest, now = [], []
+    v = types.SimpleNamespace()
+
+    def call(kernel, outs, args, final=False, **options):
+        if final:
+            outs = outs + [((8, LANES), F32)]
+            kernel = functools.partial(marked, kernel)
+        known = flat(args)[0] + list(options.get("fetch", ()))
+        after = [last for last in latest if all(last is not arg for arg in known)]
+        cost = COSTS.get(now[0], 0.1)
+        results = launch(kernel, outs, args, after=after, cost=cost, name=now[0], **options)
+        latest[:] = results[-1:] if final else flat(results)[0][:1]
+        return results[:-1] if final else results
+
     rows32 = ((quarter, model_width), F32)
     rows16 = ((quarter, model_width), BF16)
+    cut16 = [((quarter // PIECES, model_width), BF16)] * PIECES
 
     def swap_core(value):
+        if isinstance(value, list):
+            return [swap_core(piece) for piece in value]
         return lax.ppermute(value, "mp", pairs(mesh_mp, 1))
 
     def swap_chip(value):
         return lax.ppermute(value, "mp", pairs(mesh_mp, 2))
 
-    def add_core(keep, send):
-        kept, low = call(pair_sum, [rows32, rows16], [keep, swap_core(send)], cost=0.3)
-        return kept, swap_chip(low)
-
     def swap_sample(value, bit):
         return lax.ppermute(value, "dp", pairs(mesh_dp, bit))
 
+    def add_near(keep, near):
+        kept, low = call(pair_sum, [rows32, rows16], [keep, near])
+        return kept, swap_chip(low)
+
     all_bits = [1 << i for i in range(mesh_dp.bit_length() - 1)]
     wide = [bit for bit in all_bits if bit * own_width % LANES == 0]
 
-    def order_from(which):
-        first = all_bits.index(wide[which % len(wide)])
-        return all_bits[first:] + all_bits[:first]
+    def order_from(axes):
+        return [wide[i] for i in axes] + [bit for bit in all_bits if bit not in wide[:3]]
 
     def steps_of(order):
         left = list(all_bits)
@@ -757,28 +882,26 @@
             left.remove(bit)
         return steps
 
-    def start_sum(load, inputs, width, order, after=()):
+    def start_sum(load, inputs, width, order):
         step = steps_of(order)[0]
         (send,) = call(
             functools.partial(sum_start, load, step, order[0]),
             [((model_width // 2, width), BF16)],
             inputs,
-            after=after,
-        )
-        return send, swap_sample(send, order[0])
+        )
+        return swap_sample(send, order[0])
 
     def halves(width, scratch_rows):
         kept = scratch_rows // 2
         return [((kept, width), F32), ((kept, width), BF16)]
 
-    def second_sum(load, inputs, got, width, order, after=()):
+    def second_sum(load, inputs, got, width, order):
         steps = steps_of(order)
         rows = model_width // 2
         keep, send = call(
             functools.partial(sum_second, load, steps[0], steps[1], order[0], order[1]),
             halves(width, rows),
             [got] + inputs,
-            after=after,
             scratch=[pltpu.VMEM((rows, width), F32)],
         )
         return keep, swap_sample(send, order[1])
@@ -796,9 +919,8 @@
             got = swap_sample(send, order[i])
         return keep, got
 
-    cot_a0, cot_b0 = call(by_chip, [rows16] * 2, [cotangent, swap_chip(cotangent)], cost=0.3)
-    cot_a1 = swap_core(cot_a0)
-    cot_b1 = swap_core(cot_b0)
+    def norm_rows(terms, gain, bias):
+        return call(norm_forward, [rows32, cut16], terms + [gain, bias])
 
     w_mix = mix_weights.transpose(1, 0, 2)
     w_attn = attn_weights.transpose(1, 0, 2)
@@ -806,291 +928,440 @@
     gain_two, bias_two = second_gain[None], second_bias[None]
     table_rows = channels + variables
     padded = -(-(table_rows + 1) // LANES) * LANES
-    (
-        table,
-        pick,
-        field_t,
-        probs,
-        values,
-        keys_t,
-        score,
-        query_col,
-        mixed_t,
-        send_a,
-        send_b,
-        keep_a,
-        keep_b,
-    ) = call(
-        functools.partial(mix_forward, pixels, quarter),
-        [
-            ((padded, model_width), BF16),
-            ((channels, channels), BF16),
-            ((channels, length), BF16),
-            ((heads * variables, length), F32),
-            ((padded, head_width), BF16),
-            ((head_width, padded), F32),
-            ((padded, LANES), F32),
-            ((head_width, LANES), F32),
-            ((head_width, length), BF16),
-            rows16,
-            rows16,
-            rows32,
-            rows32,
-        ],
-        [variable_query],
-        fetch=[input_field, patch_table, variable_table, w_mix, mix_output],
-        smem=[variable_ids],
-    )
-    blocks = [
-        (pos_table, (quarter, model_width), lambda ref, k=k: ref.at[pl.ds((2 * k + my_core()) * quarter, quarter)])
-        for k in range(2)
-    ]
-    base_a, base_b = call(
-        base_rows, [rows32] * 2, [], fetch=blocks + [lead_table], smem=[lead_bucket], cost=0.3
-    )
-    kept_a, far_a = add_core(keep_a, send_a)
-    kept_b, far_b = add_core(keep_b, send_b)
-
-    def norm_rows(terms, gain, bias, after=()):
-        return call(norm_forward, [rows32, rows16], terms + [gain, bias], after=after, cost=0.5)
-
-    in_a, one_a0 = norm_rows([kept_a, far_a, base_a], gain_one, bias_one)
-    one_a1 = swap_core(one_a0)
+    lines = -(-(4 + 2 * mesh_dp) // LANES) * LANES
+    mix_width = head_width + quarter + lines
+    attn_width = 4 * head_width
+    final = own_width // mesh_mp
+    own_field = (channels, quarter)
     proj_kind = ((3, half, head_width), BF16)
-    (proj_a,) = call(project, [proj_kind], [one_a0, one_a1, w_attn])
-    (grad_hidden_a,) = call(hidden_back, [((half, hidden_width), F32)], [cot_a0, cot_a1, down_weight])
-    (grad_hidden_b,) = call(hidden_back, [((half, hidden_width), F32)], [cot_b0, cot_b1, down_weight])
-    in_b, one_b0 = norm_rows(
-        [kept_b, far_b, base_b], gain_one, bias_one, after=[grad_hidden_a, grad_hidden_b]
-    )
-    one_b1 = swap_core(one_b0)
-    attend_kinds = [((half, head_width), BF16), ((8, half), F32), rows32, rows16]
-    proj_b, attended_a, logs_a, keep_a, send_a = call(
-        attend_first,
-        [proj_kind] + attend_kinds,
-        [one_b0, one_b1, w_attn, proj_a, attn_output],
-    )
-    attended_b, logs_b, keep_b, send_b = call(
-        attend_second, attend_kinds, [proj_a, proj_b, attn_output]
-    )
-    kept_a, far_a = add_core(keep_a, send_a)
-    kept_b, far_b = add_core(keep_b, send_b)
-    mid_a, two_a0 = norm_rows([kept_a, far_a, in_a], gain_two, bias_two)
-    two_a1 = swap_core(two_a0)
-    mlp_kinds = [((half, hidden_width), BF16)] * 2 + [rows32, rows16]
-    hidden_a, pre_a, keep_a, send_a = call(mlp, mlp_kinds, [two_a0, two_a1, up_weight, grad_hidden_a])
-    kept_a, far_a = add_core(keep_a, send_a)
-    mid_b, two_b0 = norm_rows([kept_b, far_b, in_b], gain_two, bias_two)
-    two_b1 = swap_core(two_b0)
-    hidden_b, pre_b, keep_b, send_b = call(mlp, mlp_kinds, [two_b0, two_b1, up_weight, grad_hidden_b])
-    kept_b, far_b = add_core(keep_b, send_b)
-
-    down_order, up_order, attn_order, mix_order = (order_from(i) for i in (1, 0, 0, 0))
-    down_in = [cot_a0, cot_a1, cot_b0, cot_b1, hidden_a, hidden_b]
-    up_in = [two_a0, two_a1, two_b0, two_b1, pre_a, pre_b]
-    down_send, down_got = start_sum(load_plain, down_in, hidden_width, down_order)
-    up_send, up_got = start_sum(load_plain, up_in, hidden_width, up_order)
-
-    sums_kind = ((8, model_width), F32)
-    back_kinds = [rows32, rows16, sums_kind]
-    back_two = functools.partial(norm_backward, False, 0)
-    grad_mid_a, mid_a0, sums_two_a = call(
-        back_two,
-        back_kinds,
-        [kept_a, far_a, mid_a, gain_two, cot_a0],
-        after=[down_send, up_send],
-        cost=0.5,
-    )
-    mid_a1 = swap_core(mid_a0)
+    attend_kinds = [((half, head_width), BF16), ((8, half), F32), rows32, cut16]
+    hidden_kind = ((half, hidden_width), F32)
+    mlp_kinds = [((half, hidden_width), BF16)] * 2 + [rows32, cut16]
+    back_kinds = [rows32, cut16, ((8, model_width), F32)]
     grad_kinds = [((half, head_width), BF16)] + [((length, head_width), F32)] * 2
-    query_grad, key_grad, value_grad = call(
-        attend_back_first, grad_kinds, [mid_a0, mid_a1, attn_output, proj_a, proj_b, logs_a]
-    )
-    grad_mid_b, mid_b0, sums_two_b = call(
-        back_two, back_kinds, [kept_b, far_b, mid_b, gain_two, cot_b0], cost=0.5
-    )
-    mid_b1 = swap_core(mid_b0)
-    grad_proj, keep_a, send_a = call(
-        attend_back_second,
-        [((3, length, head_width), BF16), rows32, rows16],
-        [
-            mid_b0,
-            mid_b1,
-            attn_output,
-            proj_a,
-            proj_b,
-            logs_b,
-            query_grad,
-            key_grad,
-            value_grad,
-            w_attn,
-        ],
-    )
-    kept_a, far_a = add_core(keep_a, send_a)
-    keep_b, send_b = call(attend_back_last, [rows32, rows16], [grad_proj, w_attn])
-    kept_b, far_b = add_core(keep_b, send_b)
-
-    attn_in = [one_a0, one_a1, one_b0, one_b1, mid_a0, mid_a1, mid_b0, mid_b1, grad_proj, attended_a, attended_b]
-    attn_width = 4 * head_width
-    attn_send, attn_got = start_sum(load_attn, attn_in, attn_width, attn_order)
-    down_keep, down_got = second_sum(load_plain, down_in, down_got, hidden_width, down_order)
-    up_keep, up_got = second_sum(load_plain, up_in, up_got, hidden_width, up_order)
-
-    grad_in_a, in_a0, sums_one_a = call(
-        functools.partial(norm_backward, True, 0),
-        back_kinds,
-        [kept_a, far_a, in_a, gain_one, grad_mid_a],
-        after=[attn_send, down_keep, up_keep],
-        cost=0.5,
-    )
-    in_a1 = swap_core(in_a0)
-    grad_in_b, in_b0, sums = call(
-        functools.partial(norm_backward, True, 3),
-        back_kinds,
-        [kept_b, far_b, in_b, gain_one, grad_mid_b, sums_one_a, sums_two_a, sums_two_b],
-        cost=0.5,
-    )
-    in_b1 = swap_core(in_b0)
-    near_sums = swap_core(sums)
-    mass, mass_low, bias, field_send, field_keep = call(
-        functools.partial(mix_backward, pixels),
-        [
-            ((head_width, padded), F32),
-            ((head_width, padded), BF16),
-            ((8, padded), F32),
-            ((channels, half), BF16),
-            ((channels, half), F32),
-        ],
-        [pick, field_t, probs, values, score, mix_output, in_a0, in_a1, in_b0, in_b1],
-    )
     mass_kinds = [
+        ((head_width + 16, padded), BF16),
         ((head_width, padded), F32),
-        ((head_width, padded), BF16),
         ((8, padded), F32),
     ]
-    for bit in all_bits[:-1]:
-        mass, mass_low, bias = call(
-            mass_add,
-            mass_kinds,
-            [mass, swap_sample(mass_low, bit), bias, swap_sample(bias, bit)],
-            cost=0.3,
-        )
-    mass_got = swap_sample(mass_low, all_bits[-1])
-    bias_got = swap_sample(bias, all_bits[-1])
-
-    (own_weights,) = call(
-        lambda source, out: out.__setitem__(Ellipsis, source[...]),
-        [((3, own_width, head_width), BF16)],
-        [],
-        fetch=[
+    rest_rows = pltpu.VMEM((quarter + lines, model_width), F32)
+    down_order, up_order, attn_order, mix_order, mass_bits = map(order_from, AXES)
+    mix_steps = steps_of(mix_order)
+    back_two = functools.partial(norm_backward, False, 0)
+
+    def mix_a():
+        v.mixed_t, v.field_t, v.probs, v.values, v.keys_t, v.score, v.query_col = call(
+            functools.partial(mix_forward, pixels, quarter),
+            [
+                ((head_width, length), BF16),
+                ((channels, length), BF16),
+                ((heads * variables, length), F32),
+                ((padded, head_width), BF16),
+                ((head_width, padded), F32),
+                ((padded, LANES), F32),
+                ((head_width, LANES), F32),
+            ],
+            [variable_query],
+            fetch=[input_field, patch_table, variable_table, w_mix],
+            smem=[variable_ids],
+            limit=FIRST_LIMIT,
+            scratch=[pltpu.VMEM((padded, model_width), BF16)],
+        )
+
+    def mix_b():
+        send_a, send_b, v.keep_a, v.keep_b = call(
+            mix_out, [rows16, rows16, rows32, rows32], [mix_output], fetch=[v.mixed_t]
+        )
+        v.near_a, v.near_b = swap_core(send_a), swap_core(send_b)
+
+    def first_a():
+        v.kept_a, v.far_a = add_near(v.keep_a, v.near_a)
+
+    def first_b():
+        v.kept_b, v.far_b = add_near(v.keep_b, v.near_b)
+
+    def second_a():
+        first_a()
+
+    def second_b():
+        first_b()
+
+    def base():
+        blocks = [
             (
-                w_mix,
-                (3, own_width, head_width),
-                lambda ref: ref.at[:, pl.ds(lax.axis_index("dp") * own_width, own_width)],
+                pos_table,
+                (quarter, model_width),
+                lambda ref, k=k: ref.at[pl.ds((2 * k + my_core()) * quarter, quarter)],
             )
-        ],
-        cost=0.1,
-    )
-    lines = -(-(4 + 2 * mesh_dp) // LANES) * LANES
-    mix_in = [in_a0, in_a1, in_b0, in_b1, mixed_t, grad_in_a, grad_in_b, sums, near_sums]
-    mix_width = head_width + quarter + lines
-    steps = steps_of(mix_order)
-    rest = pltpu.VMEM((quarter + lines, model_width), F32)
-    (send,) = call(
-        functools.partial(mix_start, mesh_dp, lines, steps[0], mix_order[0]),
-        [((model_width // 2, mix_width), BF16)],
-        mix_in,
-        smem=[lead_bucket],
-        scratch=[rest],
-    )
-    got = swap_sample(send, mix_order[0])
-    mix_keep, send = call(
-        functools.partial(mix_second, mesh_dp, lines, steps[0], steps[1], mix_order[0], mix_order[1]),
-        halves(mix_width, model_width // 2),
-        [got] + mix_in,
-        smem=[lead_bucket],
-        scratch=[rest, pltpu.VMEM((model_width // 2, mix_width), F32)],
-    )
-    mix_keep, mix_got = rest_sum(mix_keep, swap_sample(send, mix_order[1]), mix_order)
-
-    own_field = (channels, quarter)
-    field_own, field_far = call(
-        field_sum, [(own_field, F32), (own_field, BF16)], [field_keep, swap_core(field_send)], cost=0.3
-    )
-    (field_grad,) = call(
-        field_last, [((1,) + own_field, F32)], [field_own, swap_chip(field_far)], cost=0.3
-    )
-
-    attn_keep, attn_got = second_sum(load_attn, attn_in, attn_got, attn_width, attn_order)
-    down_keep, down_got = rest_sum(down_keep, down_got, down_order)
-    up_keep, up_got = rest_sum(up_keep, up_got, up_order)
-    attn_keep, attn_got = rest_sum(attn_keep, attn_got, attn_order)
-
-    keep_a, send_a, keep_b, send_b = call(
-        mlp_out, [rows32, rows16] * 2, [hidden_a, hidden_b, down_weight], after=[in_b0]
-    )
-    rows_own, rows_far = call(
-        rows_sum,
-        [rows32, rows16],
-        [keep_a, swap_core(send_a), keep_b, swap_core(send_b), mid_a, mid_b],
-        cost=0.3,
-    )
-    (activations,) = call(last_plain, [rows32], [rows_own, swap_chip(rows_far)], cost=0.3)
-
-    final = own_width // mesh_mp
-    grad_mix, keep, send = call(
-        mix_finish,
-        [((3, own_width, head_width), F32)] + [((own_width // 2, padded), F32)] * 2,
-        [mass, mass_got, bias, bias_got, query_col, keys_t, table, own_weights, variable_query],
-        scratch=[pltpu.VMEM((own_width, padded), F32)],
-    )
-    keep, send = call(
-        tables_next,
-        [((final, padded), F32)] * 2,
-        [keep, swap_chip(send)],
-        scratch=[pltpu.VMEM((own_width // 2, padded), F32)],
-        cost=0.3,
-    )
-    patch_total, variable_total, query_total = call(
-        functools.partial(tables_last, pixels, variables),
-        [((pixels, final, variables), F32), ((final, variables), F32), ((8, final), F32)],
-        [keep, swap_core(send)],
-    )
-    (down_sum,) = call(last_turned, [((hidden_width, own_width), F32)], [down_keep, down_got])
-    (up_sum,) = call(last_plain, [((own_width, hidden_width), F32)], [up_keep, up_got])
-    attn_sum, attn_out_sum = call(
-        last_attn,
-        [((3, own_width, head_width), F32), ((head_width, own_width), F32)],
-        [attn_keep, attn_got],
-    )
-    mix_out_sum, pos_sum, lead_total, small = call(
-        functools.partial(mix_last, mesh_dp, quarter, final),
-        [
-            ((head_width, own_width), F32),
-            ((quarter, own_width), F32),
-            ((final, lead_table.shape[0]), F32),
-            ((8, final), F32),
-        ],
-        [mix_keep, mix_got],
-    )
+            for k in range(2)
+        ]
+        v.base_a, v.base_b = call(
+            base_rows, [rows32] * 2, [], fetch=blocks + [lead_table], smem=[lead_bucket]
+        )
+
+    def norm_a():
+        v.in_a, v.one_a0 = norm_rows([v.kept_a, v.far_a, v.base_a], gain_one, bias_one)
+        v.one_a1 = swap_core(v.one_a0)
+
+    def proj():
+        (v.proj_a,) = call(project, [proj_kind], [v.one_a0, v.one_a1, w_attn])
+
+    def norm_b():
+        v.in_b, v.one_b0, v.cot_own = call(
+            norm_relay,
+            [rows32, cut16, rows16],
+            [cotangent, v.kept_b, v.far_b, v.base_b, gain_one, bias_one],
+        )
+        v.one_b1 = swap_core(v.one_b0)
+        v.cot_far = swap_chip(v.cot_own)
+
+    def attend_a():
+        v.proj_b, v.attended_a, v.logs_a, v.keep_a, send_a = call(
+            attend_first,
+            [proj_kind] + attend_kinds,
+            [v.one_b0, v.one_b1, w_attn, v.proj_a, attn_output],
+        )
+        v.near_a = swap_core(send_a)
+
+    def attend_b():
+        v.attended_b, v.logs_b, v.keep_b, send_b = call(
+            attend_second, attend_kinds, [v.proj_a, v.proj_b, attn_output]
+        )
+        v.near_b = swap_core(send_b)
+
+    def cot():
+        v.cot_a0, v.cot_b0 = call(by_chip, [cut16] * 2, [v.cot_own, v.cot_far])
+        v.cot_a1, v.cot_b1 = swap_core(v.cot_a0), swap_core(v.cot_b0)
+
+    def hidden_a():
+        (v.grad_hidden_a,) = call(hidden_back, [hidden_kind], [v.cot_a0, v.cot_a1, down_weight])
+
+    def hidden_b():
+        (v.grad_hidden_b,) = call(hidden_back, [hidden_kind], [v.cot_b0, v.cot_b1, down_weight])
+
+    def two_a():
+        v.mid_a, v.two_a0 = norm_rows([v.kept_a, v.far_a, v.in_a], gain_two, bias_two)
+        v.two_a1 = swap_core(v.two_a0)
+
+    def two_b():
+        v.mid_b, v.two_b0 = norm_rows([v.kept_b, v.far_b, v.in_b], gain_two, bias_two)
+        v.two_b1 = swap_core(v.two_b0)
+
+    def mlp_a():
+        v.hidden_a, v.pre_a, v.m_keep_a, send_a = call(
+            mlp, mlp_kinds, [v.two_a0, v.two_a1, up_weight, v.grad_hidden_a]
+        )
+        v.m_near_a = swap_core(send_a)
+
+    def mlp_b():
+        v.hidden_b, v.pre_b, v.m_keep_b, send_b = call(
+            mlp, mlp_kinds, [v.two_b0, v.two_b1, up_weight, v.grad_hidden_b]
+        )
+        v.m_near_b = swap_core(send_b)
+
+    def third_a():
+        v.m_kept_a, v.m_far_a = add_near(v.m_keep_a, v.m_near_a)
+
+    def third_b():
+        v.m_kept_b, v.m_far_b = add_near(v.m_keep_b, v.m_near_b)
+
+    def down_in():
+        return [v.cot_a0, v.cot_a1, v.cot_b0, v.cot_b1, v.hidden_a, v.hidden_b]
+
+    def up_in():
+        return [v.two_a0, v.two_a1, v.two_b0, v.two_b1, v.pre_a, v.pre_b]
+
+    def attn_in():
+        one = [v.one_a0, v.one_a1, v.one_b0, v.one_b1]
+        mid = [v.back_a0, v.back_a1, v.back_b0, v.back_b1]
+        return one + mid + [v.grad_proj, v.attended_a, v.attended_b]
+
+    def up_1():
+        v.up_got = start_sum(load_plain, up_in(), hidden_width, up_order)
+
+    def down_1():
+        v.down_got = start_sum(load_plain, down_in(), hidden_width, down_order)
+
+    def attn_1():
+        v.attn_got = start_sum(load_attn, attn_in(), attn_width, attn_order)
+
+    def up_2():
+        v.up_keep, v.up_got = second_sum(load_plain, up_in(), v.up_got, hidden_width, up_order)
+
+    def down_2():
+        v.down_keep, v.down_got = second_sum(
+            load_plain, down_in(), v.down_got, hidden_width, down_order
+        )
+
+    def attn_2():
+        v.attn_keep, v.attn_got = second_sum(
+            load_attn, attn_in(), v.attn_got, attn_width, attn_order
+        )
+
+    def up_3():
+        v.up_keep, v.up_got = rest_sum(v.up_keep, v.up_got, up_order)
+
+    def down_3():
+        v.down_keep, v.down_got = rest_sum(v.down_keep, v.down_got, down_order)
+
+    def attn_3():
+        v.attn_keep, v.attn_got = rest_sum(v.attn_keep, v.attn_got, attn_order)
+
+    def mid_a():
+        v.grad_mid_a, v.back_a0, v.sums_two_a = call(
+            back_two, back_kinds, [v.m_kept_a, v.m_far_a, v.mid_a, gain_two, v.cot_a0]
+        )
+        v.back_a1 = swap_core(v.back_a0)
+
+    def mid_b():
+        v.grad_mid_b, v.back_b0, v.sums_two_b = call(
+            back_two, back_kinds, [v.m_kept_b, v.m_far_b, v.mid_b, gain_two, v.cot_b0]
+        )
+        v.back_b1 = swap_core(v.back_b0)
+
+    def back_a():
+        v.query_grad, v.key_grad, v.value_grad = call(
+            attend_back_first,
+            grad_kinds,
+            [v.back_a0, v.back_a1, attn_output, v.proj_a, v.proj_b, v.logs_a],
+        )
+
+    def back_b():
+        v.grad_proj, v.p_keep_a, send_a = call(
+            attend_back_second,
+            [((3, length, head_width), BF16), rows32, cut16],
+            [
+                v.back_b0,
+                v.back_b1,
+                attn_output,
+                v.proj_a,
+                v.proj_b,
+                v.logs_b,
+                v.query_grad,
+                v.key_grad,
+                v.value_grad,
+                w_attn,
+            ],
+        )
+        v.p_near_a = swap_core(send_a)
+
+    def back_c():
+        v.p_keep_b, send_b = call(attend_back_last, [rows32, cut16], [v.grad_proj, w_attn])
+        v.p_near_b = swap_core(send_b)
+
+    def fourth_a():
+        v.p_kept_a, v.p_far_a = add_near(v.p_keep_a, v.p_near_a)
+
+    def fourth_b():
+        v.p_kept_b, v.p_far_b = add_near(v.p_keep_b, v.p_near_b)
+
+    def in_a():
+        v.grad_in_a, v.in_a0, v.sums_one_a = call(
+            functools.partial(norm_backward, True, 0),
+            back_kinds,
+            [v.p_kept_a, v.p_far_a, v.in_a, gain_one, v.grad_mid_a],
+        )
+        v.in_a1 = swap_core(v.in_a0)
+
+    def in_b():
+        v.grad_in_b, v.in_b0, v.sums = call(
+            functools.partial(norm_backward, True, 3),
+            back_kinds,
+            [
+                v.p_kept_b,
+                v.p_far_b,
+                v.in_b,
+                gain_one,
+                v.grad_mid_b,
+                v.sums_one_a,
+                v.sums_two_a,
+                v.sums_two_b,
+            ],
+        )
+        v.in_b1 = swap_core(v.in_b0)
+        v.near_sums = swap_core(v.sums)
+
+    def mass_1():
+        packed, v.mass, v.bias, v.field_send, v.field_keep = call(
+            functools.partial(mix_backward, pixels),
+            mass_kinds + [((channels, half), BF16), ((channels, half), F32)],
+            [v.pick, v.field_t, v.probs, v.values, v.score, mix_output, v.in_a0, v.in_a1, v.in_b0, v.in_b1],
+        )
+        v.mass_got = swap_sample(packed, mass_bits[0])
+        v.field_near = swap_core(v.field_send)
+
+    def add_masses(bits):
+        for bit in bits:
+            packed, v.mass, v.bias = call(mass_add, mass_kinds, [v.mass, v.bias, v.mass_got])
+            v.mass_got = swap_sample(packed, bit)
+
+    def mass_2():
+        add_masses(mass_bits[1:2])
+
+    def mass_3():
+        add_masses(mass_bits[2:])
+
+    def mix_in():
+        rows = [v.in_a0, v.in_a1, v.in_b0, v.in_b1]
+        return rows + [v.grad_in_a, v.grad_in_b, v.sums, v.near_sums]
+
+    def mix_1():
+        (send,) = call(
+            functools.partial(mix_start, mesh_dp, lines, mix_steps[0], mix_order[0]),
+            [((model_width // 2, mix_width), BF16)],
+            [v.mixed_t] + mix_in(),
+            smem=[lead_bucket],
+            scratch=[rest_rows],
+        )
+        v.mix_got = swap_sample(send, mix_order[0])
+
+    def mix_2():
+        v.mix_keep, send = call(
+            functools.partial(
+                mix_second, mesh_dp, lines, mix_steps[0], mix_steps[1], mix_order[0], mix_order[1]
+            ),
+            halves(mix_width, model_width // 2),
+            [v.mixed_t, v.mix_got] + mix_in(),
+            smem=[lead_bucket],
+            scratch=[rest_rows, pltpu.VMEM((model_width // 2, mix_width), F32)],
+        )
+        v.mix_got = swap_sample(send, mix_order[1])
+
+    def mix_3():
+        v.mix_keep, v.mix_got = rest_sum(v.mix_keep, v.mix_got, mix_order)
+
+    def field_1():
+        v.field_own, far = call(
+            field_sum, [(own_field, F32), (own_field, BF16)], [v.field_keep, v.field_near]
+        )
+        v.field_got = swap_chip(far)
+
+    def field_2():
+        (v.field_grad,) = call(
+            field_last, [((1,) + own_field, F32)], [v.field_own, v.field_got], final=True
+        )
+
+    def rows_1():
+        v.r_keep_a, send_a, v.r_keep_b, send_b = call(
+            mlp_out, [rows32, cut16] * 2, [v.hidden_a, v.hidden_b, down_weight]
+        )
+        v.r_near_a, v.r_near_b = swap_core(send_a), swap_core(send_b)
+
+    def rows_2():
+        v.rows_own, far = call(
+            rows_sum,
+            [rows32, rows16],
+            [v.r_keep_a, v.r_near_a, v.r_keep_b, v.r_near_b, v.mid_a, v.mid_b],
+        )
+        v.rows_got = swap_chip(far)
+
+    def rows_3():
+        (v.activations,) = call(last_plain, [rows32], [v.rows_own, v.rows_got], final=True)
+
+    def weights():
+        v.own_weights, v.pick = call(
+            functools.partial(take_weights, pixels),
+            [((3, own_width, head_width), BF16), ((channels, channels), BF16)],
+            [],
+            smem=[variable_ids],
+            fetch=[
+                (
+                    w_mix,
+                    (3, own_width, head_width),
+                    lambda ref: ref.at[:, pl.ds(lax.axis_index("dp") * own_width, own_width)],
+                )
+            ],
+        )
+
+    def finish():
+        v.t_keep, send, v.grad_mix = call(
+            functools.partial(mix_finish, pixels),
+            [((own_width // 2, padded), F32)] * 2 + [((3, own_width, head_width), F32)],
+            [
+                v.query_col,
+                v.keys_t,
+                patch_table,
+                variable_table,
+                v.mass,
+                v.bias,
+                v.mass_got,
+                v.own_weights,
+                variable_query,
+            ],
+            scratch=[pltpu.VMEM((own_width, padded), F32)],
+        )
+        v.t_far = swap_chip(send)
+
+    def tables_1():
+        v.t_keep, send = call(
+            tables_next,
+            [((final, padded), F32)] * 2,
+            [v.t_keep, v.t_far],
+            scratch=[pltpu.VMEM((own_width // 2, padded), F32)],
+        )
+        v.t_near = swap_core(send)
+
+    def tables_2():
+        v.patch_total, v.variable_total, v.query_total = call(
+            functools.partial(tables_last, pixels, variables),
+            [((pixels, final, variables), F32), ((final, variables), F32), ((8, final), F32)],
+            [v.t_keep, v.t_near],
+            final=True,
+        )
+
+    def down_4():
+        (v.down_sum,) = call(
+            last_turned, [((hidden_width, own_width), F32)], [v.down_keep, v.down_got], final=True
+        )
+
+    def up_4():
+        (v.up_sum,) = call(
+            last_plain, [((own_width, hidden_width), F32)], [v.up_keep, v.up_got], final=True
+        )
+
+    def mix_4():
+        v.mix_out_sum, v.pos_sum, v.lead_total, v.small = call(
+            functools.partial(mix_last, mesh_dp, quarter, final),
+            [
+                ((head_width, own_width), F32),
+                ((quarter, own_width), F32),
+                ((final, lead_table.shape[0]), F32),
+                ((8, final), F32),
+            ],
+            [v.mix_keep, v.mix_got],
+            final=True,
+        )
+
+    def attn_4():
+        v.attn_sum, v.attn_out_sum = call(
+            last_attn,
+            [((3, own_width, head_width), F32), ((head_width, own_width), F32)],
+            [v.attn_keep, v.attn_got],
+            final=True,
+        )
+
+    steps = dict(locals())
+    for name in ORDER:
+        now[:] = [name]
+        steps[name]()
     return (
-        activations,
-        field_grad,
-        patch_total.transpose(2, 0, 1),
-        variable_total.T,
-        query_total[7],
-        grad_mix.transpose(1, 0, 2),
-        mix_out_sum,
-        pos_sum,
-        lead_total.T,
-        small[0],
-        small[1],
-        attn_sum.transpose(1, 0, 2),
-        attn_out_sum,
-        small[2],
-        small[3],
-        up_sum,
-        down_sum,
+        v.activations,
+        v.field_grad,
+        v.patch_total.transpose(2, 0, 1),
+        v.variable_total.T,
+        v.query_total[7],
+        v.grad_mix.transpose(1, 0, 2),
+        v.mix_out_sum,
+        v.pos_sum,
+        v.lead_total.T,
+        v.small[0],
+        v.small[1],
+        v.attn_sum.transpose(1, 0, 2),
+        v.attn_out_sum,
+        v.small[2],
+        v.small[3],
+        v.up_sum,
+        v.down_sum,
     )
 
 

time: 193 us -> 160 us (0.83)
  waiting for transfers between devices: 89 us -> 65.1 us
  starting transfers between devices: 50.4 us -> 42.7 us
  local copies, waits for them, and re-layouts: 7.71 us -> 2.95 us
  Pallas kernels: 43.6 us -> 46.6 us
    ppermute x18 -> x15, waiting for transfers between devices: 55.6 us -> 32.1 us  [swap_sample(): return lax.ppermute(value, 'dp', pairs(mesh_dp, bit))]
    ppermute x18 -> x15, starting transfers between devices: 28 us -> 16.3 us  [swap_sample(): return lax.ppermute(value, 'dp', pairs(mesh_dp, bit))]
    ppermute x12, waiting for transfers between devices: 31.6 us -> 23.6 us  [swap_chip(): return lax.ppermute(value, 'mp', pairs(mesh_mp, 2))]
    ppermute x23 -> x41, waiting for transfers between devices: 1.78 us -> 9.42 us  [swap_core(): return lax.ppermute(value, 'mp', pairs(mesh_mp, 1))]
    ppermute x23 -> x41, starting transfers between devices: 4.94 us -> 10.8 us  [swap_core(): return lax.ppermute(value, 'mp', pairs(mesh_mp, 1))]
    unnamed x42 -> x50, local copies, waits for them, and re-layouts: 6.67 us -> 1.91 us
    pallas_call x57 -> x58, Pallas kernels: 43.6 us -> 46.6 us  [launch(): pl.pallas_call(run, out_shape=[jax.ShapeDtypeStruct(shape, kind) for shap...]
    ppermute x12, starting transfers between devices: 17.5 us -> 15.5 us  [swap_chip(): return lax.ppermute(value, 'mp', pairs(mesh_mp, 2))]
  transfers between devices with their start and end apart: 53 -> 68, of which waited for: 22 -> 36; matrix products, arithmetic and copies ran while one was open for 1% -> 0% of each run, Pallas kernels for 19% -> 23%
where the time goes in v1:
time: 160 us
  waiting for transfers between devices  65.1 us (41%)
  Pallas kernels  46.6 us (29%)
  starting transfers between devices  42.7 us (27%)
  local copies, waits for them, and re-layouts  2.95 us (2%)
  between operations  2.23 us (1%)
    pallas_call x58, Pallas kernels, launch(): pl.pallas_call(run, out_shape=[jax.ShapeDtypeStruct(shape, kind) for shap...  46.6 us
    ppermute x15, waiting for transfers between devices, swap_sample(): return lax.ppermute(value, 'dp', pairs(mesh_dp, bit))  32.1 us
    ppermute x12, waiting for transfers between devices, swap_chip(): return lax.ppermute(value, 'mp', pairs(mesh_mp, 2))  23.6 us
    ppermute x15, starting transfers between devices, swap_sample(): return lax.ppermute(value, 'dp', pairs(mesh_dp, bit))  16.3 us
    ppermute x12, starting transfers between devices, swap_chip(): return lax.ppermute(value, 'mp', pairs(mesh_mp, 2))  15.5 us
    ppermute x41, starting transfers between devices, swap_core(): return lax.ppermute(value, 'mp', pairs(mesh_mp, 1))  10.8 us
    ppermute x41, waiting for transfers between devices, swap_core(): return lax.ppermute(value, 'mp', pairs(mesh_mp, 1))  9.42 us
  transfers between devices with their start and end apart: 68, of which 36 were waited for; matrix products, arithmetic and copies ran while one was open for 0% of the time, Pallas kernels for 23%

profile of v1, /device:TPU:0, one launch (start us, length us, event | category | flops | bytes accessed | tf_op | source)
XLA Modules:
  0.0 159.6 jit_solution(12724360390917196515)
XLA Ops:
  0.7 4.9 %mix_a.1 = (bf16[256,512]{1,0:T(8,128)(2,1)}, bf16[192,512]{1,0:T(8,128)(2,1)}, f32[192,512]{1,0:T(8,128)}, bf16[256,256]{1,0:T(8,128)(2,1)}, f32[256,256]{1,0:T...) custom-call(s32[48]{0:T(128)} %refs_0_.8, bf16[1,192,512]{2,1,0:T(8,128)(2,1)} %refs_1_.3, bf16[48,4,1024]{2,1,0:T(4,128)(2,1)} %refs_2_.9, ...), custom_call_target="tpu_custom_call" | custom-call | flops 100000000 | tf_op jit(solution)/shard_map/mix_a/pallas_call | solution.py:115
  8.9 3.0 %collective-permute-start.3 = (bf16[128,1024]{1,0:T(8,128)(2,1)S(1)}, bf16[128,1024]{1,0:T(8,128)(2,1)S(1)}, u32[]{:S(2)}, u32[]{:S(2)}) collective-permute-start(bf16[128,1024]{1,0:T(8,128)(2,1)S(1)} %get-tuple-element.182), channel_id=1, source_target_pairs={{0,2},{1,3},{2,0},{3,1},{4,6},{5,7},{6,4},{7,5},{8,10},{9,11},{10,... | collective-permute-start | bytes 786440 | tf_op jit(solution)/shard_map/ppermute | solution.py:862
  13.7 5.2 %collective-permute-done.3.refs_1_ = bf16[128,1024]{1,0:T(8,128)(2,1)S(1)} collective-permute-done((bf16[128,1024]{1,0:T(8,128)(2,1)S(1)}, bf16[128,1024]{1,0:T(8,128)(2,1)S(1)}, u32[]{:S(2)}, u32[]{:S(2)}) %collective-permute-start.3) | collective-permute-done | bytes 262176 | tf_op jit(solution)/shard_map/ppermute | solution.py:862
  21.4 2.7 %collective-permute-done.2.refs_2_ = bf16[128,1024]{1,0:T(8,128)(2,1)S(1)} collective-permute-done((bf16[128,1024]{1,0:T(8,128)(2,1)S(1)}, bf16[128,1024]{1,0:T(8,128)(2,1)S(1)}, u32[]{:S(2)}, u32[]{:S(2)}) %collective-permute-start.2) | collective-permute-done | bytes 262176 | tf_op jit(solution)/shard_map/ppermute | solution.py:862
  25.0 1.7 %collective-permute-start.11 = (bf16[128,1024]{1,0:T(8,128)(2,1)S(1)}, bf16[128,1024]{1,0:T(8,128)(2,1)S(1)}, u32[]{:S(2)}, u32[]{:S(2)}) collective-permute-start(bf16[128,1024]{1,0:T(8,128)(2,1)S(1)} %get-tuple-element.196.refs_0_), channel_id=1, source_target_pairs={{0,2},{1,3},{2,0},{3,1},{4,6},{5,7},{6,4},{7,5},{8,10},{9,11},{10,... | collective-permute-start | bytes 786440 | tf_op jit(solution)/shard_map/ppermute | solution.py:862
  26.7 2.8 %attend_a.1 = (bf16[3,256,256]{2,1,0:T(8,128)(2,1)S(1)}, bf16[256,256]{1,0:T(8,128)(2,1)S(1)}, f32[8,256]{1,0:T(8,128)S(1)}, f32[128,1024]{1,0:T(8,128)S(1)}, bf...) custom-call(bf16[64,1024]{1,0:T(8,128)(2,1)S(1)} %get-tuple-element.187.refs_0_.refs_4_.refs_5_, ...), custom_call_target="tpu_custom_call" | custom-call | flops 100000000 | tf_op jit(solution)/shard_map/attend_a/pallas_call | solution.py:115
  33.9 2.2 %attend_b.1 = (bf16[256,256]{1,0:T(8,128)(2,1)S(1)}, f32[8,256]{1,0:T(8,128)S(1)}, f32[128,1024]{1,0:T(8,128)S(1)}, bf16[64,1024]{1,0:T(8,128)(2,1)S(1)}, bf16[64,1024]{1,0:T(8,128)(2,1)S(1)}) custom-call(bf16[3,256,256]{2,1,0:T(8,128)(2,1)S(1)} %proj.1.refs_6_.refs_5_.refs_0_, bf16[3,256,256]{2,1,0:T(8,128)(2,1)S(1)} %get-tuple-element.193.refs_3_.refs_1_.refs_6_, ...), custom_call_target="tpu_custom_call" | custom-call | flops 100000000 | tf_op jit(solution)/shard_map/attend_b/pallas_call | solution.py:115
  37.8 1.8 %collective-permute-start.18 = (bf16[128,1024]{1,0:T(8,128)(2,1)S(1)}, bf16[128,1024]{1,0:T(8,128)(2,1)S(1)}, u32[]{:S(2)}, u32[]{:S(2)}) collective-permute-start(bf16[128,1024]{1,0:T(8,128)(2,1)S(1)} %get-tuple-element.208), channel_id=1, source_target_pairs={{0,2},{1,3},{2,0},{3,1},{4,6},{5,7},{6,4},{7,5},{8,10},{9,11},{10,... | collective-permute-start | bytes 786440 | tf_op jit(solution)/shard_map/ppermute | solution.py:862
  41.7 1.9 %mlp_a.1 = (bf16[256,1024]{1,0:T(8,128)(2,1)S(1)}, bf16[256,1024]{1,0:T(8,128)(2,1)S(1)}, f32[128,1024]{1,0:T(8,128)S(1)}, bf16[64,1024]{1,0:T(8,128)(2,1)S(1)}, bf16[64,1024]{1,0:T(8,128)(2,1)S(1)}) custom-call(bf16[64,1024]{1,0:T(8,128)(2,1)S(1)} %get-tuple-element.204.refs_0_.refs_1_, bf16[64,1024]{1,0:T(8,128)(2,1)S(1)} %get-tuple-element.205.refs_1_.refs_2_, ...), custom_call_target="tpu_custom_call" | custom-call | flops 100000000 | tf_op jit(solution)/shard_map/mlp_a/pallas_call | solution.py:115
  48.2 1.9 %mlp_b.1 = (bf16[256,1024]{1,0:T(8,128)(2,1)S(1)}, bf16[256,1024]{1,0:T(8,128)(2,1)S(1)}, f32[128,1024]{1,0:T(8,128)S(1)}, bf16[64,1024]{1,0:T(8,128)(2,1)S(1)}, bf16[64,1024]{1,0:T(8,128)(2,1)S(1)}) custom-call(bf16[64,1024]{1,0:T(8,128)(2,1)S(1)} %get-tuple-element.211.refs_0_.refs_4_.refs_5_, ...), custom_call_target="tpu_custom_call" | custom-call | flops 12000000000 | tf_op jit(solution)/shard_map/mlp_b/pallas_call | solution.py:115
  50.9 1.8 %collective-permute-start.25 = (bf16[512,1024]{1,0:T(8,128)(2,1)S(1)}, bf16[512,1024]{1,0:T(8,128)(2,1)S(1)}, u32[]{:S(2)}, u32[]{:S(2)}) collective-permute-start(bf16[512,1024]{1,0:T(8,128)(2,1)S(1)} %down_1.1.refs_10_), channel_id=1, source_target_pairs={{0,4},{4,0},{8,12},{12,8},{16,20},{20,16},{24,28},{28,24},{1,5},{5... | collective-permute-start | bytes 3145736 | tf_op jit(solution)/shard_map/ppermute | solution.py:865
  53.7 1.6 %collective-permute-start.37 = (bf16[512,1024]{1,0:T(8,128)(2,1)S(1)}, bf16[512,1024]{1,0:T(8,128)(2,1)S(1)}, u32[]{:S(2)}, u32[]{:S(2)}) collective-permute-start(bf16[512,1024]{1,0:T(8,128)(2,1)S(1)} %up_1.1.refs_3_), channel_id=1, source_target_pairs={{0,8},{4,12},{8,0},{12,4},{16,24},{20,28},{24,16},{28,20},{1,9},{5... | collective-permute-start | bytes 3145736 | tf_op jit(solution)/shard_map/ppermute | solution.py:865
  59.0 5.5 %collective-permute-done.29.refs_1_ = bf16[128,1024]{1,0:T(8,128)(2,1)S(1)} collective-permute-done((bf16[128,1024]{1,0:T(8,128)(2,1)S(1)}, bf16[128,1024]{1,0:T(8,128)(2,1)S(1)}, u32[]{:S(2)}, u32[]{:S(2)}) %collective-permute-start.29) | collective-permute-done | bytes 262176 | tf_op jit(solution)/shard_map/ppermute | solution.py:862
  66.6 2.8 %back_a.1 = (bf16[256,256]{1,0:T(8,128)(2,1)S(1)}, f32[512,256]{1,0:T(8,128)S(1)}, f32[512,256]{1,0:T(8,128)S(1)}) custom-call(bf16[64,1024]{1,0:T(8,128)(2,1)S(1)} %get-tuple-element.227.refs_0_.refs_8_.refs_9_, bf16[64,1024]{1,0:T(8,128)(2,1)S(1)} %get-tuple-element.228.refs_1_.refs_9_.refs_10_, ...), custom_call_target="tpu_custom_call" | custom-call | flops 100000000 | tf_op jit(solution)/shard_map/back_a/pallas_call | solution.py:115
  71.7 3.2 %back_b.1 = (bf16[3,512,256]{2,1,0:T(8,128)(2,1)S(1)}, f32[128,1024]{1,0:T(8,128)S(1)}, bf16[64,1024]{1,0:T(8,128)(2,1)S(1)}, bf16[64,1024]{1,0:T(8,128)(2,1)S(1)}) custom-call(bf16[64,1024]{1,0:T(8,128)(2,1)S(1)} %get-tuple-element.232.refs_0_.refs_12_.refs_13_, bf16[64,1024]{1,0:T(8,128)(2,1)S(1)} %get-tuple-element.233.refs_1_.refs_13_.refs_14_, ...), custom_call_target="tpu_custom_call" | custom-call | flops 100000000 | tf_op jit(solution)/shard_map/back_b/pallas_call | solution.py:115
  78.3 1.6 collective-permute-start.36
  83.8 2.8 %collective-permute-start.51 = (bf16[256,1024]{1,0:T(8,128)(2,1)S(1)}, bf16[256,1024]{1,0:T(8,128)(2,1)S(1)}, u32[]{:S(2)}, u32[]{:S(2)}) collective-permute-start(bf16[256,1024]{1,0:T(8,128)(2,1)S(1)} %get-tuple-element.280), channel_id=1, source_target_pairs={{0,16},{4,20},{8,24},{12,28},{16,0},{20,4},{24,8},{28,12},{1,17},{... | collective-permute-start | bytes 1572872 | tf_op jit(solution)/shard_map/ppermute | solution.py:865
  88.1 4.2 %collective-permute-done.42.refs_1_ = bf16[128,1024]{1,0:T(8,128)(2,1)S(1)} collective-permute-done((bf16[128,1024]{1,0:T(8,128)(2,1)S(1)}, bf16[128,1024]{1,0:T(8,128)(2,1)S(1)}, u32[]{:S(2)}, u32[]{:S(2)}) %collective-permute-start.42) | collective-permute-done | bytes 262176 | tf_op jit(solution)/shard_map/ppermute | solution.py:862
  95.1 1.6 %mass_1.1 = (bf16[272,256]{1,0:T(8,128)(2,1)S(1)}, f32[256,256]{1,0:T(8,128)S(1)}, f32[8,256]{1,0:T(8,128)S(1)}, bf16[192,256]{1,0:T(8,128)(2,1)S(1)}, f32[192,256]{1,0:T(8,128)S(1)}) custom-call(bf16[192,192]{1,0:T(8,128)(2,1)S(1)} %get-tuple-element.246.refs_0_, bf16[192,512]{1,0:T(8,128)(2,1)S(1)} %copy-done.14, f32[192,512]{1,0:T(8,128)S(1)} %copy-done.11, ...), custom_call_target="tpu_custom_call" | custom-call | flops 100000000 | tf_op jit(solution)/shard_map/mass_1/pallas_call | solution.py:115
  96.9 10.5 %collective-permute-done.49.refs_1_ = bf16[256,1024]{1,0:T(8,128)(2,1)S(1)} collective-permute-done((bf16[256,1024]{1,0:T(8,128)(2,1)S(1)}, bf16[256,1024]{1,0:T(8,128)(2,1)S(1)}, u32[]{:S(2)}, u32[]{:S(2)}) %collective-permute-start.49) | collective-permute-done | bytes 524320 | tf_op jit(solution)/shard_map/ppermute | solution.py:865
  109.0 1.6 collective-permute-start.60
  113.0 1.6 %collective-permute-start.50 = (bf16[272,256]{1,0:T(8,128)(2,1)S(1)}, bf16[272,256]{1,0:T(8,128)(2,1)S(1)}, u32[]{:S(2)}, u32[]{:S(2)}) collective-permute-start(bf16[272,256]{1,0:T(8,128)(2,1)S(1)} %get-tuple-element.279.refs_2_), channel_id=1, source_target_pairs={{0,4},{4,0},{8,12},{12,8},{16,20},{20,16},{24,28},{28,24},{1,5},{5... | collective-permute-start | bytes 417800 | tf_op jit(solution)/shard_map/ppermute | solution.py:865
  115.4 11.5 %collective-permute-done.50.refs_2_ = bf16[272,256]{1,0:T(8,128)(2,1)S(1)} collective-permute-done((bf16[272,256]{1,0:T(8,128)(2,1)S(1)}, bf16[272,256]{1,0:T(8,128)(2,1)S(1)}, u32[]{:S(2)}, u32[]{:S(2)}) %collective-permute-start.50) | collective-permute-done | bytes 139296 | tf_op jit(solution)/shard_map/ppermute | solution.py:865
  128.8 1.5 collective-permute-done.56.refs_1_
  130.9 2.1 %collective-permute-start.63 = (bf16[272,256]{1,0:T(8,128)(2,1)S(1)}, bf16[272,256]{1,0:T(8,128)(2,1)S(1)}, u32[]{:S(2)}, u32[]{:S(2)}) collective-permute-start(bf16[272,256]{1,0:T(8,128)(2,1)S(1)} %get-tuple-element.282.refs_3_), channel_id=1, source_target_pairs={{0,16},{4,20},{8,24},{12,28},{16,0},{20,4},{24,8},{28,12},{1,17},{... | collective-permute-start | bytes 417800 | tf_op jit(solution)/shard_map/ppermute | solution.py:865
  136.1 1.9 %collective-permute-start.61 = (bf16[128,1024]{1,0:T(8,128)(2,1)S(1)}, bf16[128,1024]{1,0:T(8,128)(2,1)S(1)}, u32[]{:S(2)}, u32[]{:S(2)}) collective-permute-start(bf16[128,1024]{1,0:T(8,128)(2,1)S(1)} %get-tuple-element.298), channel_id=1, source_target_pairs={{0,16},{4,20},{8,24},{12,28},{16,0},{20,4},{24,8},{28,12},{1,17},{... | collective-permute-start | bytes 786440 | tf_op jit(solution)/shard_map/ppermute | solution.py:865
  139.3 1.7 %collective-permute-done.63.refs_6_ = bf16[272,256]{1,0:T(8,128)(2,1)S(1)} collective-permute-done((bf16[272,256]{1,0:T(8,128)(2,1)S(1)}, bf16[272,256]{1,0:T(8,128)(2,1)S(1)}, u32[]{:S(2)}, u32[]{:S(2)}) %collective-permute-start.63) | collective-permute-done | bytes 139296 | tf_op jit(solution)/shard_map/ppermute | solution.py:865
  141.0 1.7 %finish.1 = (f32[64,256]{1,0:T(8,128)S(1)}, f32[64,256]{1,0:T(8,128)S(1)}, f32[3,128,256]{2,1,0:T(8,128)}) custom-call(f32[256,128]{1,0:T(8,128)S(1)} %copy-done.15, f32[256,256]{1,0:T(8,128)S(1)} %copy-done.13, bf16[48,4,1024]{2,1,0:T(4,128)(2,1)S(1)} %copy-done.9, bf16[48,1024]{1,0:T(8,128)(2,1)S(1)} %copy-done.10, ...), custom_call_target="tpu_custom_call" | custom-call | flops 100000000 | tf_op jit(solution)/shard_map/finish/pallas_call | solution.py:115
  144.8 2.6 %collective-permute-done.64.refs_1_ = f32[64,256]{1,0:T(8,128)S(1)} collective-permute-done((f32[64,256]{1,0:T(8,128)S(1)}, f32[64,256]{1,0:T(8,128)S(1)}, u32[]{:S(2)}, u32[]{:S(2)}) %collective-permute-start.64) | collective-permute-done | bytes 65568 | tf_op jit(solution)/shard_map/ppermute | solution.py:862
  147.5 2.4 %collective-permute-done.62.refs_1_ = bf16[256,512]{1,0:T(8,128)(2,1)S(1)} collective-permute-done((bf16[256,512]{1,0:T(8,128)(2,1)S(1)}, bf16[256,512]{1,0:T(8,128)(2,1)S(1)}, u32[]{:S(2)}, u32[]{:S(2)}) %collective-permute-start.62) | collective-permute-done | bytes 262176 | tf_op jit(solution)/shard_map/ppermute | solution.py:865
  150.1 1.6 %collective-permute-done.61.refs_1_ = bf16[128,1024]{1,0:T(8,128)(2,1)S(1)} collective-permute-done((bf16[128,1024]{1,0:T(8,128)(2,1)S(1)}, bf16[128,1024]{1,0:T(8,128)(2,1)S(1)}, u32[]{:S(2)}, u32[]{:S(2)}) %collective-permute-start.61) | collective-permute-done | bytes 262176 | tf_op jit(solution)/shard_map/ppermute | solution.py:865
  155.3 2.9 %collective-permute-done.67.refs_1_ = bf16[128,512]{1,0:T(8,128)(2,1)S(1)} collective-permute-done((bf16[128,512]{1,0:T(8,128)(2,1)S(1)}, bf16[128,512]{1,0:T(8,128)(2,1)S(1)}, u32[]{:S(2)}, u32[]{:S(2)}) %collective-permute-start.67) | collective-permute-done | bytes 131104 | tf_op jit(solution)/shard_map/ppermute | solution.py:865
  (214 shorter events, 60.6 us)
Async XLA Ops:
  8.9 10.0 %collective-permute-start.3 = (bf16[128,1024]{1,0:T(8,128)(2,1)S(1)}, bf16[128,1024]{1,0:T(8,128)(2,1)S(1)}, u32[]{:S(2)}, u32[]{:S(2)}) collective-permute-start(bf16[128,1024]{1,0:T(8,128)(2,1)S(1)} %get-tuple-element.182), channel_id=1, source_target_pairs={{0,2},{1,3},{2,0},{3,1},{4,6},{5,7},{6,4},{7,5},{8,10},{9,11},{10,... | collective-permute-start | bytes 786440 | tf_op jit(solution)/shard_map/ppermute | solution.py:862
  12.0 12.1 %collective-permute-start.2 = (bf16[128,1024]{1,0:T(8,128)(2,1)S(1)}, bf16[128,1024]{1,0:T(8,128)(2,1)S(1)}, u32[]{:S(2)}, u32[]{:S(2)}) collective-permute-start(bf16[128,1024]{1,0:T(8,128)(2,1)S(1)} %get-tuple-element.180), channel_id=1, source_target_pairs={{0,2},{1,3},{2,0},{3,1},{4,6},{5,7},{6,4},{7,5},{8,10},{9,11},{10,... | collective-permute-start | bytes 786440 | tf_op jit(solution)/shard_map/ppermute | solution.py:862
  25.0 8.3 %collective-permute-start.11 = (bf16[128,1024]{1,0:T(8,128)(2,1)S(1)}, bf16[128,1024]{1,0:T(8,128)(2,1)S(1)}, u32[]{:S(2)}, u32[]{:S(2)}) collective-permute-start(bf16[128,1024]{1,0:T(8,128)(2,1)S(1)} %get-tuple-element.196.refs_0_), channel_id=1, source_target_pairs={{0,2},{1,3},{2,0},{3,1},{4,6},{5,7},{6,4},{7,5},{8,10},{9,11},{10,... | collective-permute-start | bytes 786440 | tf_op jit(solution)/shard_map/ppermute | solution.py:862
  31.2 8.6 %collective-permute-start.10 = (bf16[128,1024]{1,0:T(8,128)(2,1)S(1)}, bf16[128,1024]{1,0:T(8,128)(2,1)S(1)}, u32[]{:S(2)}, u32[]{:S(2)}) collective-permute-start(bf16[128,1024]{1,0:T(8,128)(2,1)S(1)} %get-tuple-element.195), channel_id=1, source_target_pairs={{0,2},{1,3},{2,0},{3,1},{4,6},{5,7},{6,4},{7,5},{8,10},{9,11},{10,... | collective-permute-start | bytes 786440 | tf_op jit(solution)/shard_map/ppermute | solution.py:862
  37.8 8.6 %collective-permute-start.18 = (bf16[128,1024]{1,0:T(8,128)(2,1)S(1)}, bf16[128,1024]{1,0:T(8,128)(2,1)S(1)}, u32[]{:S(2)}, u32[]{:S(2)}) collective-permute-start(bf16[128,1024]{1,0:T(8,128)(2,1)S(1)} %get-tuple-element.208), channel_id=1, source_target_pairs={{0,2},{1,3},{2,0},{3,1},{4,6},{5,7},{6,4},{7,5},{8,10},{9,11},{10,... | collective-permute-start | bytes 786440 | tf_op jit(solution)/shard_map/ppermute | solution.py:862
  50.9 27.3 %collective-permute-start.25 = (bf16[512,1024]{1,0:T(8,128)(2,1)S(1)}, bf16[512,1024]{1,0:T(8,128)(2,1)S(1)}, u32[]{:S(2)}, u32[]{:S(2)}) collective-permute-start(bf16[512,1024]{1,0:T(8,128)(2,1)S(1)} %down_1.1.refs_10_), channel_id=1, source_target_pairs={{0,4},{4,0},{8,12},{12,8},{16,20},{20,16},{24,28},{28,24},{1,5},{5... | collective-permute-start | bytes 3145736 | tf_op jit(solution)/shard_map/ppermute | solution.py:865
  53.7 29.2 %collective-permute-start.37 = (bf16[512,1024]{1,0:T(8,128)(2,1)S(1)}, bf16[512,1024]{1,0:T(8,128)(2,1)S(1)}, u32[]{:S(2)}, u32[]{:S(2)}) collective-permute-start(bf16[512,1024]{1,0:T(8,128)(2,1)S(1)} %up_1.1.refs_3_), channel_id=1, source_target_pairs={{0,8},{4,12},{8,0},{12,4},{16,24},{20,28},{24,16},{28,20},{1,9},{5... | collective-permute-start | bytes 3145736 | tf_op jit(solution)/shard_map/ppermute | solution.py:865
  55.3 9.2 %collective-permute-start.29 = (bf16[128,1024]{1,0:T(8,128)(2,1)S(1)}, bf16[128,1024]{1,0:T(8,128)(2,1)S(1)}, u32[]{:S(2)}, u32[]{:S(2)}) collective-permute-start(bf16[128,1024]{1,0:T(8,128)(2,1)S(1)} %get-tuple-element.226), channel_id=1, source_target_pairs={{0,2},{1,3},{2,0},{3,1},{4,6},{5,7},{6,4},{7,5},{8,10},{9,11},{10,... | collective-permute-start | bytes 786440 | tf_op jit(solution)/shard_map/ppermute | solution.py:862
  58.5 11.0 %collective-permute-start.28 = (bf16[128,1024]{1,0:T(8,128)(2,1)S(1)}, bf16[128,1024]{1,0:T(8,128)(2,1)S(1)}, u32[]{:S(2)}, u32[]{:S(2)}) collective-permute-start(bf16[128,1024]{1,0:T(8,128)(2,1)S(1)} %get-tuple-element.225), channel_id=1, source_target_pairs={{0,2},{1,3},{2,0},{3,1},{4,6},{5,7},{6,4},{7,5},{8,10},{9,11},{10,... | collective-permute-start | bytes 786440 | tf_op jit(solution)/shard_map/ppermute | solution.py:862
  75.7 34.9 %collective-permute-start.46 = (bf16[512,1024]{1,0:T(8,128)(2,1)S(1)}, bf16[512,1024]{1,0:T(8,128)(2,1)S(1)}, u32[]{:S(2)}, u32[]{:S(2)}) collective-permute-start(bf16[512,1024]{1,0:T(8,128)(2,1)S(1)} %attn_1.1.refs_2_), channel_id=1, source_target_pairs={{0,4},{4,0},{8,12},{12,8},{16,20},{20,16},{24,28},{28,24},{1,5},{5... | collective-permute-start | bytes 3145736 | tf_op jit(solution)/shard_map/ppermute | solution.py:865
  78.3 9.2 %collective-permute-start.36 = (bf16[128,1024]{1,0:T(8,128)(2,1)S(1)}, bf16[128,1024]{1,0:T(8,128)(2,1)S(1)}, u32[]{:S(2)}, u32[]{:S(2)}) collective-permute-start(bf16[128,1024]{1,0:T(8,128)(2,1)S(1)} %get-tuple-element.251), channel_id=1, source_target_pairs={{0,2},{1,3},{2,0},{3,1},{4,6},{5,7},{6,4},{7,5},{8,10},{9,11},{10,... | collective-permute-start | bytes 786440 | tf_op jit(solution)/shard_map/ppermute | solution.py:862
  82.0 10.3 %collective-permute-start.42 = (bf16[128,1024]{1,0:T(8,128)(2,1)S(1)}, bf16[128,1024]{1,0:T(8,128)(2,1)S(1)}, u32[]{:S(2)}, u32[]{:S(2)}) collective-permute-start(bf16[128,1024]{1,0:T(8,128)(2,1)S(1)} %get-tuple-element.259), channel_id=1, source_target_pairs={{0,2},{1,3},{2,0},{3,1},{4,6},{5,7},{6,4},{7,5},{8,10},{9,11},{10,... | collective-permute-start | bytes 786440 | tf_op jit(solution)/shard_map/ppermute | solution.py:862
  82.6 24.8 %collective-permute-start.49 = (bf16[256,1024]{1,0:T(8,128)(2,1)S(1)}, bf16[256,1024]{1,0:T(8,128)(2,1)S(1)}, u32[]{:S(2)}, u32[]{:S(2)}) collective-permute-start(bf16[256,1024]{1,0:T(8,128)(2,1)S(1)} %get-tuple-element.273), channel_id=1, source_target_pairs={{0,8},{4,12},{8,0},{12,4},{16,24},{20,28},{24,16},{28,20},{1,9},{5... | collective-permute-start | bytes 1572872 | tf_op jit(solution)/shard_map/ppermute | solution.py:865
  83.8 30.8 %collective-permute-start.51 = (bf16[256,1024]{1,0:T(8,128)(2,1)S(1)}, bf16[256,1024]{1,0:T(8,128)(2,1)S(1)}, u32[]{:S(2)}, u32[]{:S(2)}) collective-permute-start(bf16[256,1024]{1,0:T(8,128)(2,1)S(1)} %get-tuple-element.280), channel_id=1, source_target_pairs={{0,16},{4,20},{8,24},{12,28},{16,0},{20,4},{24,8},{28,12},{1,17},{... | collective-permute-start | bytes 1572872 | tf_op jit(solution)/shard_map/ppermute | solution.py:865
  88.0 4.8 %collective-permute-start.40 = (bf16[64,1024]{1,0:T(8,128)(2,1)S(1)}, bf16[64,1024]{1,0:T(8,128)(2,1)S(1)}, u32[]{:S(2)}, u32[]{:S(2)}) collective-permute-start(bf16[64,1024]{1,0:T(8,128)(2,1)S(1)} %get-tuple-element.257.refs_6_.refs_2_.refs_3_), channel_id=1, source_target_pairs={{0,1},{1,0},{2,3},{3,2},{4,5},{5,4},{6,7},{7,6},{8,9},{9,8},{10,11... | collective-permute-start | bytes 393224 | tf_op jit(solution)/shard_map/ppermute | solution.py:859
  94.4 13.2 %collective-permute-start.48 = (f32[8,1024]{1,0:T(8,128)S(1)}, f32[8,1024]{1,0:T(8,128)S(1)}, u32[]{:S(2)}, u32[]{:S(2)}) collective-permute-start(f32[8,1024]{1,0:T(8,128)S(1)} %get-tuple-element.272.refs_12_.refs_13_), channel_id=1, source_target_pairs={{0,1},{1,0},{2,3},{3,2},{4,5},{5,4},{6,7},{7,6},{8,9},{9,8},{10,11... | collective-permute-start | bytes 98312 | tf_op jit(solution)/shard_map/ppermute | solution.py:859
  96.7 13.8 %collective-permute-start.47 = (bf16[192,256]{1,0:T(8,128)(2,1)S(1)}, bf16[192,256]{1,0:T(8,128)(2,1)S(1)}, u32[]{:S(2)}, u32[]{:S(2)}) collective-permute-start(bf16[192,256]{1,0:T(8,128)(2,1)S(1)} %get-tuple-element.271), channel_id=1, source_target_pairs={{0,1},{1,0},{2,3},{3,2},{4,5},{5,4},{6,7},{7,6},{8,9},{9,8},{10,11... | collective-permute-start | bytes 294920 | tf_op jit(solution)/shard_map/ppermute | solution.py:859
  107.4 5.6 %collective-permute-start.45 = (bf16[272,256]{1,0:T(8,128)(2,1)S(1)}, bf16[272,256]{1,0:T(8,128)(2,1)S(1)}, u32[]{:S(2)}, u32[]{:S(2)}) collective-permute-start(bf16[272,256]{1,0:T(8,128)(2,1)S(1)} %get-tuple-element.269.refs_2_), channel_id=1, source_target_pairs={{0,8},{4,12},{8,0},{12,4},{16,24},{20,28},{24,16},{28,20},{1,9},{5... | collective-permute-start | bytes 417800 | tf_op jit(solution)/shard_map/ppermute | solution.py:865
  109.0 26.0 %collective-permute-start.60 = (bf16[512,512]{1,0:T(8,128)(2,1)S(1)}, bf16[512,512]{1,0:T(8,128)(2,1)S(1)}, u32[]{:S(2)}, u32[]{:S(2)}) collective-permute-start(bf16[512,512]{1,0:T(8,128)(2,1)S(1)} %mix_1.1.refs_2_), channel_id=1, source_target_pairs={{0,4},{4,0},{8,12},{12,8},{16,20},{20,16},{24,28},{28,24},{1,5},{5... | collective-permute-start | bytes 1572872 | tf_op jit(solution)/shard_map/ppermute | solution.py:865
  111.6 24.3 %collective-permute-start.59 = (bf16[256,1024]{1,0:T(8,128)(2,1)S(1)}, bf16[256,1024]{1,0:T(8,128)(2,1)S(1)}, u32[]{:S(2)}, u32[]{:S(2)}) collective-permute-start(bf16[256,1024]{1,0:T(8,128)(2,1)S(1)} %get-tuple-element.295), channel_id=1, source_target_pairs={{0,8},{4,12},{8,0},{12,4},{16,24},{20,28},{24,16},{28,20},{1,9},{5... | collective-permute-start | bytes 1572872 | tf_op jit(solution)/shard_map/ppermute | solution.py:865
  113.0 15.3 %collective-permute-start.57 = (bf16[128,1024]{1,0:T(8,128)(2,1)S(1)}, bf16[128,1024]{1,0:T(8,128)(2,1)S(1)}, u32[]{:S(2)}, u32[]{:S(2)}) collective-permute-start(bf16[128,1024]{1,0:T(8,128)(2,1)S(1)} %get-tuple-element.290), channel_id=1, source_target_pairs={{0,16},{4,20},{8,24},{12,28},{16,0},{20,4},{24,8},{28,12},{1,17},{... | collective-permute-start | bytes 786440 | tf_op jit(solution)/shard_map/ppermute | solution.py:865
  113.0 13.9 %collective-permute-start.50 = (bf16[272,256]{1,0:T(8,128)(2,1)S(1)}, bf16[272,256]{1,0:T(8,128)(2,1)S(1)}, u32[]{:S(2)}, u32[]{:S(2)}) collective-permute-start(bf16[272,256]{1,0:T(8,128)(2,1)S(1)} %get-tuple-element.279.refs_2_), channel_id=1, source_target_pairs={{0,4},{4,0},{8,12},{12,8},{16,20},{20,16},{24,28},{28,24},{1,5},{5... | collective-permute-start | bytes 417800 | tf_op jit(solution)/shard_map/ppermute | solution.py:865
  114.9 15.5 %collective-permute-start.56 = (bf16[128,1024]{1,0:T(8,128)(2,1)S(1)}, bf16[128,1024]{1,0:T(8,128)(2,1)S(1)}, u32[]{:S(2)}, u32[]{:S(2)}) collective-permute-start(bf16[128,1024]{1,0:T(8,128)(2,1)S(1)} %get-tuple-element.289), channel_id=1, source_target_pairs={{0,4},{4,0},{8,12},{12,8},{16,20},{20,16},{24,28},{28,24},{1,5},{5... | collective-permute-start | bytes 786440 | tf_op jit(solution)/shard_map/ppermute | solution.py:865
  130.3 4.5 %collective-permute-start.54 = (bf16[64,1024]{1,0:T(8,128)(2,1)S(1)}, bf16[64,1024]{1,0:T(8,128)(2,1)S(1)}, u32[]{:S(2)}, u32[]{:S(2)}) collective-permute-start(bf16[64,1024]{1,0:T(8,128)(2,1)S(1)} %get-tuple-element.287), channel_id=1, source_target_pairs={{0,1},{1,0},{2,3},{3,2},{4,5},{5,4},{6,7},{7,6},{8,9},{9,8},{10,11... | collective-permute-start | bytes 393224 | tf_op jit(solution)/shard_map/ppermute | solution.py:859
  130.9 10.2 %collective-permute-start.63 = (bf16[272,256]{1,0:T(8,128)(2,1)S(1)}, bf16[272,256]{1,0:T(8,128)(2,1)S(1)}, u32[]{:S(2)}, u32[]{:S(2)}) collective-permute-start(bf16[272,256]{1,0:T(8,128)(2,1)S(1)} %get-tuple-element.282.refs_3_), channel_id=1, source_target_pairs={{0,16},{4,20},{8,24},{12,28},{16,0},{20,4},{24,8},{28,12},{1,17},{... | collective-permute-start | bytes 417800 | tf_op jit(solution)/shard_map/ppermute | solution.py:865
  135.9 14.0 %collective-permute-start.62 = (bf16[256,512]{1,0:T(8,128)(2,1)S(1)}, bf16[256,512]{1,0:T(8,128)(2,1)S(1)}, u32[]{:S(2)}, u32[]{:S(2)}) collective-permute-start(bf16[256,512]{1,0:T(8,128)(2,1)S(1)} %get-tuple-element.299), channel_id=1, source_target_pairs={{0,8},{4,12},{8,0},{12,4},{16,24},{20,28},{24,16},{28,20},{1,9},{5... | collective-permute-start | bytes 786440 | tf_op jit(solution)/shard_map/ppermute | solution.py:865
  136.1 15.5 %collective-permute-start.61 = (bf16[128,1024]{1,0:T(8,128)(2,1)S(1)}, bf16[128,1024]{1,0:T(8,128)(2,1)S(1)}, u32[]{:S(2)}, u32[]{:S(2)}) collective-permute-start(bf16[128,1024]{1,0:T(8,128)(2,1)S(1)} %get-tuple-element.298), channel_id=1, source_target_pairs={{0,16},{4,20},{8,24},{12,28},{16,0},{20,4},{24,8},{28,12},{1,17},{... | collective-permute-start | bytes 786440 | tf_op jit(solution)/shard_map/ppermute | solution.py:865
  138.0 14.5 %collective-permute-start.58 = (bf16[128,1024]{1,0:T(8,128)(2,1)S(1)}, bf16[128,1024]{1,0:T(8,128)(2,1)S(1)}, u32[]{:S(2)}, u32[]{:S(2)}) collective-permute-start(bf16[128,1024]{1,0:T(8,128)(2,1)S(1)} %get-tuple-element.294), channel_id=1, source_target_pairs={{0,2},{1,3},{2,0},{3,1},{4,6},{5,7},{6,4},{7,5},{8,10},{9,11},{10,... | collective-permute-start | bytes 786440 | tf_op jit(solution)/shard_map/ppermute | solution.py:862
  142.7 4.7 %collective-permute-start.64 = (f32[64,256]{1,0:T(8,128)S(1)}, f32[64,256]{1,0:T(8,128)S(1)}, u32[]{:S(2)}, u32[]{:S(2)}) collective-permute-start(f32[64,256]{1,0:T(8,128)S(1)} %get-tuple-element.305), channel_id=1, source_target_pairs={{0,2},{1,3},{2,0},{3,1},{4,6},{5,7},{6,4},{7,5},{8,10},{9,11},{10,... | collective-permute-start | bytes 196616 | tf_op jit(solution)/shard_map/ppermute | solution.py:862
  144.0 9.4 %collective-permute-start.65 = (bf16[192,128]{1,0:T(8,128)(2,1)S(1)}, bf16[192,128]{1,0:T(8,128)(2,1)S(1)}, u32[]{:S(2)}, u32[]{:S(2)}) collective-permute-start(bf16[192,128]{1,0:T(8,128)(2,1)S(1)} %get-tuple-element.310), channel_id=1, source_target_pairs={{0,2},{1,3},{2,0},{3,1},{4,6},{5,7},{6,4},{7,5},{8,10},{9,11},{10,... | collective-permute-start | bytes 147464 | tf_op jit(solution)/shard_map/ppermute | solution.py:862
  147.4 6.6 %collective-permute-start.66 = (f32[32,256]{1,0:T(8,128)S(1)}, f32[32,256]{1,0:T(8,128)S(1)}, u32[]{:S(2)}, u32[]{:S(2)}) collective-permute-start(f32[32,256]{1,0:T(8,128)S(1)} %get-tuple-element.313), channel_id=1, source_target_pairs={{0,1},{1,0},{2,3},{3,2},{4,5},{5,4},{6,7},{7,6},{8,9},{9,8},{10,11... | collective-permute-start | bytes 98312 | tf_op jit(solution)/shard_map/ppermute | solution.py:859
  150.0 8.2 %collective-permute-start.67 = (bf16[128,512]{1,0:T(8,128)(2,1)S(1)}, bf16[128,512]{1,0:T(8,128)(2,1)S(1)}, u32[]{:S(2)}, u32[]{:S(2)}) collective-permute-start(bf16[128,512]{1,0:T(8,128)(2,1)S(1)} %get-tuple-element.319), channel_id=1, source_target_pairs={{0,16},{4,20},{8,24},{12,28},{16,0},{20,4},{24,8},{28,12},{1,17},{... | collective-permute-start | bytes 393224 | tf_op jit(solution)/shard_map/ppermute | solution.py:865
  (61 other events, 220.1 us)

commit v2 on v1

--- a/solution.py
+++ b/solution.py
@@ -25,11 +25,11 @@
 AXES = ((0, 1, 2), (1, 2, 0), (0, 1, 2), (0, 1, 2), (1, 0, 2))
 ORDER = (
     "mix_a", "mix_b", "first_a", "first_b", "base", "norm_a", "proj", "norm_b", "attend_a", "second_a", "cot",
-    "attend_b", "hidden_a", "second_b", "two_a", "mlp_a", "hidden_b", "two_b", "third_a", "mlp_b", "down_1",
+    "attend_b", "hidden_a", "second_b", "two_a", "mlp_a", "two_b", "hidden_b", "third_a", "mlp_b", "down_1",
     "up_1", "third_b", "mid_a", "back_a", "mid_b", "back_b", "attn_1", "back_c", "fourth_a", "down_2",
-    "weights", "fourth_b", "up_2", "in_a", "in_b", "mass_1", "down_3", "mix_1", "field_1", "attn_2", "mass_2",
-    "up_3", "mass_3", "rows_1", "down_4", "up_4", "rows_2", "mix_2", "attn_3", "finish", "tables_1", "mix_3",
-    "attn_4", "rows_3", "field_2", "tables_2", "mix_4",
+    "weights", "fourth_b", "up_2", "in_a", "in_b", "mix_1", "mass_1", "down_3", "attn_2", "mass_2", "up_3",
+    "field_1", "mass_3", "rows_1", "down_4", "up_4", "rows_2", "mix_2", "attn_3", "finish", "tables_1",
+    "mix_3", "attn_4", "rows_3", "field_2", "tables_2", "mix_4",
 )
 COSTS = {
     "two_a": 1,
@@ -37,10 +37,11 @@
     "mlp_b": 12,
     "mid_a": 1,
     "up_2": 1,
-    "in_a": 1,
+    "in_a": 0.5,
     "down_3": 2,
     "up_3": 1,
     "tables_1": 1,
+    "weights": 5,
 }
 
 
@@ -84,7 +85,7 @@
     return out, counts
 
 
-def launch(kernel, outs, args, fetch=(), smem=(), after=(), limit=24, scratch=(), cost=0.1, name=None):
+def launch(kernel, outs, args, fetch=(), smem=(), after=(), limit=24, scratch=(), cost=0.1, name=None, lazy=False):
     fetch = [item if isinstance(item, tuple) else (item, item.shape, None) for item in fetch]
     args, arg_counts = flat(args)
     outs, out_counts = flat(outs)
@@ -106,11 +107,17 @@
             copies.append(pltpu.make_async_copy(source, places[i], marks.at[i]))
         for copy in copies:
             copy.start()
+        if lazy:
+            kernel([copy.wait for copy in copies], *refs[:count], *places, *inputs, *results, *rest)
+            return
         for copy in copies:
             copy.wait()
         kernel(*refs[:count], *places, *inputs, *results, *rest)
 
-    places = [pltpu.VMEM(shape, array.dtype) for array, shape, _ in fetch]
+    places = [
+        (pltpu.SMEM if array.dtype == jnp.int32 else pltpu.VMEM)(shape, array.dtype)
+        for array, shape, _ in fetch
+    ]
     marks = [pltpu.SemaphoreType.DMA((len(fetch),))] if fetch else []
     results = pl.pallas_call(
         run,
@@ -195,6 +202,7 @@
 def mix_forward(
     pixels,
     quarter,
+    waits,
     ids_ref,
     x_ref,
     patch_ref,
@@ -216,12 +224,17 @@
     width = w_ref.shape[2]
     heads = width // HEAD_DIM
     bottom = rows - channels - variables
+    wait_ids, wait_field, wait_patch, wait_variable, wait_weights, wait_query = waits
+    wait_patch()
     flat = patch_ref[...].reshape(channels, model_width)
     table_ref[0:channels] = dot(pixel_major(channels, pixels), flat).astype(BF16)
+    wait_variable()
     table_ref[channels : channels + variables] = variable_ref[...]
     if bottom:
         table_ref[channels + variables :] = jnp.zeros((bottom, model_width), BF16)
+    wait_ids()
     pick = (iota((channels, channels), 0) == places(ids_ref, variables, pixels)).astype(F32)
+    wait_field()
     core = my_core()
     starts = [core, 1 - core, core + 2, 3 - core]
     field = jnp.concatenate(
@@ -229,6 +242,8 @@
     )
     xt = dot(pick.astype(BF16), field)
     xt_ref[...] = xt.astype(BF16)
+    wait_weights()
+    wait_query()
     query_rows = jnp.broadcast_to(query_ref[...].astype(F32)[None], (16, model_width)).astype(BF16)
     query = dot(query_rows, w_ref[0])[0:1].astype(BF16).astype(F32)
     table = table_ref[...]
@@ -961,10 +976,10 @@
                 ((padded, LANES), F32),
                 ((head_width, LANES), F32),
             ],
-            [variable_query],
-            fetch=[input_field, patch_table, variable_table, w_mix],
-            smem=[variable_ids],
+            [],
+            fetch=[variable_ids, input_field, patch_table, variable_table, w_mix, variable_query],
             limit=FIRST_LIMIT,
+            lazy=True,
             scratch=[pltpu.VMEM((padded, model_width), BF16)],
         )
 

time: 160 us -> 155 us (0.969)
  waiting for transfers between devices: 65.1 us -> 52.5 us
  starting transfers between devices: 42.7 us -> 52.4 us
    ppermute x15, waiting for transfers between devices: 32.1 us -> 21.8 us  [swap_sample(): return lax.ppermute(value, 'dp', pairs(mesh_dp, bit))]
    ppermute x15, starting transfers between devices: 16.3 us -> 26.4 us  [swap_sample(): return lax.ppermute(value, 'dp', pairs(mesh_dp, bit))]
    ppermute x12, waiting for transfers between devices: 23.6 us -> 21.9 us  [swap_chip(): return lax.ppermute(value, 'mp', pairs(mesh_mp, 2))]
  transfers between devices with their start and end apart: 68 -> 68, of which waited for: 36 -> 41; matrix products, arithmetic and copies ran while one was open for 0% -> 0% of each run, Pallas kernels for 23% -> 24%
where the time goes in v2:
time: 155 us
  waiting for transfers between devices  52.5 us (34%)
  starting transfers between devices  52.4 us (34%)
  Pallas kernels  45.5 us (29%)
  between operations  2.24 us (1%)
  local copies, waits for them, and re-layouts  2.21 us (1%)
    pallas_call x58, Pallas kernels, launch(): pl.pallas_call(run, out_shape=[jax.ShapeDtypeStruct(shape, kind) for shap...  45.5 us
    ppermute x15, starting transfers between devices, swap_sample(): return lax.ppermute(value, 'dp', pairs(mesh_dp, bit))  26.4 us
    ppermute x12, waiting for transfers between devices, swap_chip(): return lax.ppermute(value, 'mp', pairs(mesh_mp, 2))  21.9 us
    ppermute x15, waiting for transfers between devices, swap_sample(): return lax.ppermute(value, 'dp', pairs(mesh_dp, bit))  21.8 us
    ppermute x12, starting transfers between devices, swap_chip(): return lax.ppermute(value, 'mp', pairs(mesh_mp, 2))  15.7 us
    ppermute x41, starting transfers between devices, swap_core(): return lax.ppermute(value, 'mp', pairs(mesh_mp, 1))  10.2 us
    ppermute x41, waiting for transfers between devices, swap_core(): return lax.ppermute(value, 'mp', pairs(mesh_mp, 1))  8.75 us
  transfers between devices with their start and end apart: 68, of which 41 were waited for; matrix products, arithmetic and copies ran while one was open for 0% of the time, Pallas kernels for 24%

profile of v2, /device:TPU:0, one launch (start us, length us, event | category | flops | bytes accessed | tf_op | source)
XLA Modules:
  0.0 154.8 jit_solution(8831095044526600309)
XLA Ops:
  0.7 4.0 %mix_a.1 = (bf16[256,512]{1,0:T(8,128)(2,1)}, bf16[192,512]{1,0:T(8,128)(2,1)}, f32[192,512]{1,0:T(8,128)}, bf16[256,256]{1,0:T(8,128)(2,1)}, f32[256,256]{1,0:T...) custom-call(s32[48]{0:T(128)} %refs_0_.8, bf16[1,192,512]{2,1,0:T(8,128)(2,1)} %refs_1_.3, bf16[48,4,1024]{2,1,0:T(4,128)(2,1)} %refs_2_.9, ...), custom_call_target="tpu_custom_call" | custom-call | flops 100000000 | tf_op jit(solution)/shard_map/mix_a/pallas_call | solution.py:122
  8.1 3.0 %collective-permute-start.3 = (bf16[128,1024]{1,0:T(8,128)(2,1)S(1)}, bf16[128,1024]{1,0:T(8,128)(2,1)S(1)}, u32[]{:S(2)}, u32[]{:S(2)}) collective-permute-start(bf16[128,1024]{1,0:T(8,128)(2,1)S(1)} %get-tuple-element.182), channel_id=1, source_target_pairs={{0,2},{1,3},{2,0},{3,1},{4,6},{5,7},{6,4},{7,5},{8,10},{9,11},{10,... | collective-permute-start | bytes 786440 | tf_op jit(solution)/shard_map/ppermute | solution.py:877
  12.9 5.2 %collective-permute-done.3.refs_1_ = bf16[128,1024]{1,0:T(8,128)(2,1)S(1)} collective-permute-done((bf16[128,1024]{1,0:T(8,128)(2,1)S(1)}, bf16[128,1024]{1,0:T(8,128)(2,1)S(1)}, u32[]{:S(2)}, u32[]{:S(2)}) %collective-permute-start.3) | collective-permute-done | bytes 262176 | tf_op jit(solution)/shard_map/ppermute | solution.py:877
  20.6 2.7 %collective-permute-done.2.refs_2_ = bf16[128,1024]{1,0:T(8,128)(2,1)S(1)} collective-permute-done((bf16[128,1024]{1,0:T(8,128)(2,1)S(1)}, bf16[128,1024]{1,0:T(8,128)(2,1)S(1)}, u32[]{:S(2)}, u32[]{:S(2)}) %collective-permute-start.2) | collective-permute-done | bytes 262176 | tf_op jit(solution)/shard_map/ppermute | solution.py:877
  24.1 1.7 %collective-permute-start.11 = (bf16[128,1024]{1,0:T(8,128)(2,1)S(1)}, bf16[128,1024]{1,0:T(8,128)(2,1)S(1)}, u32[]{:S(2)}, u32[]{:S(2)}) collective-permute-start(bf16[128,1024]{1,0:T(8,128)(2,1)S(1)} %get-tuple-element.196.refs_0_), channel_id=1, source_target_pairs={{0,2},{1,3},{2,0},{3,1},{4,6},{5,7},{6,4},{7,5},{8,10},{9,11},{10,... | collective-permute-start | bytes 786440 | tf_op jit(solution)/shard_map/ppermute | solution.py:877
  25.9 2.8 %attend_a.1 = (bf16[3,256,256]{2,1,0:T(8,128)(2,1)S(1)}, bf16[256,256]{1,0:T(8,128)(2,1)S(1)}, f32[8,256]{1,0:T(8,128)S(1)}, f32[128,1024]{1,0:T(8,128)S(1)}, bf...) custom-call(bf16[64,1024]{1,0:T(8,128)(2,1)S(1)} %get-tuple-element.187.refs_0_.refs_4_.refs_5_, ...), custom_call_target="tpu_custom_call" | custom-call | flops 100000000 | tf_op jit(solution)/shard_map/attend_a/pallas_call | solution.py:122
  33.0 2.2 %attend_b.1 = (bf16[256,256]{1,0:T(8,128)(2,1)S(1)}, f32[8,256]{1,0:T(8,128)S(1)}, f32[128,1024]{1,0:T(8,128)S(1)}, bf16[64,1024]{1,0:T(8,128)(2,1)S(1)}, bf16[64,1024]{1,0:T(8,128)(2,1)S(1)}) custom-call(bf16[3,256,256]{2,1,0:T(8,128)(2,1)S(1)} %proj.1.refs_6_.refs_5_.refs_0_, bf16[3,256,256]{2,1,0:T(8,128)(2,1)S(1)} %get-tuple-element.193.refs_3_.refs_1_.refs_6_, ...), custom_call_target="tpu_custom_call" | custom-call | flops 100000000 | tf_op jit(solution)/shard_map/attend_b/pallas_call | solution.py:122
  36.9 1.8 %collective-permute-start.18 = (bf16[128,1024]{1,0:T(8,128)(2,1)S(1)}, bf16[128,1024]{1,0:T(8,128)(2,1)S(1)}, u32[]{:S(2)}, u32[]{:S(2)}) collective-permute-start(bf16[128,1024]{1,0:T(8,128)(2,1)S(1)} %get-tuple-element.208), channel_id=1, source_target_pairs={{0,2},{1,3},{2,0},{3,1},{4,6},{5,7},{6,4},{7,5},{8,10},{9,11},{10,... | collective-permute-start | bytes 786440 | tf_op jit(solution)/shard_map/ppermute | solution.py:877
  40.8 1.9 %mlp_a.1 = (bf16[256,1024]{1,0:T(8,128)(2,1)S(1)}, bf16[256,1024]{1,0:T(8,128)(2,1)S(1)}, f32[128,1024]{1,0:T(8,128)S(1)}, bf16[64,1024]{1,0:T(8,128)(2,1)S(1)}, bf16[64,1024]{1,0:T(8,128)(2,1)S(1)}) custom-call(bf16[64,1024]{1,0:T(8,128)(2,1)S(1)} %get-tuple-element.204.refs_0_.refs_1_, bf16[64,1024]{1,0:T(8,128)(2,1)S(1)} %get-tuple-element.205.refs_1_.refs_2_, ...), custom_call_target="tpu_custom_call" | custom-call | flops 100000000 | tf_op jit(solution)/shard_map/mlp_a/pallas_call | solution.py:122
  43.3 2.2 %collective-permute-done.18.refs_1_ = bf16[128,1024]{1,0:T(8,128)(2,1)S(1)} collective-permute-done((bf16[128,1024]{1,0:T(8,128)(2,1)S(1)}, bf16[128,1024]{1,0:T(8,128)(2,1)S(1)}, u32[]{:S(2)}, u32[]{:S(2)}) %collective-permute-start.18) | collective-permute-done | bytes 262176 | tf_op jit(solution)/shard_map/ppermute | solution.py:877
  47.4 1.9 %mlp_b.1 = (bf16[256,1024]{1,0:T(8,128)(2,1)S(1)}, bf16[256,1024]{1,0:T(8,128)(2,1)S(1)}, f32[128,1024]{1,0:T(8,128)S(1)}, bf16[64,1024]{1,0:T(8,128)(2,1)S(1)}, bf16[64,1024]{1,0:T(8,128)(2,1)S(1)}) custom-call(bf16[64,1024]{1,0:T(8,128)(2,1)S(1)} %get-tuple-element.209.refs_0_.refs_4_.refs_5_, ...), custom_call_target="tpu_custom_call" | custom-call | flops 12000000000 | tf_op jit(solution)/shard_map/mlp_b/pallas_call | solution.py:122
  50.0 1.8 %collective-permute-start.25 = (bf16[512,1024]{1,0:T(8,128)(2,1)S(1)}, bf16[512,1024]{1,0:T(8,128)(2,1)S(1)}, u32[]{:S(2)}, u32[]{:S(2)}) collective-permute-start(bf16[512,1024]{1,0:T(8,128)(2,1)S(1)} %down_1.1.refs_10_), channel_id=1, source_target_pairs={{0,4},{4,0},{8,12},{12,8},{16,20},{20,16},{24,28},{28,24},{1,5},{5... | collective-permute-start | bytes 3145736 | tf_op jit(solution)/shard_map/ppermute | solution.py:880
  57.1 3.9 %collective-permute-done.29.refs_1_ = bf16[128,1024]{1,0:T(8,128)(2,1)S(1)} collective-permute-done((bf16[128,1024]{1,0:T(8,128)(2,1)S(1)}, bf16[128,1024]{1,0:T(8,128)(2,1)S(1)}, u32[]{:S(2)}, u32[]{:S(2)}) %collective-permute-start.29) | collective-permute-done | bytes 262176 | tf_op jit(solution)/shard_map/ppermute | solution.py:877
  63.1 2.8 %back_a.1 = (bf16[256,256]{1,0:T(8,128)(2,1)S(1)}, f32[512,256]{1,0:T(8,128)S(1)}, f32[512,256]{1,0:T(8,128)S(1)}) custom-call(bf16[64,1024]{1,0:T(8,128)(2,1)S(1)} %get-tuple-element.227.refs_0_.refs_8_.refs_9_, bf16[64,1024]{1,0:T(8,128)(2,1)S(1)} %get-tuple-element.228.refs_1_.refs_9_.refs_10_, ...), custom_call_target="tpu_custom_call" | custom-call | flops 100000000 | tf_op jit(solution)/shard_map/back_a/pallas_call | solution.py:122
  68.2 3.2 %back_b.1 = (bf16[3,512,256]{2,1,0:T(8,128)(2,1)S(1)}, f32[128,1024]{1,0:T(8,128)S(1)}, bf16[64,1024]{1,0:T(8,128)(2,1)S(1)}, bf16[64,1024]{1,0:T(8,128)(2,1)S(1)}) custom-call(bf16[64,1024]{1,0:T(8,128)(2,1)S(1)} %get-tuple-element.232.refs_0_.refs_12_.refs_13_, bf16[64,1024]{1,0:T(8,128)(2,1)S(1)} %get-tuple-element.233.refs_1_.refs_13_.refs_14_, ...), custom_call_target="tpu_custom_call" | custom-call | flops 100000000 | tf_op jit(solution)/shard_map/back_b/pallas_call | solution.py:122
  75.5 1.8 %collective-permute-start.36 = (bf16[128,1024]{1,0:T(8,128)(2,1)S(1)}, bf16[128,1024]{1,0:T(8,128)(2,1)S(1)}, u32[]{:S(2)}, u32[]{:S(2)}) collective-permute-start(bf16[128,1024]{1,0:T(8,128)(2,1)S(1)} %get-tuple-element.251), channel_id=1, source_target_pairs={{0,2},{1,3},{2,0},{3,1},{4,6},{5,7},{6,4},{7,5},{8,10},{9,11},{10,... | collective-permute-start | bytes 786440 | tf_op jit(solution)/shard_map/ppermute | solution.py:877
  79.8 1.9 %collective-permute-start.48 = (bf16[256,1024]{1,0:T(8,128)(2,1)S(1)}, bf16[256,1024]{1,0:T(8,128)(2,1)S(1)}, u32[]{:S(2)}, u32[]{:S(2)}) collective-permute-start(bf16[256,1024]{1,0:T(8,128)(2,1)S(1)} %get-tuple-element.271), channel_id=1, source_target_pairs={{0,8},{4,12},{8,0},{12,4},{16,24},{20,28},{24,16},{28,20},{1,9},{5... | collective-permute-start | bytes 1572872 | tf_op jit(solution)/shard_map/ppermute | solution.py:880
  82.6 2.1 %collective-permute-done.36.refs_1_ = bf16[128,1024]{1,0:T(8,128)(2,1)S(1)} collective-permute-done((bf16[128,1024]{1,0:T(8,128)(2,1)S(1)}, bf16[128,1024]{1,0:T(8,128)(2,1)S(1)}, u32[]{:S(2)}, u32[]{:S(2)}) %collective-permute-start.36) | collective-permute-done | bytes 262176 | tf_op jit(solution)/shard_map/ppermute | solution.py:877
  85.3 3.0 %collective-permute-start.51 = (bf16[256,1024]{1,0:T(8,128)(2,1)S(1)}, bf16[256,1024]{1,0:T(8,128)(2,1)S(1)}, u32[]{:S(2)}, u32[]{:S(2)}) collective-permute-start(bf16[256,1024]{1,0:T(8,128)(2,1)S(1)} %get-tuple-element.279), channel_id=1, source_target_pairs={{0,16},{4,20},{8,24},{12,28},{16,0},{20,4},{24,8},{28,12},{1,17},{... | collective-permute-start | bytes 1572872 | tf_op jit(solution)/shard_map/ppermute | solution.py:880
  92.9 1.8 %collective-permute-start.60 = (bf16[512,512]{1,0:T(8,128)(2,1)S(1)}, bf16[512,512]{1,0:T(8,128)(2,1)S(1)}, u32[]{:S(2)}, u32[]{:S(2)}) collective-permute-start(bf16[512,512]{1,0:T(8,128)(2,1)S(1)} %mix_1.1.refs_14_), channel_id=1, source_target_pairs={{0,4},{4,0},{8,12},{12,8},{16,20},{20,16},{24,28},{28,24},{1,5},{5... | collective-permute-start | bytes 1572872 | tf_op jit(solution)/shard_map/ppermute | solution.py:880
  96.3 1.6 %collective-permute-start.46 = (bf16[272,256]{1,0:T(8,128)(2,1)S(1)}, bf16[272,256]{1,0:T(8,128)(2,1)S(1)}, u32[]{:S(2)}, u32[]{:S(2)}) collective-permute-start(bf16[272,256]{1,0:T(8,128)(2,1)S(1)} %get-tuple-element.270.refs_2_), channel_id=1, source_target_pairs={{0,8},{4,12},{8,0},{12,4},{16,24},{20,28},{24,16},{28,20},{1,9},{5... | collective-permute-start | bytes 417800 | tf_op jit(solution)/shard_map/ppermute | solution.py:880
  99.8 1.6 %collective-permute-start.59 = (bf16[256,1024]{1,0:T(8,128)(2,1)S(1)}, bf16[256,1024]{1,0:T(8,128)(2,1)S(1)}, u32[]{:S(2)}, u32[]{:S(2)}) collective-permute-start(bf16[256,1024]{1,0:T(8,128)(2,1)S(1)} %get-tuple-element.295), channel_id=1, source_target_pairs={{0,8},{4,12},{8,0},{12,4},{16,24},{20,28},{24,16},{28,20},{1,9},{5... | collective-permute-start | bytes 1572872 | tf_op jit(solution)/shard_map/ppermute | solution.py:880
  101.4 6.9 %collective-permute-done.46.refs_2_ = bf16[272,256]{1,0:T(8,128)(2,1)S(1)} collective-permute-done((bf16[272,256]{1,0:T(8,128)(2,1)S(1)}, bf16[272,256]{1,0:T(8,128)(2,1)S(1)}, u32[]{:S(2)}, u32[]{:S(2)}) %collective-permute-start.46) | collective-permute-done | bytes 139296 | tf_op jit(solution)/shard_map/ppermute | solution.py:880
  108.3 3.5 %collective-permute-start.57 = (bf16[128,1024]{1,0:T(8,128)(2,1)S(1)}, bf16[128,1024]{1,0:T(8,128)(2,1)S(1)}, u32[]{:S(2)}, u32[]{:S(2)}) collective-permute-start(bf16[128,1024]{1,0:T(8,128)(2,1)S(1)} %get-tuple-element.290), channel_id=1, source_target_pairs={{0,16},{4,20},{8,24},{12,28},{16,0},{20,4},{24,8},{28,12},{1,17},{... | collective-permute-start | bytes 786440 | tf_op jit(solution)/shard_map/ppermute | solution.py:880
  112.5 2.2 %collective-permute-start.49 = (bf16[272,256]{1,0:T(8,128)(2,1)S(1)}, bf16[272,256]{1,0:T(8,128)(2,1)S(1)}, u32[]{:S(2)}, u32[]{:S(2)}) collective-permute-start(bf16[272,256]{1,0:T(8,128)(2,1)S(1)} %get-tuple-element.276.refs_2_), channel_id=1, source_target_pairs={{0,4},{4,0},{8,12},{12,8},{16,20},{20,16},{24,28},{28,24},{1,5},{5... | collective-permute-start | bytes 417800 | tf_op jit(solution)/shard_map/ppermute | solution.py:880
  115.0 4.0 %collective-permute-done.49.refs_2_ = bf16[272,256]{1,0:T(8,128)(2,1)S(1)} collective-permute-done((bf16[272,256]{1,0:T(8,128)(2,1)S(1)}, bf16[272,256]{1,0:T(8,128)(2,1)S(1)}, u32[]{:S(2)}, u32[]{:S(2)}) %collective-permute-start.49) | collective-permute-done | bytes 139296 | tf_op jit(solution)/shard_map/ppermute | solution.py:880
  120.4 2.6 %collective-permute-done.57.refs_1_ = bf16[128,1024]{1,0:T(8,128)(2,1)S(1)} collective-permute-done((bf16[128,1024]{1,0:T(8,128)(2,1)S(1)}, bf16[128,1024]{1,0:T(8,128)(2,1)S(1)}, u32[]{:S(2)}, u32[]{:S(2)}) %collective-permute-start.57) | collective-permute-done | bytes 262176 | tf_op jit(solution)/shard_map/ppermute | solution.py:880
  124.4 3.4 %collective-permute-start.63 = (bf16[272,256]{1,0:T(8,128)(2,1)S(1)}, bf16[272,256]{1,0:T(8,128)(2,1)S(1)}, u32[]{:S(2)}, u32[]{:S(2)}) collective-permute-start(bf16[272,256]{1,0:T(8,128)(2,1)S(1)} %get-tuple-element.282.refs_3_), channel_id=1, source_target_pairs={{0,16},{4,20},{8,24},{12,28},{16,0},{20,4},{24,8},{28,12},{1,17},{... | collective-permute-start | bytes 417800 | tf_op jit(solution)/shard_map/ppermute | solution.py:880
  131.3 2.7 %collective-permute-start.61 = (bf16[128,1024]{1,0:T(8,128)(2,1)S(1)}, bf16[128,1024]{1,0:T(8,128)(2,1)S(1)}, u32[]{:S(2)}, u32[]{:S(2)}) collective-permute-start(bf16[128,1024]{1,0:T(8,128)(2,1)S(1)} %get-tuple-element.298), channel_id=1, source_target_pairs={{0,16},{4,20},{8,24},{12,28},{16,0},{20,4},{24,8},{28,12},{1,17},{... | collective-permute-start | bytes 786440 | tf_op jit(solution)/shard_map/ppermute | solution.py:880
  135.6 1.7 %finish.1 = (f32[64,256]{1,0:T(8,128)S(1)}, f32[64,256]{1,0:T(8,128)S(1)}, f32[3,128,256]{2,1,0:T(8,128)}) custom-call(f32[256,128]{1,0:T(8,128)S(1)} %copy-done.15, f32[256,256]{1,0:T(8,128)S(1)} %copy-done.13, bf16[48,4,1024]{2,1,0:T(4,128)(2,1)S(1)} %copy-done.9, bf16[48,1024]{1,0:T(8,128)(2,1)S(1)} %copy-done.10, ...), custom_call_target="tpu_custom_call" | custom-call | flops 100000000 | tf_op jit(solution)/shard_map/finish/pallas_call | solution.py:122
  139.3 4.2 %collective-permute-done.64.refs_1_ = f32[64,256]{1,0:T(8,128)S(1)} collective-permute-done((f32[64,256]{1,0:T(8,128)S(1)}, f32[64,256]{1,0:T(8,128)S(1)}, u32[]{:S(2)}, u32[]{:S(2)}) %collective-permute-start.64) | collective-permute-done | bytes 65568 | tf_op jit(solution)/shard_map/ppermute | solution.py:877
  149.6 3.7 %collective-permute-done.67.refs_1_ = bf16[128,512]{1,0:T(8,128)(2,1)S(1)} collective-permute-done((bf16[128,512]{1,0:T(8,128)(2,1)S(1)}, bf16[128,512]{1,0:T(8,128)(2,1)S(1)}, u32[]{:S(2)}, u32[]{:S(2)}) %collective-permute-start.67) | collective-permute-done | bytes 131104 | tf_op jit(solution)/shard_map/ppermute | solution.py:880
  (214 shorter events, 62.7 us)
Async XLA Ops:
  8.1 10.1 %collective-permute-start.3 = (bf16[128,1024]{1,0:T(8,128)(2,1)S(1)}, bf16[128,1024]{1,0:T(8,128)(2,1)S(1)}, u32[]{:S(2)}, u32[]{:S(2)}) collective-permute-start(bf16[128,1024]{1,0:T(8,128)(2,1)S(1)} %get-tuple-element.182), channel_id=1, source_target_pairs={{0,2},{1,3},{2,0},{3,1},{4,6},{5,7},{6,4},{7,5},{8,10},{9,11},{10,... | collective-permute-start | bytes 786440 | tf_op jit(solution)/shard_map/ppermute | solution.py:877
  11.1 12.1 %collective-permute-start.2 = (bf16[128,1024]{1,0:T(8,128)(2,1)S(1)}, bf16[128,1024]{1,0:T(8,128)(2,1)S(1)}, u32[]{:S(2)}, u32[]{:S(2)}) collective-permute-start(bf16[128,1024]{1,0:T(8,128)(2,1)S(1)} %get-tuple-element.180), channel_id=1, source_target_pairs={{0,2},{1,3},{2,0},{3,1},{4,6},{5,7},{6,4},{7,5},{8,10},{9,11},{10,... | collective-permute-start | bytes 786440 | tf_op jit(solution)/shard_map/ppermute | solution.py:877
  24.1 8.3 %collective-permute-start.11 = (bf16[128,1024]{1,0:T(8,128)(2,1)S(1)}, bf16[128,1024]{1,0:T(8,128)(2,1)S(1)}, u32[]{:S(2)}, u32[]{:S(2)}) collective-permute-start(bf16[128,1024]{1,0:T(8,128)(2,1)S(1)} %get-tuple-element.196.refs_0_), channel_id=1, source_target_pairs={{0,2},{1,3},{2,0},{3,1},{4,6},{5,7},{6,4},{7,5},{8,10},{9,11},{10,... | collective-permute-start | bytes 786440 | tf_op jit(solution)/shard_map/ppermute | solution.py:877
  30.4 8.6 %collective-permute-start.10 = (bf16[128,1024]{1,0:T(8,128)(2,1)S(1)}, bf16[128,1024]{1,0:T(8,128)(2,1)S(1)}, u32[]{:S(2)}, u32[]{:S(2)}) collective-permute-start(bf16[128,1024]{1,0:T(8,128)(2,1)S(1)} %get-tuple-element.195), channel_id=1, source_target_pairs={{0,2},{1,3},{2,0},{3,1},{4,6},{5,7},{6,4},{7,5},{8,10},{9,11},{10,... | collective-permute-start | bytes 786440 | tf_op jit(solution)/shard_map/ppermute | solution.py:877
  36.9 8.6 %collective-permute-start.18 = (bf16[128,1024]{1,0:T(8,128)(2,1)S(1)}, bf16[128,1024]{1,0:T(8,128)(2,1)S(1)}, u32[]{:S(2)}, u32[]{:S(2)}) collective-permute-start(bf16[128,1024]{1,0:T(8,128)(2,1)S(1)} %get-tuple-element.208), channel_id=1, source_target_pairs={{0,2},{1,3},{2,0},{3,1},{4,6},{5,7},{6,4},{7,5},{8,10},{9,11},{10,... | collective-permute-start | bytes 786440 | tf_op jit(solution)/shard_map/ppermute | solution.py:877
  39.8 6.1 %collective-permute-start.21 = (bf16[64,1024]{1,0:T(8,128)(2,1)S(1)}, bf16[64,1024]{1,0:T(8,128)(2,1)S(1)}, u32[]{:S(2)}, u32[]{:S(2)}) collective-permute-start(bf16[64,1024]{1,0:T(8,128)(2,1)S(1)} %get-tuple-element.211.refs_0_.refs_4_.refs_5_), channel_id=1, source_target_pairs={{0,1},{1,0},{2,3},{3,2},{4,5},{5,4},{6,7},{7,6},{8,9},{9,8},{10,11... | collective-permute-start | bytes 393224 | tf_op jit(solution)/shard_map/ppermute | solution.py:874
  39.9 6.5 %collective-permute-start.22 = (bf16[64,1024]{1,0:T(8,128)(2,1)S(1)}, bf16[64,1024]{1,0:T(8,128)(2,1)S(1)}, u32[]{:S(2)}, u32[]{:S(2)}) collective-permute-start(bf16[64,1024]{1,0:T(8,128)(2,1)S(1)} %get-tuple-element.212.refs_1_.refs_5_.refs_6_), channel_id=1, source_target_pairs={{0,1},{1,0},{2,3},{3,2},{4,5},{5,4},{6,7},{7,6},{8,9},{9,8},{10,11... | collective-permute-start | bytes 393224 | tf_op jit(solution)/shard_map/ppermute | solution.py:874
  50.0 25.4 %collective-permute-start.25 = (bf16[512,1024]{1,0:T(8,128)(2,1)S(1)}, bf16[512,1024]{1,0:T(8,128)(2,1)S(1)}, u32[]{:S(2)}, u32[]{:S(2)}) collective-permute-start(bf16[512,1024]{1,0:T(8,128)(2,1)S(1)} %down_1.1.refs_10_), channel_id=1, source_target_pairs={{0,4},{4,0},{8,12},{12,8},{16,20},{20,16},{24,28},{28,24},{1,5},{5... | collective-permute-start | bytes 3145736 | tf_op jit(solution)/shard_map/ppermute | solution.py:880
  51.8 9.2 %collective-permute-start.29 = (bf16[128,1024]{1,0:T(8,128)(2,1)S(1)}, bf16[128,1024]{1,0:T(8,128)(2,1)S(1)}, u32[]{:S(2)}, u32[]{:S(2)}) collective-permute-start(bf16[128,1024]{1,0:T(8,128)(2,1)S(1)} %get-tuple-element.226), channel_id=1, source_target_pairs={{0,2},{1,3},{2,0},{3,1},{4,6},{5,7},{6,4},{7,5},{8,10},{9,11},{10,... | collective-permute-start | bytes 786440 | tf_op jit(solution)/shard_map/ppermute | solution.py:877
  55.0 10.9 %collective-permute-start.28 = (bf16[128,1024]{1,0:T(8,128)(2,1)S(1)}, bf16[128,1024]{1,0:T(8,128)(2,1)S(1)}, u32[]{:S(2)}, u32[]{:S(2)}) collective-permute-start(bf16[128,1024]{1,0:T(8,128)(2,1)S(1)} %get-tuple-element.225), channel_id=1, source_target_pairs={{0,2},{1,3},{2,0},{3,1},{4,6},{5,7},{6,4},{7,5},{8,10},{9,11},{10,... | collective-permute-start | bytes 786440 | tf_op jit(solution)/shard_map/ppermute | solution.py:877
  55.5 26.1 %collective-permute-start.37 = (bf16[512,1024]{1,0:T(8,128)(2,1)S(1)}, bf16[512,1024]{1,0:T(8,128)(2,1)S(1)}, u32[]{:S(2)}, u32[]{:S(2)}) collective-permute-start(bf16[512,1024]{1,0:T(8,128)(2,1)S(1)} %up_1.1.refs_3_), channel_id=1, source_target_pairs={{0,8},{4,12},{8,0},{12,4},{16,24},{20,28},{24,16},{28,20},{1,9},{5... | collective-permute-start | bytes 3145736 | tf_op jit(solution)/shard_map/ppermute | solution.py:880
  72.7 26.1 %collective-permute-start.47 = (bf16[512,1024]{1,0:T(8,128)(2,1)S(1)}, bf16[512,1024]{1,0:T(8,128)(2,1)S(1)}, u32[]{:S(2)}, u32[]{:S(2)}) collective-permute-start(bf16[512,1024]{1,0:T(8,128)(2,1)S(1)} %attn_1.1.refs_2_), channel_id=1, source_target_pairs={{0,4},{4,0},{8,12},{12,8},{16,20},{20,16},{24,28},{28,24},{1,5},{5... | collective-permute-start | bytes 3145736 | tf_op jit(solution)/shard_map/ppermute | solution.py:880
  75.5 9.2 %collective-permute-start.36 = (bf16[128,1024]{1,0:T(8,128)(2,1)S(1)}, bf16[128,1024]{1,0:T(8,128)(2,1)S(1)}, u32[]{:S(2)}, u32[]{:S(2)}) collective-permute-start(bf16[128,1024]{1,0:T(8,128)(2,1)S(1)} %get-tuple-element.251), channel_id=1, source_target_pairs={{0,2},{1,3},{2,0},{3,1},{4,6},{5,7},{6,4},{7,5},{8,10},{9,11},{10,... | collective-permute-start | bytes 786440 | tf_op jit(solution)/shard_map/ppermute | solution.py:877
  79.5 9.3 %collective-permute-start.42 = (bf16[128,1024]{1,0:T(8,128)(2,1)S(1)}, bf16[128,1024]{1,0:T(8,128)(2,1)S(1)}, u32[]{:S(2)}, u32[]{:S(2)}) collective-permute-start(bf16[128,1024]{1,0:T(8,128)(2,1)S(1)} %get-tuple-element.259), channel_id=1, source_target_pairs={{0,2},{1,3},{2,0},{3,1},{4,6},{5,7},{6,4},{7,5},{8,10},{9,11},{10,... | collective-permute-start | bytes 786440 | tf_op jit(solution)/shard_map/ppermute | solution.py:877
  79.8 18.2 %collective-permute-start.48 = (bf16[256,1024]{1,0:T(8,128)(2,1)S(1)}, bf16[256,1024]{1,0:T(8,128)(2,1)S(1)}, u32[]{:S(2)}, u32[]{:S(2)}) collective-permute-start(bf16[256,1024]{1,0:T(8,128)(2,1)S(1)} %get-tuple-element.271), channel_id=1, source_target_pairs={{0,8},{4,12},{8,0},{12,4},{16,24},{20,28},{24,16},{28,20},{1,9},{5... | collective-permute-start | bytes 1572872 | tf_op jit(solution)/shard_map/ppermute | solution.py:880
  85.3 27.1 %collective-permute-start.51 = (bf16[256,1024]{1,0:T(8,128)(2,1)S(1)}, bf16[256,1024]{1,0:T(8,128)(2,1)S(1)}, u32[]{:S(2)}, u32[]{:S(2)}) collective-permute-start(bf16[256,1024]{1,0:T(8,128)(2,1)S(1)} %get-tuple-element.279), channel_id=1, source_target_pairs={{0,16},{4,20},{8,24},{12,28},{16,0},{20,4},{24,8},{28,12},{1,17},{... | collective-permute-start | bytes 1572872 | tf_op jit(solution)/shard_map/ppermute | solution.py:880
  92.9 37.0 %collective-permute-start.60 = (bf16[512,512]{1,0:T(8,128)(2,1)S(1)}, bf16[512,512]{1,0:T(8,128)(2,1)S(1)}, u32[]{:S(2)}, u32[]{:S(2)}) collective-permute-start(bf16[512,512]{1,0:T(8,128)(2,1)S(1)} %mix_1.1.refs_14_), channel_id=1, source_target_pairs={{0,4},{4,0},{8,12},{12,8},{16,20},{20,16},{24,28},{28,24},{1,5},{5... | collective-permute-start | bytes 1572872 | tf_op jit(solution)/shard_map/ppermute | solution.py:880
  96.3 12.0 %collective-permute-start.46 = (bf16[272,256]{1,0:T(8,128)(2,1)S(1)}, bf16[272,256]{1,0:T(8,128)(2,1)S(1)}, u32[]{:S(2)}, u32[]{:S(2)}) collective-permute-start(bf16[272,256]{1,0:T(8,128)(2,1)S(1)} %get-tuple-element.270.refs_2_), channel_id=1, source_target_pairs={{0,8},{4,12},{8,0},{12,4},{16,24},{20,28},{24,16},{28,20},{1,9},{5... | collective-permute-start | bytes 417800 | tf_op jit(solution)/shard_map/ppermute | solution.py:880
  99.8 31.3 %collective-permute-start.59 = (bf16[256,1024]{1,0:T(8,128)(2,1)S(1)}, bf16[256,1024]{1,0:T(8,128)(2,1)S(1)}, u32[]{:S(2)}, u32[]{:S(2)}) collective-permute-start(bf16[256,1024]{1,0:T(8,128)(2,1)S(1)} %get-tuple-element.295), channel_id=1, source_target_pairs={{0,8},{4,12},{8,0},{12,4},{16,24},{20,28},{24,16},{28,20},{1,9},{5... | collective-permute-start | bytes 1572872 | tf_op jit(solution)/shard_map/ppermute | solution.py:880
  101.4 13.5 %collective-permute-start.50 = (bf16[192,256]{1,0:T(8,128)(2,1)S(1)}, bf16[192,256]{1,0:T(8,128)(2,1)S(1)}, u32[]{:S(2)}, u32[]{:S(2)}) collective-permute-start(bf16[192,256]{1,0:T(8,128)(2,1)S(1)} %get-tuple-element.278), channel_id=1, source_target_pairs={{0,1},{1,0},{2,3},{3,2},{4,5},{5,4},{6,7},{7,6},{8,9},{9,8},{10,11... | collective-permute-start | bytes 294920 | tf_op jit(solution)/shard_map/ppermute | solution.py:874
  108.3 14.7 %collective-permute-start.57 = (bf16[128,1024]{1,0:T(8,128)(2,1)S(1)}, bf16[128,1024]{1,0:T(8,128)(2,1)S(1)}, u32[]{:S(2)}, u32[]{:S(2)}) collective-permute-start(bf16[128,1024]{1,0:T(8,128)(2,1)S(1)} %get-tuple-element.290), channel_id=1, source_target_pairs={{0,16},{4,20},{8,24},{12,28},{16,0},{20,4},{24,8},{28,12},{1,17},{... | collective-permute-start | bytes 786440 | tf_op jit(solution)/shard_map/ppermute | solution.py:880
  112.5 6.5 %collective-permute-start.49 = (bf16[272,256]{1,0:T(8,128)(2,1)S(1)}, bf16[272,256]{1,0:T(8,128)(2,1)S(1)}, u32[]{:S(2)}, u32[]{:S(2)}) collective-permute-start(bf16[272,256]{1,0:T(8,128)(2,1)S(1)} %get-tuple-element.276.refs_2_), channel_id=1, source_target_pairs={{0,4},{4,0},{8,12},{12,8},{16,20},{20,16},{24,28},{28,24},{1,5},{5... | collective-permute-start | bytes 417800 | tf_op jit(solution)/shard_map/ppermute | solution.py:880
  114.9 8.4 %collective-permute-start.56 = (bf16[128,1024]{1,0:T(8,128)(2,1)S(1)}, bf16[128,1024]{1,0:T(8,128)(2,1)S(1)}, u32[]{:S(2)}, u32[]{:S(2)}) collective-permute-start(bf16[128,1024]{1,0:T(8,128)(2,1)S(1)} %get-tuple-element.289), channel_id=1, source_target_pairs={{0,4},{4,0},{8,12},{12,8},{16,20},{20,16},{24,28},{28,24},{1,5},{5... | collective-permute-start | bytes 786440 | tf_op jit(solution)/shard_map/ppermute | solution.py:880
  123.3 6.2 %collective-permute-start.54 = (bf16[64,1024]{1,0:T(8,128)(2,1)S(1)}, bf16[64,1024]{1,0:T(8,128)(2,1)S(1)}, u32[]{:S(2)}, u32[]{:S(2)}) collective-permute-start(bf16[64,1024]{1,0:T(8,128)(2,1)S(1)} %get-tuple-element.287), channel_id=1, source_target_pairs={{0,1},{1,0},{2,3},{3,2},{4,5},{5,4},{6,7},{7,6},{8,9},{9,8},{10,11... | collective-permute-start | bytes 393224 | tf_op jit(solution)/shard_map/ppermute | solution.py:874
  123.5 6.1 %collective-permute-start.55 = (bf16[64,1024]{1,0:T(8,128)(2,1)S(1)}, bf16[64,1024]{1,0:T(8,128)(2,1)S(1)}, u32[]{:S(2)}, u32[]{:S(2)}) collective-permute-start(bf16[64,1024]{1,0:T(8,128)(2,1)S(1)} %get-tuple-element.288), channel_id=1, source_target_pairs={{0,1},{1,0},{2,3},{3,2},{4,5},{5,4},{6,7},{7,6},{8,9},{9,8},{10,11... | collective-permute-start | bytes 393224 | tf_op jit(solution)/shard_map/ppermute | solution.py:874
  124.4 11.2 %collective-permute-start.63 = (bf16[272,256]{1,0:T(8,128)(2,1)S(1)}, bf16[272,256]{1,0:T(8,128)(2,1)S(1)}, u32[]{:S(2)}, u32[]{:S(2)}) collective-permute-start(bf16[272,256]{1,0:T(8,128)(2,1)S(1)} %get-tuple-element.282.refs_3_), channel_id=1, source_target_pairs={{0,16},{4,20},{8,24},{12,28},{16,0},{20,4},{24,8},{28,12},{1,17},{... | collective-permute-start | bytes 417800 | tf_op jit(solution)/shard_map/ppermute | solution.py:880
  130.7 13.8 %collective-permute-start.62 = (bf16[256,512]{1,0:T(8,128)(2,1)S(1)}, bf16[256,512]{1,0:T(8,128)(2,1)S(1)}, u32[]{:S(2)}, u32[]{:S(2)}) collective-permute-start(bf16[256,512]{1,0:T(8,128)(2,1)S(1)} %get-tuple-element.299), channel_id=1, source_target_pairs={{0,8},{4,12},{8,0},{12,4},{16,24},{20,28},{24,16},{28,20},{1,9},{5... | collective-permute-start | bytes 786440 | tf_op jit(solution)/shard_map/ppermute | solution.py:880
  131.3 14.7 %collective-permute-start.61 = (bf16[128,1024]{1,0:T(8,128)(2,1)S(1)}, bf16[128,1024]{1,0:T(8,128)(2,1)S(1)}, u32[]{:S(2)}, u32[]{:S(2)}) collective-permute-start(bf16[128,1024]{1,0:T(8,128)(2,1)S(1)} %get-tuple-element.298), channel_id=1, source_target_pairs={{0,16},{4,20},{8,24},{12,28},{16,0},{20,4},{24,8},{28,12},{1,17},{... | collective-permute-start | bytes 786440 | tf_op jit(solution)/shard_map/ppermute | solution.py:880
  134.0 12.8 %collective-permute-start.58 = (bf16[128,1024]{1,0:T(8,128)(2,1)S(1)}, bf16[128,1024]{1,0:T(8,128)(2,1)S(1)}, u32[]{:S(2)}, u32[]{:S(2)}) collective-permute-start(bf16[128,1024]{1,0:T(8,128)(2,1)S(1)} %get-tuple-element.294), channel_id=1, source_target_pairs={{0,2},{1,3},{2,0},{3,1},{4,6},{5,7},{6,4},{7,5},{8,10},{9,11},{10,... | collective-permute-start | bytes 786440 | tf_op jit(solution)/shard_map/ppermute | solution.py:877
  137.3 6.2 %collective-permute-start.64 = (f32[64,256]{1,0:T(8,128)S(1)}, f32[64,256]{1,0:T(8,128)S(1)}, u32[]{:S(2)}, u32[]{:S(2)}) collective-permute-start(f32[64,256]{1,0:T(8,128)S(1)} %get-tuple-element.305), channel_id=1, source_target_pairs={{0,2},{1,3},{2,0},{3,1},{4,6},{5,7},{6,4},{7,5},{8,10},{9,11},{10,... | collective-permute-start | bytes 196616 | tf_op jit(solution)/shard_map/ppermute | solution.py:877
  138.2 9.5 %collective-permute-start.65 = (bf16[192,128]{1,0:T(8,128)(2,1)S(1)}, bf16[192,128]{1,0:T(8,128)(2,1)S(1)}, u32[]{:S(2)}, u32[]{:S(2)}) collective-permute-start(bf16[192,128]{1,0:T(8,128)(2,1)S(1)} %get-tuple-element.310), channel_id=1, source_target_pairs={{0,2},{1,3},{2,0},{3,1},{4,6},{5,7},{6,4},{7,5},{8,10},{9,11},{10,... | collective-permute-start | bytes 147464 | tf_op jit(solution)/shard_map/ppermute | solution.py:877
  144.5 8.8 %collective-permute-start.67 = (bf16[128,512]{1,0:T(8,128)(2,1)S(1)}, bf16[128,512]{1,0:T(8,128)(2,1)S(1)}, u32[]{:S(2)}, u32[]{:S(2)}) collective-permute-start(bf16[128,512]{1,0:T(8,128)(2,1)S(1)} %get-tuple-element.319), channel_id=1, source_target_pairs={{0,16},{4,20},{8,24},{12,28},{16,0},{20,4},{24,8},{28,12},{1,17},{... | collective-permute-start | bytes 393224 | tf_op jit(solution)/shard_map/ppermute | solution.py:880
  (61 other events, 225.0 us)

commit v3 on v2

--- a/solution.py
+++ b/solution.py
@@ -25,23 +25,33 @@
 AXES = ((0, 1, 2), (1, 2, 0), (0, 1, 2), (0, 1, 2), (1, 0, 2))
 ORDER = (
     "mix_a", "mix_b", "first_a", "first_b", "base", "norm_a", "proj", "norm_b", "attend_a", "second_a", "cot",
-    "attend_b", "hidden_a", "second_b", "two_a", "mlp_a", "two_b", "hidden_b", "third_a", "mlp_b", "down_1",
-    "up_1", "third_b", "mid_a", "back_a", "mid_b", "back_b", "attn_1", "back_c", "fourth_a", "down_2",
-    "weights", "fourth_b", "up_2", "in_a", "in_b", "mix_1", "mass_1", "down_3", "attn_2", "mass_2", "up_3",
-    "field_1", "mass_3", "rows_1", "down_4", "up_4", "rows_2", "mix_2", "attn_3", "finish", "tables_1",
-    "mix_3", "attn_4", "rows_3", "field_2", "tables_2", "mix_4",
+    "attend_b", "hidden_a", "second_b", "two_a", "hidden_b", "mlp_a", "third_a", "two_b", "mlp_b", "down_1",
+    "up_1", "mid_a", "third_b", "back_a", "mid_b", "back_b", "attn_1", "fourth_a", "back_c", "fourth_b",
+    "down_2", "up_2", "weights", "in_a", "in_b", "mass_1", "mix_1", "down_3", "attn_2", "up_3", "mass_2",
+    "mass_3", "rows_1", "down_4", "rows_2", "mix_2", "field_1", "attn_3", "finish", "tables_1", "mix_3",
+    "rows_3", "field_2", "up_4", "attn_4", "tables_2", "mix_4",
 )
 COSTS = {
-    "two_a": 1,
-    "two_b": 0.3,
-    "mlp_b": 12,
-    "mid_a": 1,
-    "up_2": 1,
-    "in_a": 0.5,
-    "down_3": 2,
-    "up_3": 1,
+    "norm_a": 12,
+    "second_a": 0.5,
+    "second_b": 1,
+    "cot": 1,
+    "hidden_b": 3,
+    "weights": 1,
+    "two_a": 6.4,
+    "mlp_a": 0.4,
+    "third_a": 1,
+    "mlp_b": 1,
+    "back_a": 1.6,
+    "back_c": 0.5,
+    "fourth_a": 0.5,
+    "attn_1": 0.5,
+    "up_2": 2,
+    "mass_2": 0.5,
+    "field_2": 0.4,
+    "up_3": 0.5,
     "tables_1": 1,
-    "weights": 5,
+    "tables_2": 0.5,
 }
 
 
@@ -420,13 +430,13 @@
     scaled = (query.astype(F32) * SCALE).astype(BF16)
     parts = []
     for head in range(keys.shape[1] // HEAD_DIM):
-        scores = dot(lanes_of(keys, head), scaled, 1, 1)
+        scores = dot(keys, lanes_of(scaled, head), 1, 1)
         top = jnp.max(scores, axis=0, keepdims=True)
         weights = jnp.exp(scores - top)
         total = jnp.sum(weights, axis=0, keepdims=True)
         logs_ref[head : head + 1] = top + jnp.log(total)
-        probs = (weights * (1.0 / total)).astype(BF16)
-        parts.append(dot(values_t[head * HEAD_DIM : (head + 1) * HEAD_DIM], probs))
+        part = dot(values_t[head * HEAD_DIM : (head + 1) * HEAD_DIM], weights.astype(BF16))
+        parts.append(part * (1.0 / total))
     return jnp.concatenate(parts, axis=0).T.astype(BF16)
 
 
@@ -440,32 +450,33 @@
     project(own_ref, near_ref, w_ref, second_ref)
     keys = jnp.concatenate([first_ref[1], second_ref[1]], axis=0)
     values = jnp.concatenate([first_ref[2], second_ref[2]], axis=0)
-    out_ref[...] = attend(first_ref[0], keys, values.astype(F32).T.astype(BF16), logs_ref)
+    out_ref[...] = attend(first_ref[0], keys, values.T, logs_ref)
     split_out(dot(out_ref[...], w_out_ref[...]), keep_ref, send_ref)
 
 
 def attend_second(first_ref, second_ref, w_out_ref, out_ref, logs_ref, keep_ref, send_ref):
     keys = jnp.concatenate([first_ref[1], second_ref[1]], axis=0)
     values = jnp.concatenate([first_ref[2], second_ref[2]], axis=0)
-    out_ref[...] = attend(second_ref[0], keys, values.astype(F32).T.astype(BF16), logs_ref)
+    out_ref[...] = attend(second_ref[0], keys, values.T, logs_ref)
     split_out(dot(out_ref[...], w_out_ref[...]), keep_ref, send_ref)
 
 
 def attend_grad(grad, query, keys, values, logs_ref):
     scaled = (query.astype(F32) * SCALE).astype(BF16)
-    keys_t = keys.astype(F32).T.astype(BF16)
+    keys_t = keys.T
     query_parts = []
     key_grad = jnp.zeros(keys.shape, F32)
     value_grad = jnp.zeros(keys.shape, F32)
     for head in range(keys.shape[1] // HEAD_DIM):
-        scores = dot(lanes_of(keys, head), scaled, 1, 1)
+        head_query, head_grad = lanes_of(scaled, head), lanes_of(grad, head)
+        scores = dot(keys, head_query, 1, 1)
         probs = jnp.exp(scores - logs_ref[head : head + 1])
-        prob_grad = dot(lanes_of(values, head), grad, 1, 1)
+        prob_grad = dot(values, head_grad, 1, 1)
         middle = jnp.sum(probs * prob_grad, axis=0, keepdims=True)
         score_grad = (probs * (prob_grad - middle)).astype(BF16)
         query_parts.append(dot(keys_t[head * HEAD_DIM : (head + 1) * HEAD_DIM], score_grad))
-        key_grad = key_grad + dot(score_grad, lanes_of(scaled, head))
-        value_grad = value_grad + dot(probs.astype(BF16), lanes_of(grad, head))
+        key_grad = key_grad + dot(score_grad, head_query)
+        value_grad = value_grad + dot(probs.astype(BF16), head_grad)
     query_grad = (jnp.concatenate(query_parts, axis=0).T * SCALE).astype(BF16)
     return query_grad, key_grad, value_grad
 

time: 155 us -> 151 us (0.974)
  waiting for transfers between devices: 52.5 us -> 47.8 us
    ppermute x15, waiting for transfers between devices: 21.8 us -> 15.7 us  [swap_sample(): return lax.ppermute(value, 'dp', pairs(mesh_dp, bit))]
    ppermute x41, waiting for transfers between devices: 8.75 us -> 10.4 us  [swap_core(): return lax.ppermute(value, 'mp', pairs(mesh_mp, 1))]
  transfers between devices with their start and end apart: 68 -> 68, of which waited for: 41 -> 29; matrix products, arithmetic and copies ran while one was open for 0% -> 0% of each run, Pallas kernels for 24% -> 26%
where the time goes in v3:
time: 151 us
  starting transfers between devices  52.7 us (35%)
  waiting for transfers between devices  47.8 us (32%)
  Pallas kernels  45.4 us (30%)
  local copies, waits for them, and re-layouts  2.77 us (2%)
  between operations  2.09 us (1%)
    pallas_call x58, Pallas kernels, launch(): pl.pallas_call(run, out_shape=[jax.ShapeDtypeStruct(shape, kind) for shap...  45.4 us
    ppermute x15, starting transfers between devices, swap_sample(): return lax.ppermute(value, 'dp', pairs(mesh_dp, bit))  25.8 us
    ppermute x12, waiting for transfers between devices, swap_chip(): return lax.ppermute(value, 'mp', pairs(mesh_mp, 2))  21.7 us
    ppermute x12, starting transfers between devices, swap_chip(): return lax.ppermute(value, 'mp', pairs(mesh_mp, 2))  16.4 us
    ppermute x15, waiting for transfers between devices, swap_sample(): return lax.ppermute(value, 'dp', pairs(mesh_dp, bit))  15.7 us
    ppermute x41, starting transfers between devices, swap_core(): return lax.ppermute(value, 'mp', pairs(mesh_mp, 1))  10.5 us
    ppermute x41, waiting for transfers between devices, swap_core(): return lax.ppermute(value, 'mp', pairs(mesh_mp, 1))  10.4 us
  transfers between devices with their start and end apart: 68, of which 29 were waited for; matrix products, arithmetic and copies ran while one was open for 0% of the time, Pallas kernels for 26%

profile of v3, /device:TPU:0, one launch (start us, length us, event | category | flops | bytes accessed | tf_op | source)
XLA Modules:
  0.0 150.8 jit_solution(16803712819698494986)
XLA Ops:
  0.7 4.0 %mix_a.1 = (bf16[256,512]{1,0:T(8,128)(2,1)}, bf16[192,512]{1,0:T(8,128)(2,1)}, f32[192,512]{1,0:T(8,128)}, bf16[256,256]{1,0:T(8,128)(2,1)}, f32[256,256]{1,0:T...) custom-call(s32[48]{0:T(128)} %refs_0_.8, bf16[1,192,512]{2,1,0:T(8,128)(2,1)} %refs_1_.3, bf16[48,4,1024]{2,1,0:T(4,128)(2,1)} %refs_2_.9, ...), custom_call_target="tpu_custom_call" | custom-call | flops 100000000 | tf_op jit(solution)/shard_map/mix_a/pallas_call | solution.py:132
  8.1 3.0 %collective-permute-start.3 = (bf16[128,1024]{1,0:T(8,128)(2,1)S(1)}, bf16[128,1024]{1,0:T(8,128)(2,1)S(1)}, u32[]{:S(2)}, u32[]{:S(2)}) collective-permute-start(bf16[128,1024]{1,0:T(8,128)(2,1)S(1)} %get-tuple-element.182), channel_id=1, source_target_pairs={{0,2},{1,3},{2,0},{3,1},{4,6},{5,7},{6,4},{7,5},{8,10},{9,11},{10,... | collective-permute-start | bytes 786440 | tf_op jit(solution)/shard_map/ppermute | solution.py:888
  12.5 5.6 %collective-permute-done.3.refs_1_ = bf16[128,1024]{1,0:T(8,128)(2,1)S(1)} collective-permute-done((bf16[128,1024]{1,0:T(8,128)(2,1)S(1)}, bf16[128,1024]{1,0:T(8,128)(2,1)S(1)}, u32[]{:S(2)}, u32[]{:S(2)}) %collective-permute-start.3) | collective-permute-done | bytes 262176 | tf_op jit(solution)/shard_map/ppermute | solution.py:888
  20.6 2.6 %collective-permute-done.2.refs_2_ = bf16[128,1024]{1,0:T(8,128)(2,1)S(1)} collective-permute-done((bf16[128,1024]{1,0:T(8,128)(2,1)S(1)}, bf16[128,1024]{1,0:T(8,128)(2,1)S(1)}, u32[]{:S(2)}, u32[]{:S(2)}) %collective-permute-start.2) | collective-permute-done | bytes 262176 | tf_op jit(solution)/shard_map/ppermute | solution.py:888
  24.1 1.7 %collective-permute-start.11 = (bf16[128,1024]{1,0:T(8,128)(2,1)S(1)}, bf16[128,1024]{1,0:T(8,128)(2,1)S(1)}, u32[]{:S(2)}, u32[]{:S(2)}) collective-permute-start(bf16[128,1024]{1,0:T(8,128)(2,1)S(1)} %get-tuple-element.196.refs_0_), channel_id=1, source_target_pairs={{0,2},{1,3},{2,0},{3,1},{4,6},{5,7},{6,4},{7,5},{8,10},{9,11},{10,... | collective-permute-start | bytes 786440 | tf_op jit(solution)/shard_map/ppermute | solution.py:888
  25.8 2.6 %attend_a.1 = (bf16[3,256,256]{2,1,0:T(8,128)(2,1)S(1)}, bf16[256,256]{1,0:T(8,128)(2,1)S(1)}, f32[8,256]{1,0:T(8,128)S(1)}, f32[128,1024]{1,0:T(8,128)S(1)}, bf...) custom-call(bf16[64,1024]{1,0:T(8,128)(2,1)S(1)} %get-tuple-element.187.refs_0_.refs_4_.refs_5_, ...), custom_call_target="tpu_custom_call" | custom-call | flops 100000000 | tf_op jit(solution)/shard_map/attend_a/pallas_call | solution.py:132
  33.0 2.0 %attend_b.1 = (bf16[256,256]{1,0:T(8,128)(2,1)S(1)}, f32[8,256]{1,0:T(8,128)S(1)}, f32[128,1024]{1,0:T(8,128)S(1)}, bf16[64,1024]{1,0:T(8,128)(2,1)S(1)}, bf16[64,1024]{1,0:T(8,128)(2,1)S(1)}) custom-call(bf16[3,256,256]{2,1,0:T(8,128)(2,1)S(1)} %proj.1.refs_6_.refs_5_.refs_0_, bf16[3,256,256]{2,1,0:T(8,128)(2,1)S(1)} %get-tuple-element.193.refs_3_.refs_1_.refs_6_, ...), custom_call_target="tpu_custom_call" | custom-call | flops 100000000 | tf_op jit(solution)/shard_map/attend_b/pallas_call | solution.py:132
  37.0 1.8 %collective-permute-start.20 = (bf16[128,1024]{1,0:T(8,128)(2,1)S(1)}, bf16[128,1024]{1,0:T(8,128)(2,1)S(1)}, u32[]{:S(2)}, u32[]{:S(2)}) collective-permute-start(bf16[128,1024]{1,0:T(8,128)(2,1)S(1)} %get-tuple-element.210), channel_id=1, source_target_pairs={{0,2},{1,3},{2,0},{3,1},{4,6},{5,7},{6,4},{7,5},{8,10},{9,11},{10,... | collective-permute-start | bytes 786440 | tf_op jit(solution)/shard_map/ppermute | solution.py:888
  41.3 1.9 %mlp_a.1 = (bf16[256,1024]{1,0:T(8,128)(2,1)S(1)}, bf16[256,1024]{1,0:T(8,128)(2,1)S(1)}, f32[128,1024]{1,0:T(8,128)S(1)}, bf16[64,1024]{1,0:T(8,128)(2,1)S(1)}, bf16[64,1024]{1,0:T(8,128)(2,1)S(1)}) custom-call(bf16[64,1024]{1,0:T(8,128)(2,1)S(1)} %get-tuple-element.204.refs_0_.refs_1_, bf16[64,1024]{1,0:T(8,128)(2,1)S(1)} %get-tuple-element.205.refs_1_.refs_2_, ...), custom_call_target="tpu_custom_call" | custom-call | flops 400000000 | tf_op jit(solution)/shard_map/mlp_a/pallas_call | solution.py:132
  46.2 1.7 %collective-permute-start.29 = (bf16[128,1024]{1,0:T(8,128)(2,1)S(1)}, bf16[128,1024]{1,0:T(8,128)(2,1)S(1)}, u32[]{:S(2)}, u32[]{:S(2)}) collective-permute-start(bf16[128,1024]{1,0:T(8,128)(2,1)S(1)} %get-tuple-element.224), channel_id=1, source_target_pairs={{0,2},{1,3},{2,0},{3,1},{4,6},{5,7},{6,4},{7,5},{8,10},{9,11},{10,... | collective-permute-start | bytes 786440 | tf_op jit(solution)/shard_map/ppermute | solution.py:888
  48.0 1.9 %mlp_b.1 = (bf16[256,1024]{1,0:T(8,128)(2,1)S(1)}, bf16[256,1024]{1,0:T(8,128)(2,1)S(1)}, f32[128,1024]{1,0:T(8,128)S(1)}, bf16[64,1024]{1,0:T(8,128)(2,1)S(1)}, bf16[64,1024]{1,0:T(8,128)(2,1)S(1)}) custom-call(bf16[64,1024]{1,0:T(8,128)(2,1)S(1)} %get-tuple-element.215.refs_0_.refs_4_.refs_5_, ...), custom_call_target="tpu_custom_call" | custom-call | flops 1000000000 | tf_op jit(solution)/shard_map/mlp_b/pallas_call | solution.py:132
  50.6 1.5 %collective-permute-start.26 = (bf16[512,1024]{1,0:T(8,128)(2,1)S(1)}, bf16[512,1024]{1,0:T(8,128)(2,1)S(1)}, u32[]{:S(2)}, u32[]{:S(2)}) collective-permute-start(bf16[512,1024]{1,0:T(8,128)(2,1)S(1)} %down_1.1.refs_10_), channel_id=1, source_target_pairs={{0,4},{4,0},{8,12},{12,8},{16,20},{20,16},{24,28},{28,24},{1,5},{5... | collective-permute-start | bytes 3145736 | tf_op jit(solution)/shard_map/ppermute | solution.py:891
  53.2 1.6 %collective-permute-start.25 = (bf16[512,1024]{1,0:T(8,128)(2,1)S(1)}, bf16[512,1024]{1,0:T(8,128)(2,1)S(1)}, u32[]{:S(2)}, u32[]{:S(2)}) collective-permute-start(bf16[512,1024]{1,0:T(8,128)(2,1)S(1)} %up_1.1.refs_6_), channel_id=1, source_target_pairs={{0,8},{4,12},{8,0},{12,4},{16,24},{20,28},{24,16},{28,20},{1,9},{5... | collective-permute-start | bytes 3145736 | tf_op jit(solution)/shard_map/ppermute | solution.py:891
  57.6 2.8 %back_a.1 = (bf16[256,256]{1,0:T(8,128)(2,1)S(1)}, f32[512,256]{1,0:T(8,128)S(1)}, f32[512,256]{1,0:T(8,128)S(1)}) custom-call(bf16[64,1024]{1,0:T(8,128)(2,1)S(1)} %get-tuple-element.228.refs_0_.refs_8_.refs_9_, bf16[64,1024]{1,0:T(8,128)(2,1)S(1)} %get-tuple-element.229.refs_1_.refs_9_.refs_10_, ...), custom_call_target="tpu_custom_call" | custom-call | flops 1600000000 | tf_op jit(solution)/shard_map/back_a/pallas_call | solution.py:132
  60.4 4.7 %collective-permute-done.30.refs_1_ = bf16[128,1024]{1,0:T(8,128)(2,1)S(1)} collective-permute-done((bf16[128,1024]{1,0:T(8,128)(2,1)S(1)}, bf16[128,1024]{1,0:T(8,128)(2,1)S(1)}, u32[]{:S(2)}, u32[]{:S(2)}) %collective-permute-start.30) | collective-permute-done | bytes 262176 | tf_op jit(solution)/shard_map/ppermute | solution.py:888
  67.1 3.2 %back_b.1 = (bf16[3,512,256]{2,1,0:T(8,128)(2,1)S(1)}, f32[128,1024]{1,0:T(8,128)S(1)}, bf16[64,1024]{1,0:T(8,128)(2,1)S(1)}, bf16[64,1024]{1,0:T(8,128)(2,1)S(1)}) custom-call(bf16[64,1024]{1,0:T(8,128)(2,1)S(1)} %get-tuple-element.232.refs_0_.refs_12_.refs_13_, bf16[64,1024]{1,0:T(8,128)(2,1)S(1)} %get-tuple-element.233.refs_1_.refs_13_.refs_14_, ...), custom_call_target="tpu_custom_call" | custom-call | flops 100000000 | tf_op jit(solution)/shard_map/back_b/pallas_call | solution.py:132
  74.6 1.5 %collective-permute-start.39 = (bf16[128,1024]{1,0:T(8,128)(2,1)S(1)}, bf16[128,1024]{1,0:T(8,128)(2,1)S(1)}, u32[]{:S(2)}, u32[]{:S(2)}) collective-permute-start(bf16[128,1024]{1,0:T(8,128)(2,1)S(1)} %get-tuple-element.255), channel_id=1, source_target_pairs={{0,2},{1,3},{2,0},{3,1},{4,6},{5,7},{6,4},{7,5},{8,10},{9,11},{10,... | collective-permute-start | bytes 786440 | tf_op jit(solution)/shard_map/ppermute | solution.py:888
  77.7 1.7 %collective-permute-start.48 = (bf16[256,1024]{1,0:T(8,128)(2,1)S(1)}, bf16[256,1024]{1,0:T(8,128)(2,1)S(1)}, u32[]{:S(2)}, u32[]{:S(2)}) collective-permute-start(bf16[256,1024]{1,0:T(8,128)(2,1)S(1)} %get-tuple-element.271), channel_id=1, source_target_pairs={{0,8},{4,12},{8,0},{12,4},{16,24},{20,28},{24,16},{28,20},{1,9},{5... | collective-permute-start | bytes 1572872 | tf_op jit(solution)/shard_map/ppermute | solution.py:891
  80.3 2.6 %collective-permute-start.46 = (bf16[256,1024]{1,0:T(8,128)(2,1)S(1)}, bf16[256,1024]{1,0:T(8,128)(2,1)S(1)}, u32[]{:S(2)}, u32[]{:S(2)}) collective-permute-start(bf16[256,1024]{1,0:T(8,128)(2,1)S(1)} %get-tuple-element.270), channel_id=1, source_target_pairs={{0,16},{4,20},{8,24},{12,28},{16,0},{20,4},{24,8},{28,12},{1,17},{... | collective-permute-start | bytes 1572872 | tf_op jit(solution)/shard_map/ppermute | solution.py:891
  84.6 3.9 %collective-permute-done.42.refs_1_ = bf16[128,1024]{1,0:T(8,128)(2,1)S(1)} collective-permute-done((bf16[128,1024]{1,0:T(8,128)(2,1)S(1)}, bf16[128,1024]{1,0:T(8,128)(2,1)S(1)}, u32[]{:S(2)}, u32[]{:S(2)}) %collective-permute-start.42) | collective-permute-done | bytes 262176 | tf_op jit(solution)/shard_map/ppermute | solution.py:888
  92.1 1.6 %mass_1.1 = (bf16[272,256]{1,0:T(8,128)(2,1)S(1)}, f32[256,256]{1,0:T(8,128)S(1)}, f32[8,256]{1,0:T(8,128)S(1)}, bf16[192,256]{1,0:T(8,128)(2,1)S(1)}, f32[192,256]{1,0:T(8,128)S(1)}) custom-call(bf16[192,192]{1,0:T(8,128)(2,1)S(1)} %get-tuple-element.250.refs_0_, bf16[192,512]{1,0:T(8,128)(2,1)S(1)} %copy-done.14, f32[192,512]{1,0:T(8,128)S(1)} %copy-done.11, ...), custom_call_target="tpu_custom_call" | custom-call | flops 100000000 | tf_op jit(solution)/shard_map/mass_1/pallas_call | solution.py:132
  93.7 1.7 %collective-permute-start.45 = (bf16[272,256]{1,0:T(8,128)(2,1)S(1)}, bf16[272,256]{1,0:T(8,128)(2,1)S(1)}, u32[]{:S(2)}, u32[]{:S(2)}) collective-permute-start(bf16[272,256]{1,0:T(8,128)(2,1)S(1)} %get-tuple-element.269.refs_14_), channel_id=1, source_target_pairs={{0,8},{4,12},{8,0},{12,4},{16,24},{20,28},{24,16},{28,20},{1,9},{5... | collective-permute-start | bytes 417800 | tf_op jit(solution)/shard_map/ppermute | solution.py:891
  97.8 4.9 %collective-permute-done.48.refs_1_ = bf16[256,1024]{1,0:T(8,128)(2,1)S(1)} collective-permute-done((bf16[256,1024]{1,0:T(8,128)(2,1)S(1)}, bf16[256,1024]{1,0:T(8,128)(2,1)S(1)}, u32[]{:S(2)}, u32[]{:S(2)}) %collective-permute-start.48) | collective-permute-done | bytes 524320 | tf_op jit(solution)/shard_map/ppermute | solution.py:891
  104.4 3.0 %collective-permute-start.60 = (bf16[256,1024]{1,0:T(8,128)(2,1)S(1)}, bf16[256,1024]{1,0:T(8,128)(2,1)S(1)}, u32[]{:S(2)}, u32[]{:S(2)}) collective-permute-start(bf16[256,1024]{1,0:T(8,128)(2,1)S(1)} %get-tuple-element.296), channel_id=1, source_target_pairs={{0,8},{4,12},{8,0},{12,4},{16,24},{20,28},{24,16},{28,20},{1,9},{5... | collective-permute-start | bytes 1572872 | tf_op jit(solution)/shard_map/ppermute | solution.py:891
  107.7 2.1 %collective-permute-start.50 = (bf16[272,256]{1,0:T(8,128)(2,1)S(1)}, bf16[272,256]{1,0:T(8,128)(2,1)S(1)}, u32[]{:S(2)}, u32[]{:S(2)}) collective-permute-start(bf16[272,256]{1,0:T(8,128)(2,1)S(1)} %get-tuple-element.278.refs_3_), channel_id=1, source_target_pairs={{0,4},{4,0},{8,12},{12,8},{16,20},{20,16},{24,28},{28,24},{1,5},{5... | collective-permute-start | bytes 417800 | tf_op jit(solution)/shard_map/ppermute | solution.py:891
  109.8 4.4 %collective-permute-done.50.refs_2_ = bf16[272,256]{1,0:T(8,128)(2,1)S(1)} collective-permute-done((bf16[272,256]{1,0:T(8,128)(2,1)S(1)}, bf16[272,256]{1,0:T(8,128)(2,1)S(1)}, u32[]{:S(2)}, u32[]{:S(2)}) %collective-permute-start.50) | collective-permute-done | bytes 139296 | tf_op jit(solution)/shard_map/ppermute | solution.py:891
  118.5 1.5 %collective-permute-start.59 = (bf16[272,256]{1,0:T(8,128)(2,1)S(1)}, bf16[272,256]{1,0:T(8,128)(2,1)S(1)}, u32[]{:S(2)}, u32[]{:S(2)}) collective-permute-start(bf16[272,256]{1,0:T(8,128)(2,1)S(1)} %get-tuple-element.279.refs_3_), channel_id=1, source_target_pairs={{0,16},{4,20},{8,24},{12,28},{16,0},{20,4},{24,8},{28,12},{1,17},{... | collective-permute-start | bytes 417800 | tf_op jit(solution)/shard_map/ppermute | solution.py:891
  122.1 3.9 %collective-permute-start.58 = (bf16[256,512]{1,0:T(8,128)(2,1)S(1)}, bf16[256,512]{1,0:T(8,128)(2,1)S(1)}, u32[]{:S(2)}, u32[]{:S(2)}) collective-permute-start(bf16[256,512]{1,0:T(8,128)(2,1)S(1)} %get-tuple-element.291), channel_id=1, source_target_pairs={{0,8},{4,12},{8,0},{12,4},{16,24},{20,28},{24,16},{28,20},{1,9},{5... | collective-permute-start | bytes 786440 | tf_op jit(solution)/shard_map/ppermute | solution.py:891
  129.2 1.7 %finish.1 = (f32[64,256]{1,0:T(8,128)S(1)}, f32[64,256]{1,0:T(8,128)S(1)}, f32[3,128,256]{2,1,0:T(8,128)}) custom-call(f32[256,128]{1,0:T(8,128)S(1)} %copy-done.15, f32[256,256]{1,0:T(8,128)S(1)} %copy-done.13, bf16[48,4,1024]{2,1,0:T(4,128)(2,1)S(1)} %copy-done.9, bf16[48,1024]{1,0:T(8,128)(2,1)S(1)} %copy-done.10, ...), custom_call_target="tpu_custom_call" | custom-call | flops 100000000 | tf_op jit(solution)/shard_map/finish/pallas_call | solution.py:132
  132.0 3.3 %collective-permute-done.62.refs_1_ = f32[64,256]{1,0:T(8,128)S(1)} collective-permute-done((f32[64,256]{1,0:T(8,128)S(1)}, f32[64,256]{1,0:T(8,128)S(1)}, u32[]{:S(2)}, u32[]{:S(2)}) %collective-permute-start.62) | collective-permute-done | bytes 65568 | tf_op jit(solution)/shard_map/ppermute | solution.py:888
  136.8 2.6 %collective-permute-start.67 = (bf16[128,512]{1,0:T(8,128)(2,1)S(1)}, bf16[128,512]{1,0:T(8,128)(2,1)S(1)}, u32[]{:S(2)}, u32[]{:S(2)}) collective-permute-start(bf16[128,512]{1,0:T(8,128)(2,1)S(1)} %get-tuple-element.319), channel_id=1, source_target_pairs={{0,16},{4,20},{8,24},{12,28},{16,0},{20,4},{24,8},{28,12},{1,17},{... | collective-permute-start | bytes 393224 | tf_op jit(solution)/shard_map/ppermute | solution.py:891
  141.8 5.4 %collective-permute-done.65.refs_1_ = bf16[128,1024]{1,0:T(8,128)(2,1)S(1)} collective-permute-done((bf16[128,1024]{1,0:T(8,128)(2,1)S(1)}, bf16[128,1024]{1,0:T(8,128)(2,1)S(1)}, u32[]{:S(2)}, u32[]{:S(2)}) %collective-permute-start.65) | collective-permute-done | bytes 262176 | tf_op jit(solution)/shard_map/ppermute | solution.py:891
  (214 shorter events, 60.1 us)
Async XLA Ops:
  6.8 4.9 %collective-permute-start = (bf16[128,1024]{1,0:T(8,128)(2,1)S(1)}, bf16[128,1024]{1,0:T(8,128)(2,1)S(1)}, u32[]{:S(2)}, u32[]{:S(2)}) collective-permute-start(bf16[128,1024]{1,0:T(8,128)(2,1)S(1)} %get-tuple-element.175), channel_id=1, source_target_pairs={{0,1},{1,0},{2,3},{3,2},{4,5},{5,4},{6,7},{7,6},{8,9},{9,8},{10,11... | collective-permute-start | bytes 786440 | tf_op jit(solution)/shard_map/ppermute | solution.py:885
  8.1 10.0 %collective-permute-start.3 = (bf16[128,1024]{1,0:T(8,128)(2,1)S(1)}, bf16[128,1024]{1,0:T(8,128)(2,1)S(1)}, u32[]{:S(2)}, u32[]{:S(2)}) collective-permute-start(bf16[128,1024]{1,0:T(8,128)(2,1)S(1)} %get-tuple-element.182), channel_id=1, source_target_pairs={{0,2},{1,3},{2,0},{3,1},{4,6},{5,7},{6,4},{7,5},{8,10},{9,11},{10,... | collective-permute-start | bytes 786440 | tf_op jit(solution)/shard_map/ppermute | solution.py:888
  11.8 11.5 %collective-permute-start.2 = (bf16[128,1024]{1,0:T(8,128)(2,1)S(1)}, bf16[128,1024]{1,0:T(8,128)(2,1)S(1)}, u32[]{:S(2)}, u32[]{:S(2)}) collective-permute-start(bf16[128,1024]{1,0:T(8,128)(2,1)S(1)} %get-tuple-element.180), channel_id=1, source_target_pairs={{0,2},{1,3},{2,0},{3,1},{4,6},{5,7},{6,4},{7,5},{8,10},{9,11},{10,... | collective-permute-start | bytes 786440 | tf_op jit(solution)/shard_map/ppermute | solution.py:888
  24.1 8.3 %collective-permute-start.11 = (bf16[128,1024]{1,0:T(8,128)(2,1)S(1)}, bf16[128,1024]{1,0:T(8,128)(2,1)S(1)}, u32[]{:S(2)}, u32[]{:S(2)}) collective-permute-start(bf16[128,1024]{1,0:T(8,128)(2,1)S(1)} %get-tuple-element.196.refs_0_), channel_id=1, source_target_pairs={{0,2},{1,3},{2,0},{3,1},{4,6},{5,7},{6,4},{7,5},{8,10},{9,11},{10,... | collective-permute-start | bytes 786440 | tf_op jit(solution)/shard_map/ppermute | solution.py:888
  30.1 8.7 %collective-permute-start.10 = (bf16[128,1024]{1,0:T(8,128)(2,1)S(1)}, bf16[128,1024]{1,0:T(8,128)(2,1)S(1)}, u32[]{:S(2)}, u32[]{:S(2)}) collective-permute-start(bf16[128,1024]{1,0:T(8,128)(2,1)S(1)} %get-tuple-element.195), channel_id=1, source_target_pairs={{0,2},{1,3},{2,0},{3,1},{4,6},{5,7},{6,4},{7,5},{8,10},{9,11},{10,... | collective-permute-start | bytes 786440 | tf_op jit(solution)/shard_map/ppermute | solution.py:888
  35.6 4.1 %collective-permute-start.18 = (bf16[64,1024]{1,0:T(8,128)(2,1)S(1)}, bf16[64,1024]{1,0:T(8,128)(2,1)S(1)}, u32[]{:S(2)}, u32[]{:S(2)}) collective-permute-start(bf16[64,1024]{1,0:T(8,128)(2,1)S(1)} %get-tuple-element.206.refs_0_.refs_4_.refs_5_), channel_id=1, source_target_pairs={{0,1},{1,0},{2,3},{3,2},{4,5},{5,4},{6,7},{7,6},{8,9},{9,8},{10,11... | collective-permute-start | bytes 393224 | tf_op jit(solution)/shard_map/ppermute | solution.py:885
  35.7 4.0 %collective-permute-start.19 = (bf16[64,1024]{1,0:T(8,128)(2,1)S(1)}, bf16[64,1024]{1,0:T(8,128)(2,1)S(1)}, u32[]{:S(2)}, u32[]{:S(2)}) collective-permute-start(bf16[64,1024]{1,0:T(8,128)(2,1)S(1)} %get-tuple-element.207.refs_1_.refs_5_.refs_6_), channel_id=1, source_target_pairs={{0,1},{1,0},{2,3},{3,2},{4,5},{5,4},{6,7},{7,6},{8,9},{9,8},{10,11... | collective-permute-start | bytes 393224 | tf_op jit(solution)/shard_map/ppermute | solution.py:885
  37.0 8.4 %collective-permute-start.20 = (bf16[128,1024]{1,0:T(8,128)(2,1)S(1)}, bf16[128,1024]{1,0:T(8,128)(2,1)S(1)}, u32[]{:S(2)}, u32[]{:S(2)}) collective-permute-start(bf16[128,1024]{1,0:T(8,128)(2,1)S(1)} %get-tuple-element.210), channel_id=1, source_target_pairs={{0,2},{1,3},{2,0},{3,1},{4,6},{5,7},{6,4},{7,5},{8,10},{9,11},{10,... | collective-permute-start | bytes 786440 | tf_op jit(solution)/shard_map/ppermute | solution.py:888
  46.2 9.1 %collective-permute-start.29 = (bf16[128,1024]{1,0:T(8,128)(2,1)S(1)}, bf16[128,1024]{1,0:T(8,128)(2,1)S(1)}, u32[]{:S(2)}, u32[]{:S(2)}) collective-permute-start(bf16[128,1024]{1,0:T(8,128)(2,1)S(1)} %get-tuple-element.224), channel_id=1, source_target_pairs={{0,2},{1,3},{2,0},{3,1},{4,6},{5,7},{6,4},{7,5},{8,10},{9,11},{10,... | collective-permute-start | bytes 786440 | tf_op jit(solution)/shard_map/ppermute | solution.py:888
  50.6 26.1 %collective-permute-start.26 = (bf16[512,1024]{1,0:T(8,128)(2,1)S(1)}, bf16[512,1024]{1,0:T(8,128)(2,1)S(1)}, u32[]{:S(2)}, u32[]{:S(2)}) collective-permute-start(bf16[512,1024]{1,0:T(8,128)(2,1)S(1)} %down_1.1.refs_10_), channel_id=1, source_target_pairs={{0,4},{4,0},{8,12},{12,8},{16,20},{20,16},{24,28},{28,24},{1,5},{5... | collective-permute-start | bytes 3145736 | tf_op jit(solution)/shard_map/ppermute | solution.py:891
  53.2 26.2 %collective-permute-start.25 = (bf16[512,1024]{1,0:T(8,128)(2,1)S(1)}, bf16[512,1024]{1,0:T(8,128)(2,1)S(1)}, u32[]{:S(2)}, u32[]{:S(2)}) collective-permute-start(bf16[512,1024]{1,0:T(8,128)(2,1)S(1)} %up_1.1.refs_6_), channel_id=1, source_target_pairs={{0,8},{4,12},{8,0},{12,4},{16,24},{20,28},{24,16},{28,20},{1,9},{5... | collective-permute-start | bytes 3145736 | tf_op jit(solution)/shard_map/ppermute | solution.py:891
  56.5 8.5 %collective-permute-start.30 = (bf16[128,1024]{1,0:T(8,128)(2,1)S(1)}, bf16[128,1024]{1,0:T(8,128)(2,1)S(1)}, u32[]{:S(2)}, u32[]{:S(2)}) collective-permute-start(bf16[128,1024]{1,0:T(8,128)(2,1)S(1)} %get-tuple-element.227), channel_id=1, source_target_pairs={{0,2},{1,3},{2,0},{3,1},{4,6},{5,7},{6,4},{7,5},{8,10},{9,11},{10,... | collective-permute-start | bytes 786440 | tf_op jit(solution)/shard_map/ppermute | solution.py:888
  71.7 31.7 %collective-permute-start.47 = (bf16[512,1024]{1,0:T(8,128)(2,1)S(1)}, bf16[512,1024]{1,0:T(8,128)(2,1)S(1)}, u32[]{:S(2)}, u32[]{:S(2)}) collective-permute-start(bf16[512,1024]{1,0:T(8,128)(2,1)S(1)} %attn_1.1.refs_3_), channel_id=1, source_target_pairs={{0,4},{4,0},{8,12},{12,8},{16,20},{20,16},{24,28},{28,24},{1,5},{5... | collective-permute-start | bytes 3145736 | tf_op jit(solution)/shard_map/ppermute | solution.py:891
  74.6 9.5 %collective-permute-start.39 = (bf16[128,1024]{1,0:T(8,128)(2,1)S(1)}, bf16[128,1024]{1,0:T(8,128)(2,1)S(1)}, u32[]{:S(2)}, u32[]{:S(2)}) collective-permute-start(bf16[128,1024]{1,0:T(8,128)(2,1)S(1)} %get-tuple-element.255), channel_id=1, source_target_pairs={{0,2},{1,3},{2,0},{3,1},{4,6},{5,7},{6,4},{7,5},{8,10},{9,11},{10,... | collective-permute-start | bytes 786440 | tf_op jit(solution)/shard_map/ppermute | solution.py:888
  76.2 12.4 %collective-permute-start.42 = (bf16[128,1024]{1,0:T(8,128)(2,1)S(1)}, bf16[128,1024]{1,0:T(8,128)(2,1)S(1)}, u32[]{:S(2)}, u32[]{:S(2)}) collective-permute-start(bf16[128,1024]{1,0:T(8,128)(2,1)S(1)} %get-tuple-element.259), channel_id=1, source_target_pairs={{0,2},{1,3},{2,0},{3,1},{4,6},{5,7},{6,4},{7,5},{8,10},{9,11},{10,... | collective-permute-start | bytes 786440 | tf_op jit(solution)/shard_map/ppermute | solution.py:888
  77.7 25.0 %collective-permute-start.48 = (bf16[256,1024]{1,0:T(8,128)(2,1)S(1)}, bf16[256,1024]{1,0:T(8,128)(2,1)S(1)}, u32[]{:S(2)}, u32[]{:S(2)}) collective-permute-start(bf16[256,1024]{1,0:T(8,128)(2,1)S(1)} %get-tuple-element.271), channel_id=1, source_target_pairs={{0,8},{4,12},{8,0},{12,4},{16,24},{20,28},{24,16},{28,20},{1,9},{5... | collective-permute-start | bytes 1572872 | tf_op jit(solution)/shard_map/ppermute | solution.py:891
  80.3 27.1 %collective-permute-start.46 = (bf16[256,1024]{1,0:T(8,128)(2,1)S(1)}, bf16[256,1024]{1,0:T(8,128)(2,1)S(1)}, u32[]{:S(2)}, u32[]{:S(2)}) collective-permute-start(bf16[256,1024]{1,0:T(8,128)(2,1)S(1)} %get-tuple-element.270), channel_id=1, source_target_pairs={{0,16},{4,20},{8,24},{12,28},{16,0},{20,4},{24,8},{28,12},{1,17},{... | collective-permute-start | bytes 1572872 | tf_op jit(solution)/shard_map/ppermute | solution.py:891
  93.7 14.0 %collective-permute-start.45 = (bf16[272,256]{1,0:T(8,128)(2,1)S(1)}, bf16[272,256]{1,0:T(8,128)(2,1)S(1)}, u32[]{:S(2)}, u32[]{:S(2)}) collective-permute-start(bf16[272,256]{1,0:T(8,128)(2,1)S(1)} %get-tuple-element.269.refs_14_), channel_id=1, source_target_pairs={{0,8},{4,12},{8,0},{12,4},{16,24},{20,28},{24,16},{28,20},{1,9},{5... | collective-permute-start | bytes 417800 | tf_op jit(solution)/shard_map/ppermute | solution.py:891
  97.2 24.1 %collective-permute-start.57 = (bf16[512,512]{1,0:T(8,128)(2,1)S(1)}, bf16[512,512]{1,0:T(8,128)(2,1)S(1)}, u32[]{:S(2)}, u32[]{:S(2)}) collective-permute-start(bf16[512,512]{1,0:T(8,128)(2,1)S(1)} %mix_1.1.refs_2_), channel_id=1, source_target_pairs={{0,4},{4,0},{8,12},{12,8},{16,20},{20,16},{24,28},{28,24},{1,5},{5... | collective-permute-start | bytes 1572872 | tf_op jit(solution)/shard_map/ppermute | solution.py:891
  102.9 14.2 %collective-permute-start.55 = (bf16[128,1024]{1,0:T(8,128)(2,1)S(1)}, bf16[128,1024]{1,0:T(8,128)(2,1)S(1)}, u32[]{:S(2)}, u32[]{:S(2)}) collective-permute-start(bf16[128,1024]{1,0:T(8,128)(2,1)S(1)} %get-tuple-element.286), channel_id=1, source_target_pairs={{0,16},{4,20},{8,24},{12,28},{16,0},{20,4},{24,8},{28,12},{1,17},{... | collective-permute-start | bytes 786440 | tf_op jit(solution)/shard_map/ppermute | solution.py:891
  104.4 24.4 %collective-permute-start.60 = (bf16[256,1024]{1,0:T(8,128)(2,1)S(1)}, bf16[256,1024]{1,0:T(8,128)(2,1)S(1)}, u32[]{:S(2)}, u32[]{:S(2)}) collective-permute-start(bf16[256,1024]{1,0:T(8,128)(2,1)S(1)} %get-tuple-element.296), channel_id=1, source_target_pairs={{0,8},{4,12},{8,0},{12,4},{16,24},{20,28},{24,16},{28,20},{1,9},{5... | collective-permute-start | bytes 1572872 | tf_op jit(solution)/shard_map/ppermute | solution.py:891
  107.7 6.5 %collective-permute-start.50 = (bf16[272,256]{1,0:T(8,128)(2,1)S(1)}, bf16[272,256]{1,0:T(8,128)(2,1)S(1)}, u32[]{:S(2)}, u32[]{:S(2)}) collective-permute-start(bf16[272,256]{1,0:T(8,128)(2,1)S(1)} %get-tuple-element.278.refs_3_), channel_id=1, source_target_pairs={{0,4},{4,0},{8,12},{12,8},{16,20},{20,16},{24,28},{28,24},{1,5},{5... | collective-permute-start | bytes 417800 | tf_op jit(solution)/shard_map/ppermute | solution.py:891
  117.7 9.6 %collective-permute-start.61 = (bf16[192,256]{1,0:T(8,128)(2,1)S(1)}, bf16[192,256]{1,0:T(8,128)(2,1)S(1)}, u32[]{:S(2)}, u32[]{:S(2)}) collective-permute-start(bf16[192,256]{1,0:T(8,128)(2,1)S(1)} %get-tuple-element.298), channel_id=1, source_target_pairs={{0,1},{1,0},{2,3},{3,2},{4,5},{5,4},{6,7},{7,6},{8,9},{9,8},{10,11... | collective-permute-start | bytes 294920 | tf_op jit(solution)/shard_map/ppermute | solution.py:885
  118.5 10.6 %collective-permute-start.59 = (bf16[272,256]{1,0:T(8,128)(2,1)S(1)}, bf16[272,256]{1,0:T(8,128)(2,1)S(1)}, u32[]{:S(2)}, u32[]{:S(2)}) collective-permute-start(bf16[272,256]{1,0:T(8,128)(2,1)S(1)} %get-tuple-element.279.refs_3_), channel_id=1, source_target_pairs={{0,16},{4,20},{8,24},{12,28},{16,0},{20,4},{24,8},{28,12},{1,17},{... | collective-permute-start | bytes 417800 | tf_op jit(solution)/shard_map/ppermute | solution.py:891
  122.1 14.5 %collective-permute-start.58 = (bf16[256,512]{1,0:T(8,128)(2,1)S(1)}, bf16[256,512]{1,0:T(8,128)(2,1)S(1)}, u32[]{:S(2)}, u32[]{:S(2)}) collective-permute-start(bf16[256,512]{1,0:T(8,128)(2,1)S(1)} %get-tuple-element.291), channel_id=1, source_target_pairs={{0,8},{4,12},{8,0},{12,4},{16,24},{20,28},{24,16},{28,20},{1,9},{5... | collective-permute-start | bytes 786440 | tf_op jit(solution)/shard_map/ppermute | solution.py:891
  126.0 10.7 %collective-permute-start.56 = (bf16[128,1024]{1,0:T(8,128)(2,1)S(1)}, bf16[128,1024]{1,0:T(8,128)(2,1)S(1)}, u32[]{:S(2)}, u32[]{:S(2)}) collective-permute-start(bf16[128,1024]{1,0:T(8,128)(2,1)S(1)} %get-tuple-element.289), channel_id=1, source_target_pairs={{0,2},{1,3},{2,0},{3,1},{4,6},{5,7},{6,4},{7,5},{8,10},{9,11},{10,... | collective-permute-start | bytes 786440 | tf_op jit(solution)/shard_map/ppermute | solution.py:888
  127.3 13.6 %collective-permute-start.66 = (bf16[128,1024]{1,0:T(8,128)(2,1)S(1)}, bf16[128,1024]{1,0:T(8,128)(2,1)S(1)}, u32[]{:S(2)}, u32[]{:S(2)}) collective-permute-start(bf16[128,1024]{1,0:T(8,128)(2,1)S(1)} %get-tuple-element.311), channel_id=1, source_target_pairs={{0,4},{4,0},{8,12},{12,8},{16,20},{20,16},{24,28},{28,24},{1,5},{5... | collective-permute-start | bytes 786440 | tf_op jit(solution)/shard_map/ppermute | solution.py:891
  129.1 18.1 %collective-permute-start.65 = (bf16[128,1024]{1,0:T(8,128)(2,1)S(1)}, bf16[128,1024]{1,0:T(8,128)(2,1)S(1)}, u32[]{:S(2)}, u32[]{:S(2)}) collective-permute-start(bf16[128,1024]{1,0:T(8,128)(2,1)S(1)} %get-tuple-element.310), channel_id=1, source_target_pairs={{0,16},{4,20},{8,24},{12,28},{16,0},{20,4},{24,8},{28,12},{1,17},{... | collective-permute-start | bytes 786440 | tf_op jit(solution)/shard_map/ppermute | solution.py:891
  130.9 4.4 %collective-permute-start.62 = (f32[64,256]{1,0:T(8,128)S(1)}, f32[64,256]{1,0:T(8,128)S(1)}, u32[]{:S(2)}, u32[]{:S(2)}) collective-permute-start(f32[64,256]{1,0:T(8,128)S(1)} %get-tuple-element.302), channel_id=1, source_target_pairs={{0,2},{1,3},{2,0},{3,1},{4,6},{5,7},{6,4},{7,5},{8,10},{9,11},{10,... | collective-permute-start | bytes 196616 | tf_op jit(solution)/shard_map/ppermute | solution.py:888
  135.3 5.0 %collective-permute-start.63 = (bf16[192,128]{1,0:T(8,128)(2,1)S(1)}, bf16[192,128]{1,0:T(8,128)(2,1)S(1)}, u32[]{:S(2)}, u32[]{:S(2)}) collective-permute-start(bf16[192,128]{1,0:T(8,128)(2,1)S(1)} %get-tuple-element.306), channel_id=1, source_target_pairs={{0,2},{1,3},{2,0},{3,1},{4,6},{5,7},{6,4},{7,5},{8,10},{9,11},{10,... | collective-permute-start | bytes 147464 | tf_op jit(solution)/shard_map/ppermute | solution.py:888
  136.6 11.4 %collective-permute-start.64 = (f32[32,256]{1,0:T(8,128)S(1)}, f32[32,256]{1,0:T(8,128)S(1)}, u32[]{:S(2)}, u32[]{:S(2)}) collective-permute-start(f32[32,256]{1,0:T(8,128)S(1)} %get-tuple-element.309), channel_id=1, source_target_pairs={{0,1},{1,0},{2,3},{3,2},{4,5},{5,4},{6,7},{7,6},{8,9},{9,8},{10,11... | collective-permute-start | bytes 98312 | tf_op jit(solution)/shard_map/ppermute | solution.py:885
  136.8 12.5 %collective-permute-start.67 = (bf16[128,512]{1,0:T(8,128)(2,1)S(1)}, bf16[128,512]{1,0:T(8,128)(2,1)S(1)}, u32[]{:S(2)}, u32[]{:S(2)}) collective-permute-start(bf16[128,512]{1,0:T(8,128)(2,1)S(1)} %get-tuple-element.319), channel_id=1, source_target_pairs={{0,16},{4,20},{8,24},{12,28},{16,0},{20,4},{24,8},{28,12},{1,17},{... | collective-permute-start | bytes 393224 | tf_op jit(solution)/shard_map/ppermute | solution.py:891
  (61 other events, 207.3 us)

commit v4 on v3

--- a/solution.py
+++ b/solution.py
@@ -996,7 +996,7 @@
 
     def mix_b():
         send_a, send_b, v.keep_a, v.keep_b = call(
-            mix_out, [rows16, rows16, rows32, rows32], [mix_output], fetch=[v.mixed_t]
+            mix_out, [rows16, rows16, rows32, rows32], [v.mixed_t, mix_output]
         )
         v.near_a, v.near_b = swap_core(send_a), swap_core(send_b)
 

time: 151 us -> 151 us (level)
  no operation moved by 1% of the time
where the time goes in v4:
time: 151 us
  starting transfers between devices  52.6 us (35%)
  waiting for transfers between devices  47.8 us (32%)
  Pallas kernels  45.4 us (30%)
  local copies, waits for them, and re-layouts  2.77 us (2%)
  between operations  2.08 us (1%)
    pallas_call x58, Pallas kernels, launch(): pl.pallas_call(run, out_shape=[jax.ShapeDtypeStruct(shape, kind) for shap...  45.4 us
    ppermute x15, starting transfers between devices, swap_sample(): return lax.ppermute(value, 'dp', pairs(mesh_dp, bit))  25.8 us
    ppermute x12, waiting for transfers between devices, swap_chip(): return lax.ppermute(value, 'mp', pairs(mesh_mp, 2))  21.7 us
    ppermute x12, starting transfers between devices, swap_chip(): return lax.ppermute(value, 'mp', pairs(mesh_mp, 2))  16.3 us
    ppermute x15, waiting for transfers between devices, swap_sample(): return lax.ppermute(value, 'dp', pairs(mesh_dp, bit))  15.7 us
    ppermute x41, starting transfers between devices, swap_core(): return lax.ppermute(value, 'mp', pairs(mesh_mp, 1))  10.5 us
    ppermute x41, waiting for transfers between devices, swap_core(): return lax.ppermute(value, 'mp', pairs(mesh_mp, 1))  10.4 us
  transfers between devices with their start and end apart: 68, of which 29 were waited for; matrix products, arithmetic and copies ran while one was open for 0% of the time, Pallas kernels for 26%

profile of v4, /device:TPU:0, one launch (start us, length us, event | category | flops | bytes accessed | tf_op | source)
XLA Modules:
  0.0 150.7 jit_solution(15973391638093235948)
XLA Ops:
  0.7 4.0 %mix_a.1 = (bf16[256,512]{1,0:T(8,128)(2,1)}, bf16[192,512]{1,0:T(8,128)(2,1)}, f32[192,512]{1,0:T(8,128)}, bf16[256,256]{1,0:T(8,128)(2,1)}, f32[256,256]{1,0:T...) custom-call(s32[48]{0:T(128)} %refs_0_.8, bf16[1,192,512]{2,1,0:T(8,128)(2,1)} %refs_1_.3, bf16[48,4,1024]{2,1,0:T(4,128)(2,1)} %refs_2_.9, ...), custom_call_target="tpu_custom_call" | custom-call | flops 100000000 | tf_op jit(solution)/shard_map/mix_a/pallas_call | solution.py:132
  8.0 3.0 %collective-permute-start.3 = (bf16[128,1024]{1,0:T(8,128)(2,1)S(1)}, bf16[128,1024]{1,0:T(8,128)(2,1)S(1)}, u32[]{:S(2)}, u32[]{:S(2)}) collective-permute-start(bf16[128,1024]{1,0:T(8,128)(2,1)S(1)} %get-tuple-element.182), channel_id=1, source_target_pairs={{0,2},{1,3},{2,0},{3,1},{4,6},{5,7},{6,4},{7,5},{8,10},{9,11},{10,... | collective-permute-start | bytes 786440 | tf_op jit(solution)/shard_map/ppermute | solution.py:888
  12.5 5.6 %collective-permute-done.3.refs_1_ = bf16[128,1024]{1,0:T(8,128)(2,1)S(1)} collective-permute-done((bf16[128,1024]{1,0:T(8,128)(2,1)S(1)}, bf16[128,1024]{1,0:T(8,128)(2,1)S(1)}, u32[]{:S(2)}, u32[]{:S(2)}) %collective-permute-start.3) | collective-permute-done | bytes 262176 | tf_op jit(solution)/shard_map/ppermute | solution.py:888
  20.6 2.6 %collective-permute-done.2.refs_2_ = bf16[128,1024]{1,0:T(8,128)(2,1)S(1)} collective-permute-done((bf16[128,1024]{1,0:T(8,128)(2,1)S(1)}, bf16[128,1024]{1,0:T(8,128)(2,1)S(1)}, u32[]{:S(2)}, u32[]{:S(2)}) %collective-permute-start.2) | collective-permute-done | bytes 262176 | tf_op jit(solution)/shard_map/ppermute | solution.py:888
  24.1 1.7 %collective-permute-start.11 = (bf16[128,1024]{1,0:T(8,128)(2,1)S(1)}, bf16[128,1024]{1,0:T(8,128)(2,1)S(1)}, u32[]{:S(2)}, u32[]{:S(2)}) collective-permute-start(bf16[128,1024]{1,0:T(8,128)(2,1)S(1)} %get-tuple-element.196.refs_0_), channel_id=1, source_target_pairs={{0,2},{1,3},{2,0},{3,1},{4,6},{5,7},{6,4},{7,5},{8,10},{9,11},{10,... | collective-permute-start | bytes 786440 | tf_op jit(solution)/shard_map/ppermute | solution.py:888
  25.8 2.6 %attend_a.1 = (bf16[3,256,256]{2,1,0:T(8,128)(2,1)S(1)}, bf16[256,256]{1,0:T(8,128)(2,1)S(1)}, f32[8,256]{1,0:T(8,128)S(1)}, f32[128,1024]{1,0:T(8,128)S(1)}, bf...) custom-call(bf16[64,1024]{1,0:T(8,128)(2,1)S(1)} %get-tuple-element.187.refs_0_.refs_4_.refs_5_, ...), custom_call_target="tpu_custom_call" | custom-call | flops 100000000 | tf_op jit(solution)/shard_map/attend_a/pallas_call | solution.py:132
  33.0 2.0 %attend_b.1 = (bf16[256,256]{1,0:T(8,128)(2,1)S(1)}, f32[8,256]{1,0:T(8,128)S(1)}, f32[128,1024]{1,0:T(8,128)S(1)}, bf16[64,1024]{1,0:T(8,128)(2,1)S(1)}, bf16[64,1024]{1,0:T(8,128)(2,1)S(1)}) custom-call(bf16[3,256,256]{2,1,0:T(8,128)(2,1)S(1)} %proj.1.refs_6_.refs_5_.refs_0_, bf16[3,256,256]{2,1,0:T(8,128)(2,1)S(1)} %get-tuple-element.193.refs_3_.refs_1_.refs_6_, ...), custom_call_target="tpu_custom_call" | custom-call | flops 100000000 | tf_op jit(solution)/shard_map/attend_b/pallas_call | solution.py:132
  37.0 1.8 %collective-permute-start.20 = (bf16[128,1024]{1,0:T(8,128)(2,1)S(1)}, bf16[128,1024]{1,0:T(8,128)(2,1)S(1)}, u32[]{:S(2)}, u32[]{:S(2)}) collective-permute-start(bf16[128,1024]{1,0:T(8,128)(2,1)S(1)} %get-tuple-element.210), channel_id=1, source_target_pairs={{0,2},{1,3},{2,0},{3,1},{4,6},{5,7},{6,4},{7,5},{8,10},{9,11},{10,... | collective-permute-start | bytes 786440 | tf_op jit(solution)/shard_map/ppermute | solution.py:888
  41.2 1.9 %mlp_a.1 = (bf16[256,1024]{1,0:T(8,128)(2,1)S(1)}, bf16[256,1024]{1,0:T(8,128)(2,1)S(1)}, f32[128,1024]{1,0:T(8,128)S(1)}, bf16[64,1024]{1,0:T(8,128)(2,1)S(1)}, bf16[64,1024]{1,0:T(8,128)(2,1)S(1)}) custom-call(bf16[64,1024]{1,0:T(8,128)(2,1)S(1)} %get-tuple-element.204.refs_0_.refs_1_, bf16[64,1024]{1,0:T(8,128)(2,1)S(1)} %get-tuple-element.205.refs_1_.refs_2_, ...), custom_call_target="tpu_custom_call" | custom-call | flops 400000000 | tf_op jit(solution)/shard_map/mlp_a/pallas_call | solution.py:132
  46.2 1.7 %collective-permute-start.29 = (bf16[128,1024]{1,0:T(8,128)(2,1)S(1)}, bf16[128,1024]{1,0:T(8,128)(2,1)S(1)}, u32[]{:S(2)}, u32[]{:S(2)}) collective-permute-start(bf16[128,1024]{1,0:T(8,128)(2,1)S(1)} %get-tuple-element.224), channel_id=1, source_target_pairs={{0,2},{1,3},{2,0},{3,1},{4,6},{5,7},{6,4},{7,5},{8,10},{9,11},{10,... | collective-permute-start | bytes 786440 | tf_op jit(solution)/shard_map/ppermute | solution.py:888
  47.9 1.9 %mlp_b.1 = (bf16[256,1024]{1,0:T(8,128)(2,1)S(1)}, bf16[256,1024]{1,0:T(8,128)(2,1)S(1)}, f32[128,1024]{1,0:T(8,128)S(1)}, bf16[64,1024]{1,0:T(8,128)(2,1)S(1)}, bf16[64,1024]{1,0:T(8,128)(2,1)S(1)}) custom-call(bf16[64,1024]{1,0:T(8,128)(2,1)S(1)} %get-tuple-element.215.refs_0_.refs_4_.refs_5_, ...), custom_call_target="tpu_custom_call" | custom-call | flops 1000000000 | tf_op jit(solution)/shard_map/mlp_b/pallas_call | solution.py:132
  50.6 1.6 %collective-permute-start.26 = (bf16[512,1024]{1,0:T(8,128)(2,1)S(1)}, bf16[512,1024]{1,0:T(8,128)(2,1)S(1)}, u32[]{:S(2)}, u32[]{:S(2)}) collective-permute-start(bf16[512,1024]{1,0:T(8,128)(2,1)S(1)} %down_1.1.refs_10_), channel_id=1, source_target_pairs={{0,4},{4,0},{8,12},{12,8},{16,20},{20,16},{24,28},{28,24},{1,5},{5... | collective-permute-start | bytes 3145736 | tf_op jit(solution)/shard_map/ppermute | solution.py:891
  53.1 1.6 %collective-permute-start.25 = (bf16[512,1024]{1,0:T(8,128)(2,1)S(1)}, bf16[512,1024]{1,0:T(8,128)(2,1)S(1)}, u32[]{:S(2)}, u32[]{:S(2)}) collective-permute-start(bf16[512,1024]{1,0:T(8,128)(2,1)S(1)} %up_1.1.refs_6_), channel_id=1, source_target_pairs={{0,8},{4,12},{8,0},{12,4},{16,24},{20,28},{24,16},{28,20},{1,9},{5... | collective-permute-start | bytes 3145736 | tf_op jit(solution)/shard_map/ppermute | solution.py:891
  57.5 2.8 %back_a.1 = (bf16[256,256]{1,0:T(8,128)(2,1)S(1)}, f32[512,256]{1,0:T(8,128)S(1)}, f32[512,256]{1,0:T(8,128)S(1)}) custom-call(bf16[64,1024]{1,0:T(8,128)(2,1)S(1)} %get-tuple-element.228.refs_0_.refs_8_.refs_9_, bf16[64,1024]{1,0:T(8,128)(2,1)S(1)} %get-tuple-element.229.refs_1_.refs_9_.refs_10_, ...), custom_call_target="tpu_custom_call" | custom-call | flops 1600000000 | tf_op jit(solution)/shard_map/back_a/pallas_call | solution.py:132
  60.3 4.7 %collective-permute-done.30.refs_1_ = bf16[128,1024]{1,0:T(8,128)(2,1)S(1)} collective-permute-done((bf16[128,1024]{1,0:T(8,128)(2,1)S(1)}, bf16[128,1024]{1,0:T(8,128)(2,1)S(1)}, u32[]{:S(2)}, u32[]{:S(2)}) %collective-permute-start.30) | collective-permute-done | bytes 262176 | tf_op jit(solution)/shard_map/ppermute | solution.py:888
  67.1 3.2 %back_b.1 = (bf16[3,512,256]{2,1,0:T(8,128)(2,1)S(1)}, f32[128,1024]{1,0:T(8,128)S(1)}, bf16[64,1024]{1,0:T(8,128)(2,1)S(1)}, bf16[64,1024]{1,0:T(8,128)(2,1)S(1)}) custom-call(bf16[64,1024]{1,0:T(8,128)(2,1)S(1)} %get-tuple-element.232.refs_0_.refs_12_.refs_13_, bf16[64,1024]{1,0:T(8,128)(2,1)S(1)} %get-tuple-element.233.refs_1_.refs_13_.refs_14_, ...), custom_call_target="tpu_custom_call" | custom-call | flops 100000000 | tf_op jit(solution)/shard_map/back_b/pallas_call | solution.py:132
  74.5 1.5 %collective-permute-start.39 = (bf16[128,1024]{1,0:T(8,128)(2,1)S(1)}, bf16[128,1024]{1,0:T(8,128)(2,1)S(1)}, u32[]{:S(2)}, u32[]{:S(2)}) collective-permute-start(bf16[128,1024]{1,0:T(8,128)(2,1)S(1)} %get-tuple-element.255), channel_id=1, source_target_pairs={{0,2},{1,3},{2,0},{3,1},{4,6},{5,7},{6,4},{7,5},{8,10},{9,11},{10,... | collective-permute-start | bytes 786440 | tf_op jit(solution)/shard_map/ppermute | solution.py:888
  77.7 1.6 %collective-permute-start.48 = (bf16[256,1024]{1,0:T(8,128)(2,1)S(1)}, bf16[256,1024]{1,0:T(8,128)(2,1)S(1)}, u32[]{:S(2)}, u32[]{:S(2)}) collective-permute-start(bf16[256,1024]{1,0:T(8,128)(2,1)S(1)} %get-tuple-element.271), channel_id=1, source_target_pairs={{0,8},{4,12},{8,0},{12,4},{16,24},{20,28},{24,16},{28,20},{1,9},{5... | collective-permute-start | bytes 1572872 | tf_op jit(solution)/shard_map/ppermute | solution.py:891
  80.3 2.6 %collective-permute-start.46 = (bf16[256,1024]{1,0:T(8,128)(2,1)S(1)}, bf16[256,1024]{1,0:T(8,128)(2,1)S(1)}, u32[]{:S(2)}, u32[]{:S(2)}) collective-permute-start(bf16[256,1024]{1,0:T(8,128)(2,1)S(1)} %get-tuple-element.270), channel_id=1, source_target_pairs={{0,16},{4,20},{8,24},{12,28},{16,0},{20,4},{24,8},{28,12},{1,17},{... | collective-permute-start | bytes 1572872 | tf_op jit(solution)/shard_map/ppermute | solution.py:891
  84.6 3.9 %collective-permute-done.42.refs_1_ = bf16[128,1024]{1,0:T(8,128)(2,1)S(1)} collective-permute-done((bf16[128,1024]{1,0:T(8,128)(2,1)S(1)}, bf16[128,1024]{1,0:T(8,128)(2,1)S(1)}, u32[]{:S(2)}, u32[]{:S(2)}) %collective-permute-start.42) | collective-permute-done | bytes 262176 | tf_op jit(solution)/shard_map/ppermute | solution.py:888
  92.0 1.6 %mass_1.1 = (bf16[272,256]{1,0:T(8,128)(2,1)S(1)}, f32[256,256]{1,0:T(8,128)S(1)}, f32[8,256]{1,0:T(8,128)S(1)}, bf16[192,256]{1,0:T(8,128)(2,1)S(1)}, f32[192,256]{1,0:T(8,128)S(1)}) custom-call(bf16[192,192]{1,0:T(8,128)(2,1)S(1)} %get-tuple-element.250.refs_0_, bf16[192,512]{1,0:T(8,128)(2,1)S(1)} %copy-done.14, f32[192,512]{1,0:T(8,128)S(1)} %copy-done.11, ...), custom_call_target="tpu_custom_call" | custom-call | flops 100000000 | tf_op jit(solution)/shard_map/mass_1/pallas_call | solution.py:132
  93.6 1.6 %collective-permute-start.45 = (bf16[272,256]{1,0:T(8,128)(2,1)S(1)}, bf16[272,256]{1,0:T(8,128)(2,1)S(1)}, u32[]{:S(2)}, u32[]{:S(2)}) collective-permute-start(bf16[272,256]{1,0:T(8,128)(2,1)S(1)} %get-tuple-element.269.refs_14_), channel_id=1, source_target_pairs={{0,8},{4,12},{8,0},{12,4},{16,24},{20,28},{24,16},{28,20},{1,9},{5... | collective-permute-start | bytes 417800 | tf_op jit(solution)/shard_map/ppermute | solution.py:891
  97.7 4.9 %collective-permute-done.48.refs_1_ = bf16[256,1024]{1,0:T(8,128)(2,1)S(1)} collective-permute-done((bf16[256,1024]{1,0:T(8,128)(2,1)S(1)}, bf16[256,1024]{1,0:T(8,128)(2,1)S(1)}, u32[]{:S(2)}, u32[]{:S(2)}) %collective-permute-start.48) | collective-permute-done | bytes 524320 | tf_op jit(solution)/shard_map/ppermute | solution.py:891
  104.4 3.0 %collective-permute-start.60 = (bf16[256,1024]{1,0:T(8,128)(2,1)S(1)}, bf16[256,1024]{1,0:T(8,128)(2,1)S(1)}, u32[]{:S(2)}, u32[]{:S(2)}) collective-permute-start(bf16[256,1024]{1,0:T(8,128)(2,1)S(1)} %get-tuple-element.296), channel_id=1, source_target_pairs={{0,8},{4,12},{8,0},{12,4},{16,24},{20,28},{24,16},{28,20},{1,9},{5... | collective-permute-start | bytes 1572872 | tf_op jit(solution)/shard_map/ppermute | solution.py:891
  107.7 2.1 %collective-permute-start.50 = (bf16[272,256]{1,0:T(8,128)(2,1)S(1)}, bf16[272,256]{1,0:T(8,128)(2,1)S(1)}, u32[]{:S(2)}, u32[]{:S(2)}) collective-permute-start(bf16[272,256]{1,0:T(8,128)(2,1)S(1)} %get-tuple-element.278.refs_3_), channel_id=1, source_target_pairs={{0,4},{4,0},{8,12},{12,8},{16,20},{20,16},{24,28},{28,24},{1,5},{5... | collective-permute-start | bytes 417800 | tf_op jit(solution)/shard_map/ppermute | solution.py:891
  109.8 4.4 %collective-permute-done.50.refs_2_ = bf16[272,256]{1,0:T(8,128)(2,1)S(1)} collective-permute-done((bf16[272,256]{1,0:T(8,128)(2,1)S(1)}, bf16[272,256]{1,0:T(8,128)(2,1)S(1)}, u32[]{:S(2)}, u32[]{:S(2)}) %collective-permute-start.50) | collective-permute-done | bytes 139296 | tf_op jit(solution)/shard_map/ppermute | solution.py:891
  118.5 1.5 %collective-permute-start.59 = (bf16[272,256]{1,0:T(8,128)(2,1)S(1)}, bf16[272,256]{1,0:T(8,128)(2,1)S(1)}, u32[]{:S(2)}, u32[]{:S(2)}) collective-permute-start(bf16[272,256]{1,0:T(8,128)(2,1)S(1)} %get-tuple-element.279.refs_3_), channel_id=1, source_target_pairs={{0,16},{4,20},{8,24},{12,28},{16,0},{20,4},{24,8},{28,12},{1,17},{... | collective-permute-start | bytes 417800 | tf_op jit(solution)/shard_map/ppermute | solution.py:891
  122.1 3.9 %collective-permute-start.58 = (bf16[256,512]{1,0:T(8,128)(2,1)S(1)}, bf16[256,512]{1,0:T(8,128)(2,1)S(1)}, u32[]{:S(2)}, u32[]{:S(2)}) collective-permute-start(bf16[256,512]{1,0:T(8,128)(2,1)S(1)} %get-tuple-element.291), channel_id=1, source_target_pairs={{0,8},{4,12},{8,0},{12,4},{16,24},{20,28},{24,16},{28,20},{1,9},{5... | collective-permute-start | bytes 786440 | tf_op jit(solution)/shard_map/ppermute | solution.py:891
  129.1 1.7 %finish.1 = (f32[64,256]{1,0:T(8,128)S(1)}, f32[64,256]{1,0:T(8,128)S(1)}, f32[3,128,256]{2,1,0:T(8,128)}) custom-call(f32[256,128]{1,0:T(8,128)S(1)} %copy-done.15, f32[256,256]{1,0:T(8,128)S(1)} %copy-done.13, bf16[48,4,1024]{2,1,0:T(4,128)(2,1)S(1)} %copy-done.9, bf16[48,1024]{1,0:T(8,128)(2,1)S(1)} %copy-done.10, ...), custom_call_target="tpu_custom_call" | custom-call | flops 100000000 | tf_op jit(solution)/shard_map/finish/pallas_call | solution.py:132
  131.9 3.3 %collective-permute-done.62.refs_1_ = f32[64,256]{1,0:T(8,128)S(1)} collective-permute-done((f32[64,256]{1,0:T(8,128)S(1)}, f32[64,256]{1,0:T(8,128)S(1)}, u32[]{:S(2)}, u32[]{:S(2)}) %collective-permute-start.62) | collective-permute-done | bytes 65568 | tf_op jit(solution)/shard_map/ppermute | solution.py:888
  136.7 2.7 %collective-permute-start.67 = (bf16[128,512]{1,0:T(8,128)(2,1)S(1)}, bf16[128,512]{1,0:T(8,128)(2,1)S(1)}, u32[]{:S(2)}, u32[]{:S(2)}) collective-permute-start(bf16[128,512]{1,0:T(8,128)(2,1)S(1)} %get-tuple-element.319), channel_id=1, source_target_pairs={{0,16},{4,20},{8,24},{12,28},{16,0},{20,4},{24,8},{28,12},{1,17},{... | collective-permute-start | bytes 393224 | tf_op jit(solution)/shard_map/ppermute | solution.py:891
  141.8 5.3 %collective-permute-done.65.refs_1_ = bf16[128,1024]{1,0:T(8,128)(2,1)S(1)} collective-permute-done((bf16[128,1024]{1,0:T(8,128)(2,1)S(1)}, bf16[128,1024]{1,0:T(8,128)(2,1)S(1)}, u32[]{:S(2)}, u32[]{:S(2)}) %collective-permute-start.65) | collective-permute-done | bytes 262176 | tf_op jit(solution)/shard_map/ppermute | solution.py:891
  (214 shorter events, 60.1 us)
Async XLA Ops:
  6.8 4.9 %collective-permute-start = (bf16[128,1024]{1,0:T(8,128)(2,1)S(1)}, bf16[128,1024]{1,0:T(8,128)(2,1)S(1)}, u32[]{:S(2)}, u32[]{:S(2)}) collective-permute-start(bf16[128,1024]{1,0:T(8,128)(2,1)S(1)} %get-tuple-element.175), channel_id=1, source_target_pairs={{0,1},{1,0},{2,3},{3,2},{4,5},{5,4},{6,7},{7,6},{8,9},{9,8},{10,11... | collective-permute-start | bytes 786440 | tf_op jit(solution)/shard_map/ppermute | solution.py:885
  8.0 10.0 %collective-permute-start.3 = (bf16[128,1024]{1,0:T(8,128)(2,1)S(1)}, bf16[128,1024]{1,0:T(8,128)(2,1)S(1)}, u32[]{:S(2)}, u32[]{:S(2)}) collective-permute-start(bf16[128,1024]{1,0:T(8,128)(2,1)S(1)} %get-tuple-element.182), channel_id=1, source_target_pairs={{0,2},{1,3},{2,0},{3,1},{4,6},{5,7},{6,4},{7,5},{8,10},{9,11},{10,... | collective-permute-start | bytes 786440 | tf_op jit(solution)/shard_map/ppermute | solution.py:888
  11.7 11.5 %collective-permute-start.2 = (bf16[128,1024]{1,0:T(8,128)(2,1)S(1)}, bf16[128,1024]{1,0:T(8,128)(2,1)S(1)}, u32[]{:S(2)}, u32[]{:S(2)}) collective-permute-start(bf16[128,1024]{1,0:T(8,128)(2,1)S(1)} %get-tuple-element.180), channel_id=1, source_target_pairs={{0,2},{1,3},{2,0},{3,1},{4,6},{5,7},{6,4},{7,5},{8,10},{9,11},{10,... | collective-permute-start | bytes 786440 | tf_op jit(solution)/shard_map/ppermute | solution.py:888
  24.1 8.3 %collective-permute-start.11 = (bf16[128,1024]{1,0:T(8,128)(2,1)S(1)}, bf16[128,1024]{1,0:T(8,128)(2,1)S(1)}, u32[]{:S(2)}, u32[]{:S(2)}) collective-permute-start(bf16[128,1024]{1,0:T(8,128)(2,1)S(1)} %get-tuple-element.196.refs_0_), channel_id=1, source_target_pairs={{0,2},{1,3},{2,0},{3,1},{4,6},{5,7},{6,4},{7,5},{8,10},{9,11},{10,... | collective-permute-start | bytes 786440 | tf_op jit(solution)/shard_map/ppermute | solution.py:888
  30.1 8.7 %collective-permute-start.10 = (bf16[128,1024]{1,0:T(8,128)(2,1)S(1)}, bf16[128,1024]{1,0:T(8,128)(2,1)S(1)}, u32[]{:S(2)}, u32[]{:S(2)}) collective-permute-start(bf16[128,1024]{1,0:T(8,128)(2,1)S(1)} %get-tuple-element.195), channel_id=1, source_target_pairs={{0,2},{1,3},{2,0},{3,1},{4,6},{5,7},{6,4},{7,5},{8,10},{9,11},{10,... | collective-permute-start | bytes 786440 | tf_op jit(solution)/shard_map/ppermute | solution.py:888
  35.6 4.1 %collective-permute-start.18 = (bf16[64,1024]{1,0:T(8,128)(2,1)S(1)}, bf16[64,1024]{1,0:T(8,128)(2,1)S(1)}, u32[]{:S(2)}, u32[]{:S(2)}) collective-permute-start(bf16[64,1024]{1,0:T(8,128)(2,1)S(1)} %get-tuple-element.206.refs_0_.refs_4_.refs_5_), channel_id=1, source_target_pairs={{0,1},{1,0},{2,3},{3,2},{4,5},{5,4},{6,7},{7,6},{8,9},{9,8},{10,11... | collective-permute-start | bytes 393224 | tf_op jit(solution)/shard_map/ppermute | solution.py:885
  35.7 4.0 %collective-permute-start.19 = (bf16[64,1024]{1,0:T(8,128)(2,1)S(1)}, bf16[64,1024]{1,0:T(8,128)(2,1)S(1)}, u32[]{:S(2)}, u32[]{:S(2)}) collective-permute-start(bf16[64,1024]{1,0:T(8,128)(2,1)S(1)} %get-tuple-element.207.refs_1_.refs_5_.refs_6_), channel_id=1, source_target_pairs={{0,1},{1,0},{2,3},{3,2},{4,5},{5,4},{6,7},{7,6},{8,9},{9,8},{10,11... | collective-permute-start | bytes 393224 | tf_op jit(solution)/shard_map/ppermute | solution.py:885
  37.0 8.4 %collective-permute-start.20 = (bf16[128,1024]{1,0:T(8,128)(2,1)S(1)}, bf16[128,1024]{1,0:T(8,128)(2,1)S(1)}, u32[]{:S(2)}, u32[]{:S(2)}) collective-permute-start(bf16[128,1024]{1,0:T(8,128)(2,1)S(1)} %get-tuple-element.210), channel_id=1, source_target_pairs={{0,2},{1,3},{2,0},{3,1},{4,6},{5,7},{6,4},{7,5},{8,10},{9,11},{10,... | collective-permute-start | bytes 786440 | tf_op jit(solution)/shard_map/ppermute | solution.py:888
  46.2 9.1 %collective-permute-start.29 = (bf16[128,1024]{1,0:T(8,128)(2,1)S(1)}, bf16[128,1024]{1,0:T(8,128)(2,1)S(1)}, u32[]{:S(2)}, u32[]{:S(2)}) collective-permute-start(bf16[128,1024]{1,0:T(8,128)(2,1)S(1)} %get-tuple-element.224), channel_id=1, source_target_pairs={{0,2},{1,3},{2,0},{3,1},{4,6},{5,7},{6,4},{7,5},{8,10},{9,11},{10,... | collective-permute-start | bytes 786440 | tf_op jit(solution)/shard_map/ppermute | solution.py:888
  50.6 26.1 %collective-permute-start.26 = (bf16[512,1024]{1,0:T(8,128)(2,1)S(1)}, bf16[512,1024]{1,0:T(8,128)(2,1)S(1)}, u32[]{:S(2)}, u32[]{:S(2)}) collective-permute-start(bf16[512,1024]{1,0:T(8,128)(2,1)S(1)} %down_1.1.refs_10_), channel_id=1, source_target_pairs={{0,4},{4,0},{8,12},{12,8},{16,20},{20,16},{24,28},{28,24},{1,5},{5... | collective-permute-start | bytes 3145736 | tf_op jit(solution)/shard_map/ppermute | solution.py:891
  53.1 26.2 %collective-permute-start.25 = (bf16[512,1024]{1,0:T(8,128)(2,1)S(1)}, bf16[512,1024]{1,0:T(8,128)(2,1)S(1)}, u32[]{:S(2)}, u32[]{:S(2)}) collective-permute-start(bf16[512,1024]{1,0:T(8,128)(2,1)S(1)} %up_1.1.refs_6_), channel_id=1, source_target_pairs={{0,8},{4,12},{8,0},{12,4},{16,24},{20,28},{24,16},{28,20},{1,9},{5... | collective-permute-start | bytes 3145736 | tf_op jit(solution)/shard_map/ppermute | solution.py:891
  56.5 8.5 %collective-permute-start.30 = (bf16[128,1024]{1,0:T(8,128)(2,1)S(1)}, bf16[128,1024]{1,0:T(8,128)(2,1)S(1)}, u32[]{:S(2)}, u32[]{:S(2)}) collective-permute-start(bf16[128,1024]{1,0:T(8,128)(2,1)S(1)} %get-tuple-element.227), channel_id=1, source_target_pairs={{0,2},{1,3},{2,0},{3,1},{4,6},{5,7},{6,4},{7,5},{8,10},{9,11},{10,... | collective-permute-start | bytes 786440 | tf_op jit(solution)/shard_map/ppermute | solution.py:888
  71.7 31.7 %collective-permute-start.47 = (bf16[512,1024]{1,0:T(8,128)(2,1)S(1)}, bf16[512,1024]{1,0:T(8,128)(2,1)S(1)}, u32[]{:S(2)}, u32[]{:S(2)}) collective-permute-start(bf16[512,1024]{1,0:T(8,128)(2,1)S(1)} %attn_1.1.refs_3_), channel_id=1, source_target_pairs={{0,4},{4,0},{8,12},{12,8},{16,20},{20,16},{24,28},{28,24},{1,5},{5... | collective-permute-start | bytes 3145736 | tf_op jit(solution)/shard_map/ppermute | solution.py:891
  74.5 9.5 %collective-permute-start.39 = (bf16[128,1024]{1,0:T(8,128)(2,1)S(1)}, bf16[128,1024]{1,0:T(8,128)(2,1)S(1)}, u32[]{:S(2)}, u32[]{:S(2)}) collective-permute-start(bf16[128,1024]{1,0:T(8,128)(2,1)S(1)} %get-tuple-element.255), channel_id=1, source_target_pairs={{0,2},{1,3},{2,0},{3,1},{4,6},{5,7},{6,4},{7,5},{8,10},{9,11},{10,... | collective-permute-start | bytes 786440 | tf_op jit(solution)/shard_map/ppermute | solution.py:888
  76.2 12.4 %collective-permute-start.42 = (bf16[128,1024]{1,0:T(8,128)(2,1)S(1)}, bf16[128,1024]{1,0:T(8,128)(2,1)S(1)}, u32[]{:S(2)}, u32[]{:S(2)}) collective-permute-start(bf16[128,1024]{1,0:T(8,128)(2,1)S(1)} %get-tuple-element.259), channel_id=1, source_target_pairs={{0,2},{1,3},{2,0},{3,1},{4,6},{5,7},{6,4},{7,5},{8,10},{9,11},{10,... | collective-permute-start | bytes 786440 | tf_op jit(solution)/shard_map/ppermute | solution.py:888
  77.7 25.0 %collective-permute-start.48 = (bf16[256,1024]{1,0:T(8,128)(2,1)S(1)}, bf16[256,1024]{1,0:T(8,128)(2,1)S(1)}, u32[]{:S(2)}, u32[]{:S(2)}) collective-permute-start(bf16[256,1024]{1,0:T(8,128)(2,1)S(1)} %get-tuple-element.271), channel_id=1, source_target_pairs={{0,8},{4,12},{8,0},{12,4},{16,24},{20,28},{24,16},{28,20},{1,9},{5... | collective-permute-start | bytes 1572872 | tf_op jit(solution)/shard_map/ppermute | solution.py:891
  80.3 27.1 %collective-permute-start.46 = (bf16[256,1024]{1,0:T(8,128)(2,1)S(1)}, bf16[256,1024]{1,0:T(8,128)(2,1)S(1)}, u32[]{:S(2)}, u32[]{:S(2)}) collective-permute-start(bf16[256,1024]{1,0:T(8,128)(2,1)S(1)} %get-tuple-element.270), channel_id=1, source_target_pairs={{0,16},{4,20},{8,24},{12,28},{16,0},{20,4},{24,8},{28,12},{1,17},{... | collective-permute-start | bytes 1572872 | tf_op jit(solution)/shard_map/ppermute | solution.py:891
  93.6 14.0 %collective-permute-start.45 = (bf16[272,256]{1,0:T(8,128)(2,1)S(1)}, bf16[272,256]{1,0:T(8,128)(2,1)S(1)}, u32[]{:S(2)}, u32[]{:S(2)}) collective-permute-start(bf16[272,256]{1,0:T(8,128)(2,1)S(1)} %get-tuple-element.269.refs_14_), channel_id=1, source_target_pairs={{0,8},{4,12},{8,0},{12,4},{16,24},{20,28},{24,16},{28,20},{1,9},{5... | collective-permute-start | bytes 417800 | tf_op jit(solution)/shard_map/ppermute | solution.py:891
  97.1 24.1 %collective-permute-start.57 = (bf16[512,512]{1,0:T(8,128)(2,1)S(1)}, bf16[512,512]{1,0:T(8,128)(2,1)S(1)}, u32[]{:S(2)}, u32[]{:S(2)}) collective-permute-start(bf16[512,512]{1,0:T(8,128)(2,1)S(1)} %mix_1.1.refs_2_), channel_id=1, source_target_pairs={{0,4},{4,0},{8,12},{12,8},{16,20},{20,16},{24,28},{28,24},{1,5},{5... | collective-permute-start | bytes 1572872 | tf_op jit(solution)/shard_map/ppermute | solution.py:891
  102.9 14.3 %collective-permute-start.55 = (bf16[128,1024]{1,0:T(8,128)(2,1)S(1)}, bf16[128,1024]{1,0:T(8,128)(2,1)S(1)}, u32[]{:S(2)}, u32[]{:S(2)}) collective-permute-start(bf16[128,1024]{1,0:T(8,128)(2,1)S(1)} %get-tuple-element.286), channel_id=1, source_target_pairs={{0,16},{4,20},{8,24},{12,28},{16,0},{20,4},{24,8},{28,12},{1,17},{... | collective-permute-start | bytes 786440 | tf_op jit(solution)/shard_map/ppermute | solution.py:891
  104.4 24.4 %collective-permute-start.60 = (bf16[256,1024]{1,0:T(8,128)(2,1)S(1)}, bf16[256,1024]{1,0:T(8,128)(2,1)S(1)}, u32[]{:S(2)}, u32[]{:S(2)}) collective-permute-start(bf16[256,1024]{1,0:T(8,128)(2,1)S(1)} %get-tuple-element.296), channel_id=1, source_target_pairs={{0,8},{4,12},{8,0},{12,4},{16,24},{20,28},{24,16},{28,20},{1,9},{5... | collective-permute-start | bytes 1572872 | tf_op jit(solution)/shard_map/ppermute | solution.py:891
  107.7 6.5 %collective-permute-start.50 = (bf16[272,256]{1,0:T(8,128)(2,1)S(1)}, bf16[272,256]{1,0:T(8,128)(2,1)S(1)}, u32[]{:S(2)}, u32[]{:S(2)}) collective-permute-start(bf16[272,256]{1,0:T(8,128)(2,1)S(1)} %get-tuple-element.278.refs_3_), channel_id=1, source_target_pairs={{0,4},{4,0},{8,12},{12,8},{16,20},{20,16},{24,28},{28,24},{1,5},{5... | collective-permute-start | bytes 417800 | tf_op jit(solution)/shard_map/ppermute | solution.py:891
  117.7 9.6 %collective-permute-start.61 = (bf16[192,256]{1,0:T(8,128)(2,1)S(1)}, bf16[192,256]{1,0:T(8,128)(2,1)S(1)}, u32[]{:S(2)}, u32[]{:S(2)}) collective-permute-start(bf16[192,256]{1,0:T(8,128)(2,1)S(1)} %get-tuple-element.298), channel_id=1, source_target_pairs={{0,1},{1,0},{2,3},{3,2},{4,5},{5,4},{6,7},{7,6},{8,9},{9,8},{10,11... | collective-permute-start | bytes 294920 | tf_op jit(solution)/shard_map/ppermute | solution.py:885
  118.5 10.6 %collective-permute-start.59 = (bf16[272,256]{1,0:T(8,128)(2,1)S(1)}, bf16[272,256]{1,0:T(8,128)(2,1)S(1)}, u32[]{:S(2)}, u32[]{:S(2)}) collective-permute-start(bf16[272,256]{1,0:T(8,128)(2,1)S(1)} %get-tuple-element.279.refs_3_), channel_id=1, source_target_pairs={{0,16},{4,20},{8,24},{12,28},{16,0},{20,4},{24,8},{28,12},{1,17},{... | collective-permute-start | bytes 417800 | tf_op jit(solution)/shard_map/ppermute | solution.py:891
  122.1 14.4 %collective-permute-start.58 = (bf16[256,512]{1,0:T(8,128)(2,1)S(1)}, bf16[256,512]{1,0:T(8,128)(2,1)S(1)}, u32[]{:S(2)}, u32[]{:S(2)}) collective-permute-start(bf16[256,512]{1,0:T(8,128)(2,1)S(1)} %get-tuple-element.291), channel_id=1, source_target_pairs={{0,8},{4,12},{8,0},{12,4},{16,24},{20,28},{24,16},{28,20},{1,9},{5... | collective-permute-start | bytes 786440 | tf_op jit(solution)/shard_map/ppermute | solution.py:891
  126.0 10.7 %collective-permute-start.56 = (bf16[128,1024]{1,0:T(8,128)(2,1)S(1)}, bf16[128,1024]{1,0:T(8,128)(2,1)S(1)}, u32[]{:S(2)}, u32[]{:S(2)}) collective-permute-start(bf16[128,1024]{1,0:T(8,128)(2,1)S(1)} %get-tuple-element.289), channel_id=1, source_target_pairs={{0,2},{1,3},{2,0},{3,1},{4,6},{5,7},{6,4},{7,5},{8,10},{9,11},{10,... | collective-permute-start | bytes 786440 | tf_op jit(solution)/shard_map/ppermute | solution.py:888
  127.3 13.7 %collective-permute-start.66 = (bf16[128,1024]{1,0:T(8,128)(2,1)S(1)}, bf16[128,1024]{1,0:T(8,128)(2,1)S(1)}, u32[]{:S(2)}, u32[]{:S(2)}) collective-permute-start(bf16[128,1024]{1,0:T(8,128)(2,1)S(1)} %get-tuple-element.311), channel_id=1, source_target_pairs={{0,4},{4,0},{8,12},{12,8},{16,20},{20,16},{24,28},{28,24},{1,5},{5... | collective-permute-start | bytes 786440 | tf_op jit(solution)/shard_map/ppermute | solution.py:891
  129.0 18.1 %collective-permute-start.65 = (bf16[128,1024]{1,0:T(8,128)(2,1)S(1)}, bf16[128,1024]{1,0:T(8,128)(2,1)S(1)}, u32[]{:S(2)}, u32[]{:S(2)}) collective-permute-start(bf16[128,1024]{1,0:T(8,128)(2,1)S(1)} %get-tuple-element.310), channel_id=1, source_target_pairs={{0,16},{4,20},{8,24},{12,28},{16,0},{20,4},{24,8},{28,12},{1,17},{... | collective-permute-start | bytes 786440 | tf_op jit(solution)/shard_map/ppermute | solution.py:891
  130.8 4.4 %collective-permute-start.62 = (f32[64,256]{1,0:T(8,128)S(1)}, f32[64,256]{1,0:T(8,128)S(1)}, u32[]{:S(2)}, u32[]{:S(2)}) collective-permute-start(f32[64,256]{1,0:T(8,128)S(1)} %get-tuple-element.302), channel_id=1, source_target_pairs={{0,2},{1,3},{2,0},{3,1},{4,6},{5,7},{6,4},{7,5},{8,10},{9,11},{10,... | collective-permute-start | bytes 196616 | tf_op jit(solution)/shard_map/ppermute | solution.py:888
  135.2 5.0 %collective-permute-start.63 = (bf16[192,128]{1,0:T(8,128)(2,1)S(1)}, bf16[192,128]{1,0:T(8,128)(2,1)S(1)}, u32[]{:S(2)}, u32[]{:S(2)}) collective-permute-start(bf16[192,128]{1,0:T(8,128)(2,1)S(1)} %get-tuple-element.306), channel_id=1, source_target_pairs={{0,2},{1,3},{2,0},{3,1},{4,6},{5,7},{6,4},{7,5},{8,10},{9,11},{10,... | collective-permute-start | bytes 147464 | tf_op jit(solution)/shard_map/ppermute | solution.py:888
  136.5 11.4 %collective-permute-start.64 = (f32[32,256]{1,0:T(8,128)S(1)}, f32[32,256]{1,0:T(8,128)S(1)}, u32[]{:S(2)}, u32[]{:S(2)}) collective-permute-start(f32[32,256]{1,0:T(8,128)S(1)} %get-tuple-element.309), channel_id=1, source_target_pairs={{0,1},{1,0},{2,3},{3,2},{4,5},{5,4},{6,7},{7,6},{8,9},{9,8},{10,11... | collective-permute-start | bytes 98312 | tf_op jit(solution)/shard_map/ppermute | solution.py:885
  136.7 12.5 %collective-permute-start.67 = (bf16[128,512]{1,0:T(8,128)(2,1)S(1)}, bf16[128,512]{1,0:T(8,128)(2,1)S(1)}, u32[]{:S(2)}, u32[]{:S(2)}) collective-permute-start(bf16[128,512]{1,0:T(8,128)(2,1)S(1)} %get-tuple-element.319), channel_id=1, source_target_pairs={{0,16},{4,20},{8,24},{12,28},{16,0},{20,4},{24,8},{28,12},{1,17},{... | collective-permute-start | bytes 393224 | tf_op jit(solution)/shard_map/ppermute | solution.py:891
  (61 other events, 207.2 us)
